TPU v7x, 32 devices: a whole 2x2x4 slice. The times are simulated.
32 devices in a mesh: half: 2 (over y), shard: 16 (over z, x, core).
Axes of the slice: x: 2, y: 2, z: 4, core: 2. Of those that a mesh axis runs over, the one named last changes fastest.
Arguments:
- recording: float32 [32, 2048, 1024], P('half', 'shard'), may hold values from -600 to 600
- source_channels: int32 [256], replicated, may hold values from 0 to 2047, as said below
Outputs:
- correlations: float32 [256, 2048, 512], P('half', 'shard')
Inputs may be any that keep to these rules, and one draw needn't show every extreme that they name: `source_channels`: distinct channel indices.
All inputs are finite; a program needn't handle non-finite values.
Results may differ from a plain program's by a relative error of at most 0.000071.
Values sent between devices are 32-bit elements; how exact they have to be, the bound alone decides.
No kernel may reach another device: no remote copies, remote signals or barrier semaphores. Data moves between devices by JAX's collectives and lax.ppermute only.
A program may use at most 128 MiB of HBM per device.

v0:
```python
import jax
import jax.numpy as jnp
from jax import lax
from jax.sharding import PartitionSpec as P

F = 128
LAGS = 512
SMOOTH = 2
SEG = 32


water_level = 0.2
epsilon = 1e-05


def partner_2(x, axis, bit):
    return lax.ppermute(x, axis, [(i, i ^ 1 << bit) for i in range(lax.axis_size(axis))])


def forward_table(samples, freq_count):
    bins = jnp.arange(freq_count, dtype=jnp.int32) + 1
    times = jnp.arange(samples, dtype=jnp.int32)
    phase = bins[:, None] * times[None, :] % samples
    angle = 2.0 * jnp.pi * phase.astype(jnp.float32) / samples
    taper = 0.5 - 0.5 * jnp.cos(2.0 * jnp.pi * times.astype(jnp.float32) / samples)
    return jnp.stack((jnp.cos(angle) * taper[None, :], -jnp.sin(angle) * taper[None, :]), axis=1)


def inverse_table(samples, freq_count, lag_count, segments):
    bins = jnp.arange(freq_count, dtype=jnp.int32) + 1
    shifts = jnp.arange(lag_count, dtype=jnp.int32) - lag_count // 2
    phase = bins[:, None] * shifts[None, :] % samples
    angle = 2.0 * jnp.pi * phase.astype(jnp.float32) / samples
    scale = 1.0 / jnp.sqrt(jnp.float32(segments * freq_count))
    return jnp.stack((jnp.cos(angle) * scale, -jnp.sin(angle) * scale), axis=1)


def whiten(spectra):
    magnitude = jnp.sqrt(spectra[:, 0] * spectra[:, 0] + spectra[:, 1] * spectra[:, 1])
    freq_count = magnitude.shape[0]
    padded = jnp.pad(magnitude, ((SMOOTH, SMOOTH), (0, 0), (0, 0)))
    smoothed = padded[0:freq_count]
    for offset in range(1, 2 * SMOOTH + 1):
        smoothed = smoothed + padded[offset : offset + freq_count]
    smoothed = smoothed / (2 * SMOOTH + 1)
    water_mark = jnp.mean(magnitude, axis=0, keepdims=True)
    divisor = smoothed + water_level * water_mark + epsilon
    return spectra / divisor[:, None]


def correlate(whitened, indices):
    sources = jnp.take(whitened, indices, axis=2)
    src_real, src_imag = (sources[:, 0], sources[:, 1])
    rec_real, rec_imag = (whitened[:, 0], whitened[:, 1])
    high = lax.Precision.HIGHEST
    cross_real = jnp.einsum("fnx,fcx->fnc", src_real, rec_real, precision=high) + jnp.einsum(
        "fnx,fcx->fnc", src_imag, rec_imag, precision=high
    )
    cross_imag = jnp.einsum("fnx,fcx->fnc", src_real, rec_imag, precision=high) - jnp.einsum(
        "fnx,fcx->fnc", src_imag, rec_real, precision=high
    )
    return jnp.stack((cross_real, cross_imag), axis=1)


def body(recording, source_channels):
    samples = recording.shape[2]
    forward = forward_table(samples, F)
    spectra = jnp.einsum("fqt,sct->fqcs", forward, recording, precision=lax.Precision.HIGHEST)
    whitened = whiten(spectra)
    by_freq = lax.all_to_all(whitened, "shard", split_axis=0, concat_axis=2, tiled=True)
    per_half = source_channels.shape[0] // lax.axis_size("half")
    half_index = lax.axis_index("half")
    own_sources = lax.dynamic_slice_in_dim(source_channels, half_index * per_half, per_half)
    partner = partner_2(by_freq, "half", 0)
    combined = jnp.concatenate((by_freq, partner), axis=3)
    cross = correlate(combined, own_sources)
    backward = inverse_table(samples, F, LAGS, SEG)
    return jnp.einsum(
        "fqnc,fql->ncl",
        lax.all_to_all(cross, "shard", split_axis=3, concat_axis=0, tiled=True),
        backward,
        precision=lax.Precision.HIGHEST,
    )


def solution(mesh):
    return jax.shard_map(
        body,
        mesh=mesh,
        in_specs=(P("half", "shard", None), P()),
        out_specs=P("half", "shard", None),
        check_vma=False,
    )
```

profile of v0, /device:TPU:11, one launch (start us, length us, event | category | flops | bytes accessed | tf_op | source)
XLA Modules:
  0.0 630.6 jit_solution(1467376965806393649)
XLA Ops:
  0.0 2.2 cosine_multiply_fusion
  2.2 9.6 %fusion.9 = f32[128,2,128,16]{2,0,3,1:T(8,128)S(1)} fusion(f32[16,128,1024]{2,1,0:T(8,128)} %param.2, f32[128,1,1024]{2,0,1:T(8,128)S(1)} %get-tuple-element.10, f32[128,1,1024]{2,0,1:T(8,128)S(1)} %get-tuple-element.9), kind=kOutput, calls=%fused_computation.14 | convolution fusion | flops 6442713088 | bytes 11534336 | tf_op jit(solution)/shard_map/fqt,sct->fqcs/dot_general | solution.py:68
  11.8 0.4 fusion.27
  12.3 0.5 add_add_fusion
  12.8 0.2 broadcast_divide_fusion
  13.0 1.2 copy.16
  14.3 53.7 %all_to_all.36 = f32[128,2,128,16]{2,3,1,0:T(8,128)S(1)} all-to-all(f32[128,2,128,16]{2,3,1,0:T(8,128)S(1)} %copy.16), channel_id=1, replica_groups=mesh['half'=2,'shard'=16] {'shard'}, dimensions={0} | all-to-all | bytes 4194304 | tf_op jit(solution)/shard_map/all_to_all | solution.py:70
  67.9 0.0 copy-start
  67.9 2.5 copy.32
  70.4 1.7 all_to_all.29
  72.2 1.3 collective-permute-start
  73.5 0.0 copy-done
  73.5 0.1 compare_and_fusion
  73.6 1.4 constant_dynamic-update-slice_fusion.1
  75.0 44.3 %collective-permute-done = f32[8,2,2048,16]{2,3,0,1:T(8,128)} collective-permute-done((f32[8,2,2048,16]{2,3,0,1:T(8,128)S(1)}, f32[8,2,2048,16]{2,3,0,1:T(8,128)}, u32[]{:S(2)}, u32[]{:S(2)}) %collective-permute-start) | collective-permute-done | bytes 2097184 | tf_op jit(solution)/shard_map/ppermute | solution.py:17
  119.4 3.1 constant_dynamic-update-slice_fusion
  122.5 10.7 %copy.18 = f32[8,2,2048,32]{3,0,2,1:T(8,128)} copy(f32[8,2,2048,32]{2,3,0,1:T(8,128)} %constant_dynamic-update-slice_fusion) | data formatting | bytes 8388608 | tf_op jit(solution)/shard_map/concatenate | solution.py:75
  133.2 6.5 %gather_fusion = f32[128,8,2,32]{3,1,2,0:T(8,128)S(1)} fusion(f32[8,2,2048,32]{3,0,2,1:T(8,128)} %copy.18, s32[1024]{0:T(1024)S(1)} %pad_clamp_fusion), kind=kCustom, calls=%fused_computation | custom fusion | bytes 524800 | tf_op jit(solution)/shard_map/jit(_take)/gather | solution.py:52
  139.7 0.4 copy.19
  140.1 8.4 %fusion.7 = f32[8,128,2048]{2,1,0:T(8,128)S(1)} fusion(f32[8,2,2048,32]{2,3,0,1:T(8,128)} %constant_dynamic-update-slice_fusion, f32[8,2,128,32]{2,3,0,1:T(8,128)S(1)} %select_bitcast_fusion), kind=kOutput, calls=%fused_computation.12 | convolution fusion | flops 805306368 | bytes 10616832 | tf_op jit(solution)/shard_map/fnx,fcx->fnc/dot_general | solution.py:59
  148.6 8.8 %fusion.8 = f32[8,128,2048]{2,1,0:T(8,128)S(1)} fusion(f32[8,2,2048,32]{2,3,0,1:T(8,128)} %constant_dynamic-update-slice_fusion, f32[8,2,128,32]{2,3,0,1:T(8,128)S(1)} %select_bitcast_fusion), kind=kOutput, calls=%fused_computation.13 | convolution fusion | flops 805306368 | bytes 10616832 | tf_op jit(solution)/shard_map/fnx,fcx->fnc/dot_general | solution.py:56
  157.4 8.5 %subtract_bitcast_fusion = f32[8,1,128,2048]{3,2,0,1:T(8,128)S(1)} fusion(f32[8,128,2048]{2,1,0:T(8,128)S(1)} %fusion.7, f32[8,2,2048,32]{2,3,0,1:T(8,128)} %constant_dynamic-update-slice_fusion, f32[8,2,128,32]{2,3,0,1:T(8,128)S(1)} %select_bitcast_fusion), kind=kOutput, calls=%fused_computation.7 | convolution fusion | flops 807403520 | bytes 19005440 | tf_op jit(solution)/shard_map/fnx,fcx->fnc/dot_general | solution.py:59
  165.9 8.7 %add_bitcast_fusion = f32[8,1,128,2048]{3,2,0,1:T(8,128)S(1)} fusion(f32[8,128,2048]{2,1,0:T(8,128)S(1)} %fusion.8, f32[8,2,2048,32]{2,3,0,1:T(8,128)} %constant_dynamic-update-slice_fusion, f32[8,2,128,32]{2,3,0,1:T(8,128)S(1)} %select_bitcast_fusion), kind=kOutput, calls=%fused_computation.8 | convolution fusion | flops 807403520 | bytes 19005440 | tf_op jit(solution)/shard_map/fnx,fcx->fnc/dot_general | solution.py:56
  174.7 6.2 pad_maximum_fusion
  180.9 17.7 %copy.20 = f32[8,2,128,2048]{2,0,1,3:T(8,128)} copy(f32[8,2,128,2048]{3,2,0,1:T(8,128)} %pad_maximum_fusion) | data formatting | bytes 33554432 | tf_op jit(solution)/shard_map/stack | solution.py:62
  198.6 6.3 all-to-all-start.1
  204.9 1.1 cosine_multiply_fusion.1
  206.0 361.0 %all-to-all-done.1 = f32[8,2,128,2048]{2,0,1,3:T(8,128)} async-done(((f32[8,2,128,2048]{2,0,1,3:T(8,128)}), f32[8,2,128,2048]{2,0,1,3:T(8,128)}, u32[]{:S(2)}, u32[]{:S(2)}) %all-to-all-start.1) | async-done | bytes 16777248 | tf_op jit(solution)/shard_map/all_to_all | solution.py:80
  567.0 17.6 %copy.22 = f32[16,8,2,128,128]{4,3,2,1,0:T(8,128)} copy(f32[16,8,2,128,128]{3,1,2,4,0:T(8,128)} %bitcast.16) | data formatting | bytes 33554432 | tf_op jit(solution)/shard_map/all_to_all | solution.py:80
  584.6 45.8 %fusion.2 = f32[128,128,512]{2,1,0:T(8,128)} fusion(f32[128,2,128,128]{3,2,1,0:T(8,128)} %bitcast.54, f32[128,1,512]{2,0,1:T(8,128)S(1)} %get-tuple-element.12, f32[128,1,512]{2,0,1:T(8,128)S(1)} %get-tuple-element.11), kind=kOutput, calls=%fused_computation.4 | convolution fusion | flops 25769934848 | bytes 50855936 | tf_op jit(solution)/shard_map/fqnc,fql->ncl/dot_general | solution.py:78
  (6 shorter events, 0.1 us)
Async XLA Ops:
  67.9 5.6 copy-start
  72.2 47.2 %collective-permute-start = (f32[8,2,2048,16]{2,3,0,1:T(8,128)S(1)}, f32[8,2,2048,16]{2,3,0,1:T(8,128)}, u32[]{:S(2)}, u32[]{:S(2)}) collective-permute-start(f32[8,2,2048,16]{2,3,0,1:T(8,128)S(1)} %all_to_all.29), channel_id=1, source_target_pairs={{0,16},{16,0},{1,17},{17,1},{2,18},{18,2},{3,19},{19,3},{4,20},{20... | collective-permute-start | bytes 6291464 | tf_op jit(solution)/shard_map/ppermute | solution.py:17
  198.6 368.4 %all-to-all-start.1 = ((f32[8,2,128,2048]{2,0,1,3:T(8,128)}), f32[8,2,128,2048]{2,0,1,3:T(8,128)}, u32[]{:S(2)}, u32[]{:S(2)}) async-start(f32[8,2,128,2048]{2,0,1,3:T(8,128)} %copy.20), calls=%async_computation.1 | async-start | bytes 33554432 | tf_op jit(solution)/shard_map/all_to_all | solution.py:80
where the time goes:
time: 639 us; the launch traced here: 631 us
  waiting for transfers between devices  405 us (63%)
  matrix products  90 us (14%)
  local copies, waits for them, and re-layouts  62.9 us (10%)
  blocking collectives  53.7 us (8%)
  other arithmetic  10.8 us (2%)
  starting transfers between devices  7.6 us (1%)
    all_to_all x1, waiting for transfers between devices, body(): lax.all_to_all(cross, 'shard', split_axis=3, concat_axis=0, tiled=True)  361 us
    all_to_all x1, blocking collectives, body(): lax.all_to_all(whitened, 'shard', split_axis=0, concat_axis=2, tiled=True)  53.7 us
    dot_general x1, matrix products, body(): jnp.einsum('fqnc,fql->ncl', lax.all_to_all(cross, 'shard', split_axis=3,...  45.8 us
    ppermute x1, waiting for transfers between devices, partner_2(): lax.ppermute(x, axis, [(i, i ^ 1 << bit) for i in range(lax.axis_size(axi...  44.3 us
    another operation x1, local copies, waits for them, and re-layouts, correlate(): return jnp.stack((cross_real, cross_imag), axis=1)  17.7 us
    all_to_all x1, local copies, waits for them, and re-layouts, body(): lax.all_to_all(cross, 'shard', split_axis=3, concat_axis=0, tiled=True)  17.6 us
    concatenate x2, local copies, waits for them, and re-layouts, body(): combined = jnp.concatenate((by_freq, partner), axis=3)  13.9 us
  transfers between devices with their start and end apart: 2, of which 2 were waited for; matrix products, arithmetic and copies ran while one was open for 0% of the time, Pallas kernels for 0%

commit v1 on v0

v1 whole, which is shorter than its diff:
```python
import functools

import jax
import jax.numpy as jnp
import numpy as np
from jax import lax
from jax.experimental import pallas as pl
from jax.experimental.pallas import tpu as pltpu
from jax.sharding import PartitionSpec as P

F = 128
LAGS = 512
SMOOTH = 2
SEG = 32
CHUNKS = 4

water_level = 0.2
epsilon = 1e-05

BF16 = jnp.bfloat16
F32 = jnp.float32


def forward_table(samples):
    bins = np.arange(F, dtype=np.int64) + 1
    times = np.arange(samples, dtype=np.int64)
    angle = 2.0 * np.pi * (bins[:, None] * times[None, :] % samples) / samples
    taper = 0.5 - 0.5 * np.cos(2.0 * np.pi * times / samples)
    return np.concatenate((np.cos(angle) * taper, -np.sin(angle) * taper)).astype(np.float32)


def inverse_table(samples):
    bins = np.arange(F, dtype=np.int64) + 1
    shifts = np.arange(LAGS, dtype=np.int64) - LAGS // 2
    angle = 2.0 * np.pi * (bins[:, None] * shifts[None, :] % samples) / samples
    scale = 1.0 / np.sqrt(float(SEG * F))
    return np.concatenate((np.cos(angle) * scale, -np.sin(angle) * scale)).astype(np.float32)


def split_const(table):
    high = table.astype(jnp.bfloat16)
    low = (table - high.astype(np.float32)).astype(jnp.bfloat16)
    return high, low


def split(x):
    high = x.astype(BF16)
    low = (x - high.astype(F32)).astype(BF16)
    return high, low


def dot_nt(a, b):
    return lax.dot_general(a, b, (((1,), (1,)), ((), ())), preferred_element_type=F32)


def dot_nn(a, b):
    return lax.dot_general(a, b, (((1,), (0,)), ((), ())), preferred_element_type=F32)


def whiten_tile(real, imag):
    magnitude = jnp.sqrt(real * real + imag * imag)
    row = lax.broadcasted_iota(jnp.int32, magnitude.shape, 0)
    smoothed = magnitude
    for offset in range(1, SMOOTH + 1):
        smoothed = smoothed + jnp.where(row >= offset, pltpu.roll(magnitude, offset, 0), 0.0)
        smoothed = smoothed + jnp.where(row < F - offset, pltpu.roll(magnitude, F - offset, 0), 0.0)
    water_mark = jnp.mean(magnitude, axis=0, keepdims=True)
    divisor = smoothed * (1.0 / (2 * SMOOTH + 1)) + water_level * water_mark + epsilon
    return real / divisor, imag / divisor


def spectra_kernel(place_ref, rec_ref, hi_ref, lo_ref, idx_ref, white_ref, *sent, segs, shards):
    step = pl.program_id(0)
    per, channels, samples = rec_ref.shape
    high, low = split(rec_ref[...].reshape(per * channels, samples))
    spectra = dot_nt(hi_ref[...], high) + (dot_nt(lo_ref[...], high) + dot_nt(hi_ref[...], low))
    for i in range(per):
        lanes = slice(i * channels, (i + 1) * channels)
        real, imag = whiten_tile(spectra[:F, lanes], spectra[F:, lanes])
        seg = step * per + i
        white_ref[pl.ds(seg, F, stride=2 * segs), :] = real
        white_ref[pl.ds(seg + segs, F, stride=2 * segs), :] = imag

    @pl.when(step == pl.num_programs(0) - 1)
    def _():
        shard, half = place_ref[0], place_ref[1]
        nsrc = idx_ref.shape[0]
        per_half = nsrc // 2
        size = per_half // CHUNKS
        rows = F // shards * 2 * segs
        own = pl.multiple_of(half * per_half, per_half)
        other = pl.multiple_of((1 - half) * per_half, per_half)
        index = jnp.concatenate((idx_ref[pl.ds(own, per_half), :], idx_ref[pl.ds(other, per_half), :]))
        lane = lax.broadcasted_iota(jnp.int32, (nsrc, channels), 1)
        hot = (index - shard * channels == lane).astype(F32).astype(BF16)
        hot = jnp.concatenate((hot, hot), axis=1)
        for r in range(shards):
            start = pl.multiple_of((shard ^ r) * rows, rows)
            high, low = split(white_ref[pl.ds(start, rows), :])
            got = dot_nt(hot, jnp.concatenate((high, low), axis=1))
            for j in range(CHUNKS):
                for h in range(2):
                    at = h * per_half + j * size
                    where, slot = place_of(r)
                    sent[4 * j + where][slot, h] = got[at : at + size]


def place_of(r):
    return (r & 1) * 2 + (r >> 1 & 1), r >> 2


def forward(recording, source_channels, shard, half, shards):
    segs, channels, samples = recording.shape
    per = 2
    nsrc = source_channels.shape[0]
    size = nsrc // 2 // CHUNKS
    lanes = F // shards * 2 * segs
    high, low = split_const(forward_table(samples))
    full = lambda shape: pl.BlockSpec(shape, lambda s, p: (0,) * len(shape))
    block = (shards // 4, 2, size, lanes)
    outs = pl.pallas_call(
        functools.partial(spectra_kernel, segs=segs, shards=shards),
        grid_spec=pltpu.PrefetchScalarGridSpec(
            num_scalar_prefetch=1,
            grid=(segs // per,),
            in_specs=[
                pl.BlockSpec((per, channels, samples), lambda s, p: (s, 0, 0)),
                full((2 * F, samples)),
                full((2 * F, samples)),
                full((nsrc, 1)),
            ],
            out_specs=[full((F * 2 * segs, channels))] + [full(block)] * (4 * CHUNKS),
        ),
        out_shape=[jax.ShapeDtypeStruct((F * 2 * segs, channels), F32)]
        + [jax.ShapeDtypeStruct(block, F32)] * (4 * CHUNKS),
        compiler_params=pltpu.CompilerParams(vmem_limit_bytes=40 * 2**20, dimension_semantics=("arbitrary",)),
        cost_estimate=pl.CostEstimate(flops=6 * 10**9, bytes_accessed=16 * 2**20, transcendentals=0),
        name="forward_whiten",
    )(jnp.stack((shard, half)), recording, high, low, source_channels[:, None])
    return outs[0], [outs[1 + 4 * j : 5 + 4 * j] for j in range(CHUNKS)]


def stack_kernel(place_ref, own_ref, oth_ref, hi_ref, lo_ref, *refs, shards, segs, size, per, aliased):
    blocks = refs[: 2 * shards]
    out_ref, real_ref, imag_ref, src_ref = refs[2 * shards + aliased :]
    step = pl.program_id(0)
    channels = own_ref.shape[1]
    bins = F // shards
    width = 2 * segs

    @pl.when(step == 0)
    def _():
        for r in range(shards):
            src_ref[r, 0] = blocks[2 * r][...]
            src_ref[r, 1] = blocks[2 * r + 1][...]

        def block(r, carry):
            base = (place_ref[0] ^ r) * bins
            own_all = src_ref[r, 0]
            oth_all = src_ref[r, 1]
            for i in range(bins):
                at = pl.multiple_of((base + i) * width, width)
                w = jnp.concatenate((own_ref[pl.ds(at, width), :], oth_ref[pl.ds(at, width), :]))
                high, low = split(w)
                turn = lambda v: jnp.concatenate(
                    (v[segs : 2 * segs], -v[:segs], v[3 * segs :], -v[2 * segs : 3 * segs])
                )
                rhs = jnp.concatenate(
                    (
                        jnp.concatenate((high, high, low)),
                        jnp.concatenate((turn(high), turn(high), turn(low))),
                    ),
                    axis=1,
                )
                lanes = slice(i * width, (i + 1) * width)
                shigh, slow = split(jnp.concatenate((own_all[:, lanes], oth_all[:, lanes]), axis=1))
                lhs = jnp.concatenate((shigh, slow, shigh), axis=1)
                row = pl.multiple_of((base + i) * size, size)
                cross = dot_nn(lhs, rhs)
                real_ref[pl.ds(row, size), :] = cross[:, :channels]
                imag_ref[pl.ds(row, size), :] = cross[:, channels:]
            return carry

        lax.fori_loop(0, shards, block, 0)

    for i in range(per):
        n = step * per + i
        both = [jnp.transpose(ref[pl.ds(n, F, stride=size), :]) for ref in (real_ref, imag_ref)]
        high, low = split(jnp.concatenate(both, axis=1))
        out_ref[i] = dot_nn(high, hi_ref[...]) + (dot_nn(low, hi_ref[...]) + dot_nn(high, lo_ref[...]))


def correlate(j, previous, shard, own, other, blocks, shards, segs, samples, nsrc):
    per_half = nsrc // 2
    size = per_half // CHUNKS
    per = 4
    channels = own.shape[1]
    high, low = split_const(inverse_table(samples))
    full = lambda shape: pl.BlockSpec(shape, lambda s, p: (0,) * len(shape))
    steps = size // per
    aliased = previous is not None
    operands = [own, other, high, low, *blocks]
    in_specs = [full(x.shape) for x in operands]
    if aliased:
        operands.append(previous)
        in_specs.append(pl.BlockSpec(memory_space=pl.ANY))
    return pl.pallas_call(
        functools.partial(stack_kernel, shards=shards, segs=segs, size=size, per=per, aliased=aliased),
        grid_spec=pltpu.PrefetchScalarGridSpec(
            num_scalar_prefetch=1,
            grid=(steps,),
            in_specs=in_specs,
            out_specs=pl.BlockSpec((per, channels, LAGS), lambda s, p: (j * steps + s, 0, 0)),
            scratch_shapes=[
                pltpu.VMEM((F * size, channels), F32),
                pltpu.VMEM((F * size, channels), F32),
                pltpu.VMEM((shards, 2, size, F // shards * 2 * segs), F32),
            ],
        ),
        out_shape=jax.ShapeDtypeStruct((per_half, channels, LAGS), F32),
        input_output_aliases={len(operands): 0} if aliased else {},
        compiler_params=pltpu.CompilerParams(vmem_limit_bytes=48 * 2**20, dimension_semantics=("arbitrary",)),
        cost_estimate=pl.CostEstimate(flops=5 * 10**9, bytes_accessed=16 * 2**20, transcendentals=0),
        name="stack_lags",
    )(shard[None], *operands)


def swap(x, axis, bits):
    return lax.ppermute(x, axis, [(i, i ^ bits) for i in range(lax.axis_size(axis))])


def spread_sources(parts):
    even, even_x, odd, odd_x = parts
    shards = 4 * even.shape[0]
    even, even_x = even + swap(odd, "shard", 1), even_x + swap(odd_x, "shard", 1)
    even = even + swap(even_x, "shard", 2)
    mine = even[0]
    for k in range(1, shards // 4):
        mine = mine + swap(even[k], "shard", 4 * k)
    pair = [mine[0], swap(mine[1], "half", 1)]
    blocks = {}
    for h in range(2):
        for k in range(shards // 4):
            blocks[4 * k, h] = swap(pair[h], "shard", 4 * k) if k else pair[h]
    for bit in (2, 1):
        for (r, h), x in list(blocks.items()):
            blocks[r ^ bit, h] = swap(x, "shard", bit)
    return [blocks[r, h] for r in range(shards) for h in range(2)]


def body(recording, source_channels):
    segs, _, samples = recording.shape
    shards = lax.axis_size("shard")
    shard, half = lax.axis_index("shard"), lax.axis_index("half")
    own, parts = forward(recording, source_channels, shard, half, shards)
    other = swap(own, "half", 1)
    result = None
    for j in range(CHUNKS):
        blocks = spread_sources(parts[j])
        result = correlate(
            j, result, shard, own, other, blocks, shards, segs, samples, source_channels.shape[0]
        )
    return result


def plain_forward_table(samples, freq_count):
    table = forward_table(samples)
    return jnp.stack((table[:freq_count], table[freq_count:]), axis=1)


def plain_inverse_table(samples, freq_count):
    table = inverse_table(samples)
    return jnp.stack((table[:freq_count], table[freq_count:]), axis=1)


def plain_whiten(spectra):
    magnitude = jnp.sqrt(spectra[:, 0] * spectra[:, 0] + spectra[:, 1] * spectra[:, 1])
    freq_count = magnitude.shape[0]
    padded = jnp.pad(magnitude, ((SMOOTH, SMOOTH), (0, 0), (0, 0)))
    smoothed = padded[0:freq_count]
    for offset in range(1, 2 * SMOOTH + 1):
        smoothed = smoothed + padded[offset : offset + freq_count]
    smoothed = smoothed / (2 * SMOOTH + 1)
    water_mark = jnp.mean(magnitude, axis=0, keepdims=True)
    divisor = smoothed + water_level * water_mark + epsilon
    return spectra / divisor[:, None]


def plain_correlate(whitened, indices):
    sources = jnp.take(whitened, indices, axis=2)
    src_real, src_imag = (sources[:, 0], sources[:, 1])
    rec_real, rec_imag = (whitened[:, 0], whitened[:, 1])
    high = lax.Precision.HIGHEST
    cross_real = jnp.einsum("fnx,fcx->fnc", src_real, rec_real, precision=high) + jnp.einsum(
        "fnx,fcx->fnc", src_imag, rec_imag, precision=high
    )
    cross_imag = jnp.einsum("fnx,fcx->fnc", src_real, rec_imag, precision=high) - jnp.einsum(
        "fnx,fcx->fnc", src_imag, rec_real, precision=high
    )
    return jnp.stack((cross_real, cross_imag), axis=1)


def plain_body(recording, source_channels):
    samples = recording.shape[2]
    high = lax.Precision.HIGHEST
    spectra = jnp.einsum("fqt,sct->fqcs", plain_forward_table(samples, F), recording, precision=high)
    whitened = plain_whiten(spectra)
    by_freq = lax.all_to_all(whitened, "shard", split_axis=0, concat_axis=2, tiled=True)
    per_half = source_channels.shape[0] // lax.axis_size("half")
    own_sources = lax.dynamic_slice_in_dim(source_channels, lax.axis_index("half") * per_half, per_half)
    combined = jnp.concatenate((by_freq, swap(by_freq, "half", 1)), axis=3)
    cross = plain_correlate(combined, own_sources)
    cross = lax.all_to_all(cross, "shard", split_axis=3, concat_axis=0, tiled=True)
    return jnp.einsum("fqnc,fql->ncl", cross, plain_inverse_table(samples, F), precision=high)


def solution(mesh):
    def run(recording, source_channels):
        shards = lax.axis_size("shard")
        fits = recording.shape[1] % 128 == 0 and shards % 4 == 0 and F % shards == 0
        return (body if fits else plain_body)(recording, source_channels)

    return jax.shard_map(
        run,
        mesh=mesh,
        in_specs=(P("half", "shard", None), P()),
        out_specs=P("half", "shard", None),
        check_vma=False,
    )
```

time: 639 us -> 255 us (0.40)
  the two profiles are of different devices: /device:TPU:11 before, /device:TPU:0 now
where the time goes in v1:
time: 255 us
  starting transfers between devices  113 us (44%)
  Pallas kernels  75.4 us (30%)
  waiting for transfers between devices  60.7 us (24%)
  local copies, waits for them, and re-layouts  4.87 us (2%)
    ppermute x149, starting transfers between devices, swap(): lax.ppermute(x, axis, [(i, i ^ bits) for i in range(lax.axis_size(axis))])  113 us
    pallas_call x4, Pallas kernels, correlate(): pl.pallas_call(functools.partial(stack_kernel, shards=shards, segs=segs,...  64.4 us
    ppermute x149, waiting for transfers between devices, swap(): lax.ppermute(x, axis, [(i, i ^ bits) for i in range(lax.axis_size(axis))])  60.7 us
    pallas_call x1, Pallas kernels, forward(): pl.pallas_call(functools.partial(spectra_kernel, segs=segs, shards=shards...  11.1 us
  transfers between devices with their start and end apart: 149, of which 49 were waited for; matrix products, arithmetic and copies ran while one was open for 0% of the time, Pallas kernels for 19%

profile of v1, /device:TPU:0, one launch (start us, length us, event | category | flops | bytes accessed | tf_op | source)
XLA Modules:
  0.0 254.9 jit_solution(13691969495578155198)
XLA Ops:
  3.0 11.1 %forward_whiten.1 = (f32[4096,128]{1,0:T(8,128)S(1)}, f32[4,2,32,256]{3,2,1,0:T(8,128)S(1)}, f32[4,2,32,256]{3,2,1,0:T(8,128)S(1)}, f32[4,2,32,256]{3,2,1,0:T(8,...) custom-call(s32[2]{0:T(128)S(1)} %pad_add_fusion.place_ref, ...), custom_call_target="tpu_custom_call" | custom-call | flops 6000000000 | bytes 16777216 | tf_op jit(solution)/shard_map/forward_whiten/pallas_call | solution.py:121
  15.8 2.9 %collective-permute-start.3 = (f32[4,2,32,256]{3,2,1,0:T(8,128)S(1)}, f32[4,2,32,256]{3,2,1,0:T(8,128)S(1)}, u32[]{:S(2)}, u32[]{:S(2)}) collective-permute-start(f32[4,2,32,256]{3,2,1,0:T(8,128)S(1)} %add.73), channel_id=1, source_target_pairs={{0,2},{1,3},{2,0},{3,1},{4,6},{5,7},{6,4},{7,5},{8,10},{9,11},{10,... | collective-permute-start | bytes 786440 | tf_op jit(solution)/shard_map/ppermute | solution.py:229
  20.1 5.7 %collective-permute-done.3 = f32[4,2,32,256]{3,2,1,0:T(8,128)S(1)} collective-permute-done((f32[4,2,32,256]{3,2,1,0:T(8,128)S(1)}, f32[4,2,32,256]{3,2,1,0:T(8,128)S(1)}, u32[]{:S(2)}, u32[]{:S(2)}) %collective-permute-start.3) | collective-permute-done | bytes 262176 | tf_op jit(solution)/shard_map/ppermute | solution.py:229
  25.8 2.1 collective-permute-start.77
  29.5 1.9 collective-permute-done.40
  31.4 2.1 collective-permute-start.114
  33.5 1.6 collective-permute-start.4
  35.2 1.8 collective-permute-done.77
  37.0 4.2 %collective-permute-start.6 = (f32[2,32,256]{2,1,0:T(8,128)S(1)}, f32[2,32,256]{2,1,0:T(8,128)S(1)}, u32[]{:S(2)}, u32[]{:S(2)}) collective-permute-start(f32[2,32,256]{2,1,0:T(8,128)S(1)} %get-tuple-element.49), channel_id=1, source_target_pairs={{0,12},{1,13},{2,14},{3,15},{4,8},{5,9},{6,10},{7,11},{8,4},{9,5},... | collective-permute-start | bytes 196616 | tf_op jit(solution)/shard_map/ppermute | solution.py:229
  42.1 1.8 collective-permute-start.41
  44.1 2.5 collective-permute-start.43
  46.8 1.7 collective-permute-start.78
  48.6 2.6 %collective-permute-start.80 = (f32[2,32,256]{2,1,0:T(8,128)S(1)}, f32[2,32,256]{2,1,0:T(8,128)S(1)}, u32[]{:S(2)}, u32[]{:S(2)}) collective-permute-start(f32[2,32,256]{2,1,0:T(8,128)S(1)} %get-tuple-element.43), channel_id=1, source_target_pairs={{0,12},{1,13},{2,14},{3,15},{4,8},{5,9},{6,10},{7,11},{8,4},{9,5},... | collective-permute-start | bytes 196616 | tf_op jit(solution)/shard_map/ppermute | solution.py:229
  51.2 3.1 %collective-permute-start.79 = (f32[2,32,256]{2,1,0:T(8,128)S(1)}, f32[2,32,256]{2,1,0:T(8,128)S(1)}, u32[]{:S(2)}, u32[]{:S(2)}) collective-permute-start(f32[2,32,256]{2,1,0:T(8,128)S(1)} %get-tuple-element.44), channel_id=1, source_target_pairs={{0,8},{1,9},{2,10},{3,11},{4,12},{5,13},{6,14},{7,15},{8,0},{9,1},... | collective-permute-start | bytes 196616 | tf_op jit(solution)/shard_map/ppermute | solution.py:229
  55.4 2.6 %collective-permute-start.117 = (f32[2,32,256]{2,1,0:T(8,128)S(1)}, f32[2,32,256]{2,1,0:T(8,128)S(1)}, u32[]{:S(2)}, u32[]{:S(2)}) collective-permute-start(f32[2,32,256]{2,1,0:T(8,128)S(1)} %get-tuple-element.40), channel_id=1, source_target_pairs={{0,12},{1,13},{2,14},{3,15},{4,8},{5,9},{6,10},{7,11},{8,4},{9,5},... | collective-permute-start | bytes 196616 | tf_op jit(solution)/shard_map/ppermute | solution.py:229
  61.7 2.6 %collective-permute-start.30 = (f32[32,256]{1,0:T(8,128)S(1)}, f32[32,256]{1,0:T(8,128)S(1)}, u32[]{:S(2)}, u32[]{:S(2)}) collective-permute-start(f32[32,256]{1,0:T(8,128)S(1)} %get-tuple-element.58.refs_0_), channel_id=1, source_target_pairs={{0,12},{1,13},{2,14},{3,15},{4,8},{5,9},{6,10},{7,11},{8,4},{9,5},... | collective-permute-start | bytes 98312 | tf_op jit(solution)/shard_map/ppermute | solution.py:229
  66.2 8.3 %collective-permute-done.7.refs_1_ = f32[32,256]{1,0:T(8,128)S(1)} collective-permute-done((f32[32,256]{1,0:T(8,128)S(1)}, f32[32,256]{1,0:T(8,128)S(1)}, u32[]{:S(2)}, u32[]{:S(2)}) %collective-permute-start.7) | collective-permute-done | bytes 32800 | tf_op jit(solution)/shard_map/ppermute | solution.py:229
  75.2 3.6 %collective-permute-start.67 = (f32[32,256]{1,0:T(8,128)S(1)}, f32[32,256]{1,0:T(8,128)S(1)}, u32[]{:S(2)}, u32[]{:S(2)}) collective-permute-start(f32[32,256]{1,0:T(8,128)S(1)} %get-tuple-element.56.refs_0_), channel_id=1, source_target_pairs={{0,12},{1,13},{2,14},{3,15},{4,8},{5,9},{6,10},{7,11},{8,4},{9,5},... | collective-permute-start | bytes 98312 | tf_op jit(solution)/shard_map/ppermute | solution.py:229
  85.9 2.2 collective-permute-start.104
  93.4 2.7 %collective-permute-start.141 = (f32[32,256]{1,0:T(8,128)S(1)}, f32[32,256]{1,0:T(8,128)S(1)}, u32[]{:S(2)}, u32[]{:S(2)}) collective-permute-start(f32[32,256]{1,0:T(8,128)S(1)} %get-tuple-element.52.refs_0_), channel_id=1, source_target_pairs={{0,12},{1,13},{2,14},{3,15},{4,8},{5,9},{6,10},{7,11},{8,4},{9,5},... | collective-permute-start | bytes 98312 | tf_op jit(solution)/shard_map/ppermute | solution.py:229
  96.2 1.6 collective-permute-start.125
  99.4 1.6 collective-permute-done.133.refs_16_
  103.0 2.4 collective-permute-start.15
  110.0 1.6 collective-permute-done.34.refs_28_
  116.0 2.1 collective-permute-start.52
  122.8 1.8 collective-permute-done.71.refs_28_
  126.0 1.8 collective-permute-start.105
  128.6 2.2 collective-permute-start.89
  132.0 1.6 collective-permute-done.97.refs_17_
  135.8 1.8 collective-permute-done.108.refs_28_
  138.7 2.4 collective-permute-start.142
  141.6 1.9 collective-permute-start.126
  144.7 1.8 collective-permute-done.134.refs_17_
  148.8 1.8 collective-permute-done.145.refs_28_
  151.4 1.8 collective-permute-start.35
  155.3 1.8 collective-permute-start.19
  157.1 1.7 collective-permute-done.27.refs_21_
  159.3 1.7 collective-permute-start.72
  161.6 1.6 collective-permute-done.72.refs_29_
  163.2 1.9 collective-permute-start.56
  167.1 1.9 collective-permute-start.109
  171.0 2.1 collective-permute-start.93
  175.0 2.0 collective-permute-start.146
  178.9 2.2 collective-permute-start.130
  187.8 16.1 %stack_lags.4.refs_32_ = f32[128,128,512]{2,1,0:T(8,128)} custom-call(s32[1]{0:T(128)} %bitcast.place_ref, f32[4096,128]{1,0:T(8,128)S(1)} %get-tuple-element.22.own_ref, f32[4096,128]{1,0:T(8,128)S(1)} %collective-permute-done.oth_ref, bf16[256,512]{1,0:T(8,128)(2,1)S(1)} %copy-done.1, bf16[256,512]{1,0:T(8,128)(2,1)S(1)} %copy-done, ...), custom_call_target="tpu_custom_call" | custom-call | flops 5000000000 | bytes 16777216 | tf_op jit(solution)/shard_map/stack_lags/pallas_call | solution.py:207
  205.1 16.1 %stack_lags.5.refs_32_ = f32[128,128,512]{2,1,0:T(8,128)} custom-call(s32[1]{0:T(128)} %bitcast.place_ref, f32[4096,128]{1,0:T(8,128)S(1)} %get-tuple-element.22.own_ref, f32[4096,128]{1,0:T(8,128)S(1)} %collective-permute-done.oth_ref, bf16[256,512]{1,0:T(8,128)(2,1)S(1)} %copy-done.1, ...), custom_call_target="tpu_custom_call", output_to_operand_aliasing={{}: (37, {})} | custom-call | flops 5000000000 | bytes 16777216 | tf_op jit(solution)/shard_map/stack_lags/pallas_call | solution.py:207
  222.6 16.1 %stack_lags.6.refs_32_ = f32[128,128,512]{2,1,0:T(8,128)} custom-call(s32[1]{0:T(128)} %bitcast.place_ref, f32[4096,128]{1,0:T(8,128)S(1)} %get-tuple-element.22.own_ref, f32[4096,128]{1,0:T(8,128)S(1)} %collective-permute-done.oth_ref, bf16[256,512]{1,0:T(8,128)(2,1)S(1)} %copy-done.1, ...), custom_call_target="tpu_custom_call", output_to_operand_aliasing={{}: (37, {})} | custom-call | flops 5000000000 | bytes 16777216 | tf_op jit(solution)/shard_map/stack_lags/pallas_call | solution.py:207
  238.7 16.2 %stack_lags.7 = f32[128,128,512]{2,1,0:T(8,128)} custom-call(s32[1]{0:T(128)} %bitcast.place_ref, f32[4096,128]{1,0:T(8,128)S(1)} %get-tuple-element.22.own_ref, f32[4096,128]{1,0:T(8,128)S(1)} %collective-permute-done.oth_ref, bf16[256,512]{1,0:T(8,128)(2,1)S(1)} %copy-done.1, bf16[256,512]{1,0:T(8,128)(2,1)S(1)} %copy-done, ...), custom_call_target="tpu_custom_call", output_to_operand_aliasing={{}: (37, {})} | custom-call | flops 5000000000 | bytes 16777216 | tf_op jit(solution)/shard_map/stack_lags/pallas_call | solution.py:207
  (285 shorter events, 77.4 us)
Async XLA Ops:
  15.8 10.0 %collective-permute-start.3 = (f32[4,2,32,256]{3,2,1,0:T(8,128)S(1)}, f32[4,2,32,256]{3,2,1,0:T(8,128)S(1)}, u32[]{:S(2)}, u32[]{:S(2)}) collective-permute-start(f32[4,2,32,256]{3,2,1,0:T(8,128)S(1)} %add.73), channel_id=1, source_target_pairs={{0,2},{1,3},{2,0},{3,1},{4,6},{5,7},{6,4},{7,5},{8,10},{9,11},{10,... | collective-permute-start | bytes 786440 | tf_op jit(solution)/shard_map/ppermute | solution.py:229
  18.7 9.2 %collective-permute-start.38 = (f32[4,2,32,256]{3,2,1,0:T(8,128)S(1)}, f32[4,2,32,256]{3,2,1,0:T(8,128)S(1)}, u32[]{:S(2)}, u32[]{:S(2)}) collective-permute-start(f32[4,2,32,256]{3,2,1,0:T(8,128)S(1)} %get-tuple-element.28), channel_id=1, source_target_pairs={{0,1},{1,0},{2,3},{3,2},{4,5},{5,4},{6,7},{7,6},{8,9},{9,8},{10,11... | collective-permute-start | bytes 786440 | tf_op jit(solution)/shard_map/ppermute | solution.py:229
  18.7 14.8 %collective-permute-start.75 = (f32[4,2,32,256]{3,2,1,0:T(8,128)S(1)}, f32[4,2,32,256]{3,2,1,0:T(8,128)S(1)}, u32[]{:S(2)}, u32[]{:S(2)}) collective-permute-start(f32[4,2,32,256]{3,2,1,0:T(8,128)S(1)} %get-tuple-element.32), channel_id=1, source_target_pairs={{0,1},{1,0},{2,3},{3,2},{4,5},{5,4},{6,7},{7,6},{8,9},{9,8},{10,11... | collective-permute-start | bytes 786440 | tf_op jit(solution)/shard_map/ppermute | solution.py:229
  19.4 21.9 %collective-permute-start.112 = (f32[4,2,32,256]{3,2,1,0:T(8,128)S(1)}, f32[4,2,32,256]{3,2,1,0:T(8,128)S(1)}, u32[]{:S(2)}, u32[]{:S(2)}) collective-permute-start(f32[4,2,32,256]{3,2,1,0:T(8,128)S(1)} %get-tuple-element.36), channel_id=1, source_target_pairs={{0,1},{1,0},{2,3},{3,2},{4,5},{5,4},{6,7},{7,6},{8,9},{9,8},{10,11... | collective-permute-start | bytes 786440 | tf_op jit(solution)/shard_map/ppermute | solution.py:229
  19.5 11.9 %collective-permute-start.40 = (f32[4,2,32,256]{3,2,1,0:T(8,128)S(1)}, f32[4,2,32,256]{3,2,1,0:T(8,128)S(1)}, u32[]{:S(2)}, u32[]{:S(2)}) collective-permute-start(f32[4,2,32,256]{3,2,1,0:T(8,128)S(1)} %add.79), channel_id=1, source_target_pairs={{0,2},{1,3},{2,0},{3,1},{4,6},{5,7},{6,4},{7,5},{8,10},{9,11},{10,... | collective-permute-start | bytes 786440 | tf_op jit(solution)/shard_map/ppermute | solution.py:229
  25.8 11.2 %collective-permute-start.77 = (f32[4,2,32,256]{3,2,1,0:T(8,128)S(1)}, f32[4,2,32,256]{3,2,1,0:T(8,128)S(1)}, u32[]{:S(2)}, u32[]{:S(2)}) collective-permute-start(f32[4,2,32,256]{3,2,1,0:T(8,128)S(1)} %add.85), channel_id=1, source_target_pairs={{0,2},{1,3},{2,0},{3,1},{4,6},{5,7},{6,4},{7,5},{8,10},{9,11},{10,... | collective-permute-start | bytes 786440 | tf_op jit(solution)/shard_map/ppermute | solution.py:229
  27.9 157.7 %collective-permute-start = (f32[4096,128]{1,0:T(8,128)S(1)}, f32[4096,128]{1,0:T(8,128)S(1)}, u32[]{:S(2)}, u32[]{:S(2)}) collective-permute-start(f32[4096,128]{1,0:T(8,128)S(1)} %get-tuple-element.22.own_ref), channel_id=1, source_target_pairs={{0,16},{16,0},{1,17},{17,1},{2,18},{18,2},{3,19},{19,3},{4,20},{20... | collective-permute-start | bytes 6291464 | tf_op jit(solution)/shard_map/ppermute | solution.py:229
  31.4 10.8 %collective-permute-start.114 = (f32[4,2,32,256]{3,2,1,0:T(8,128)S(1)}, f32[4,2,32,256]{3,2,1,0:T(8,128)S(1)}, u32[]{:S(2)}, u32[]{:S(2)}) collective-permute-start(f32[4,2,32,256]{3,2,1,0:T(8,128)S(1)} %add.91), channel_id=1, source_target_pairs={{0,2},{1,3},{2,0},{3,1},{4,6},{5,7},{6,4},{7,5},{8,10},{9,11},{10,... | collective-permute-start | bytes 786440 | tf_op jit(solution)/shard_map/ppermute | solution.py:229
  33.5 10.5 %collective-permute-start.4 = (f32[2,32,256]{2,1,0:T(8,128)S(1)}, f32[2,32,256]{2,1,0:T(8,128)S(1)}, u32[]{:S(2)}, u32[]{:S(2)}) collective-permute-start(f32[2,32,256]{2,1,0:T(8,128)S(1)} %get-tuple-element.48), channel_id=1, source_target_pairs={{0,4},{1,5},{2,6},{3,7},{4,0},{5,1},{6,2},{7,3},{8,12},{9,13},{10,... | collective-permute-start | bytes 196616 | tf_op jit(solution)/shard_map/ppermute | solution.py:229
  37.0 9.6 %collective-permute-start.6 = (f32[2,32,256]{2,1,0:T(8,128)S(1)}, f32[2,32,256]{2,1,0:T(8,128)S(1)}, u32[]{:S(2)}, u32[]{:S(2)}) collective-permute-start(f32[2,32,256]{2,1,0:T(8,128)S(1)} %get-tuple-element.49), channel_id=1, source_target_pairs={{0,12},{1,13},{2,14},{3,15},{4,8},{5,9},{6,10},{7,11},{8,4},{9,5},... | collective-permute-start | bytes 196616 | tf_op jit(solution)/shard_map/ppermute | solution.py:229
  42.1 6.4 %collective-permute-start.41 = (f32[2,32,256]{2,1,0:T(8,128)S(1)}, f32[2,32,256]{2,1,0:T(8,128)S(1)}, u32[]{:S(2)}, u32[]{:S(2)}) collective-permute-start(f32[2,32,256]{2,1,0:T(8,128)S(1)} %get-tuple-element.45), channel_id=1, source_target_pairs={{0,4},{1,5},{2,6},{3,7},{4,0},{5,1},{6,2},{7,3},{8,12},{9,13},{10,... | collective-permute-start | bytes 196616 | tf_op jit(solution)/shard_map/ppermute | solution.py:229
  44.1 7.1 %collective-permute-start.43 = (f32[2,32,256]{2,1,0:T(8,128)S(1)}, f32[2,32,256]{2,1,0:T(8,128)S(1)}, u32[]{:S(2)}, u32[]{:S(2)}) collective-permute-start(f32[2,32,256]{2,1,0:T(8,128)S(1)} %get-tuple-element.46), channel_id=1, source_target_pairs={{0,12},{1,13},{2,14},{3,15},{4,8},{5,9},{6,10},{7,11},{8,4},{9,5},... | collective-permute-start | bytes 196616 | tf_op jit(solution)/shard_map/ppermute | solution.py:229
  46.6 8.7 %collective-permute-start.42 = (f32[2,32,256]{2,1,0:T(8,128)S(1)}, f32[2,32,256]{2,1,0:T(8,128)S(1)}, u32[]{:S(2)}, u32[]{:S(2)}) collective-permute-start(f32[2,32,256]{2,1,0:T(8,128)S(1)} %get-tuple-element.47), channel_id=1, source_target_pairs={{0,8},{1,9},{2,10},{3,11},{4,12},{5,13},{6,14},{7,15},{8,0},{9,1},... | collective-permute-start | bytes 196616 | tf_op jit(solution)/shard_map/ppermute | solution.py:229
  46.8 8.6 %collective-permute-start.78 = (f32[2,32,256]{2,1,0:T(8,128)S(1)}, f32[2,32,256]{2,1,0:T(8,128)S(1)}, u32[]{:S(2)}, u32[]{:S(2)}) collective-permute-start(f32[2,32,256]{2,1,0:T(8,128)S(1)} %get-tuple-element.42), channel_id=1, source_target_pairs={{0,4},{1,5},{2,6},{3,7},{4,0},{5,1},{6,2},{7,3},{8,12},{9,13},{10,... | collective-permute-start | bytes 196616 | tf_op jit(solution)/shard_map/ppermute | solution.py:229
  48.6 9.4 %collective-permute-start.80 = (f32[2,32,256]{2,1,0:T(8,128)S(1)}, f32[2,32,256]{2,1,0:T(8,128)S(1)}, u32[]{:S(2)}, u32[]{:S(2)}) collective-permute-start(f32[2,32,256]{2,1,0:T(8,128)S(1)} %get-tuple-element.43), channel_id=1, source_target_pairs={{0,12},{1,13},{2,14},{3,15},{4,8},{5,9},{6,10},{7,11},{8,4},{9,5},... | collective-permute-start | bytes 196616 | tf_op jit(solution)/shard_map/ppermute | solution.py:229
  51.2 9.0 %collective-permute-start.79 = (f32[2,32,256]{2,1,0:T(8,128)S(1)}, f32[2,32,256]{2,1,0:T(8,128)S(1)}, u32[]{:S(2)}, u32[]{:S(2)}) collective-permute-start(f32[2,32,256]{2,1,0:T(8,128)S(1)} %get-tuple-element.44), channel_id=1, source_target_pairs={{0,8},{1,9},{2,10},{3,11},{4,12},{5,13},{6,14},{7,15},{8,0},{9,1},... | collective-permute-start | bytes 196616 | tf_op jit(solution)/shard_map/ppermute | solution.py:229
  55.3 6.4 %collective-permute-start.115 = (f32[2,32,256]{2,1,0:T(8,128)S(1)}, f32[2,32,256]{2,1,0:T(8,128)S(1)}, u32[]{:S(2)}, u32[]{:S(2)}) collective-permute-start(f32[2,32,256]{2,1,0:T(8,128)S(1)} %get-tuple-element.39), channel_id=1, source_target_pairs={{0,4},{1,5},{2,6},{3,7},{4,0},{5,1},{6,2},{7,3},{8,12},{9,13},{10,... | collective-permute-start | bytes 196616 | tf_op jit(solution)/shard_map/ppermute | solution.py:229
  55.4 9.0 %collective-permute-start.117 = (f32[2,32,256]{2,1,0:T(8,128)S(1)}, f32[2,32,256]{2,1,0:T(8,128)S(1)}, u32[]{:S(2)}, u32[]{:S(2)}) collective-permute-start(f32[2,32,256]{2,1,0:T(8,128)S(1)} %get-tuple-element.40), channel_id=1, source_target_pairs={{0,12},{1,13},{2,14},{3,15},{4,8},{5,9},{6,10},{7,11},{8,4},{9,5},... | collective-permute-start | bytes 196616 | tf_op jit(solution)/shard_map/ppermute | solution.py:229
  58.0 7.4 %collective-permute-start.116 = (f32[2,32,256]{2,1,0:T(8,128)S(1)}, f32[2,32,256]{2,1,0:T(8,128)S(1)}, u32[]{:S(2)}, u32[]{:S(2)}) collective-permute-start(f32[2,32,256]{2,1,0:T(8,128)S(1)} %get-tuple-element.41), channel_id=1, source_target_pairs={{0,8},{1,9},{2,10},{3,11},{4,12},{5,13},{6,14},{7,15},{8,0},{9,1},... | collective-permute-start | bytes 196616 | tf_op jit(solution)/shard_map/ppermute | solution.py:229
  60.2 14.2 %collective-permute-start.7 = (f32[32,256]{1,0:T(8,128)S(1)}, f32[32,256]{1,0:T(8,128)S(1)}, u32[]{:S(2)}, u32[]{:S(2)}) collective-permute-start(f32[32,256]{1,0:T(8,128)S(1)} %get-tuple-element.57), channel_id=1, source_target_pairs={{0,16},{16,0},{1,17},{17,1},{2,18},{18,2},{3,19},{19,3},{4,20},{20... | collective-permute-start | bytes 98312 | tf_op jit(solution)/shard_map/ppermute | solution.py:229
  61.7 13.3 %collective-permute-start.30 = (f32[32,256]{1,0:T(8,128)S(1)}, f32[32,256]{1,0:T(8,128)S(1)}, u32[]{:S(2)}, u32[]{:S(2)}) collective-permute-start(f32[32,256]{1,0:T(8,128)S(1)} %get-tuple-element.58.refs_0_), channel_id=1, source_target_pairs={{0,12},{1,13},{2,14},{3,15},{4,8},{5,9},{6,10},{7,11},{8,4},{9,5},... | collective-permute-start | bytes 98312 | tf_op jit(solution)/shard_map/ppermute | solution.py:229
  64.4 10.8 %collective-permute-start.22 = (f32[32,256]{1,0:T(8,128)S(1)}, f32[32,256]{1,0:T(8,128)S(1)}, u32[]{:S(2)}, u32[]{:S(2)}) collective-permute-start(f32[32,256]{1,0:T(8,128)S(1)} %get-tuple-element.58.refs_0_), channel_id=1, source_target_pairs={{0,8},{1,9},{2,10},{3,11},{4,12},{5,13},{6,14},{7,15},{8,0},{9,1},... | collective-permute-start | bytes 98312 | tf_op jit(solution)/shard_map/ppermute | solution.py:229
  65.4 13.4 %collective-permute-start.14 = (f32[32,256]{1,0:T(8,128)S(1)}, f32[32,256]{1,0:T(8,128)S(1)}, u32[]{:S(2)}, u32[]{:S(2)}) collective-permute-start(f32[32,256]{1,0:T(8,128)S(1)} %get-tuple-element.58.refs_0_), channel_id=1, source_target_pairs={{0,4},{1,5},{2,6},{3,7},{4,0},{5,1},{6,2},{7,3},{8,12},{9,13},{10,... | collective-permute-start | bytes 98312 | tf_op jit(solution)/shard_map/ppermute | solution.py:229
  75.2 9.1 %collective-permute-start.67 = (f32[32,256]{1,0:T(8,128)S(1)}, f32[32,256]{1,0:T(8,128)S(1)}, u32[]{:S(2)}, u32[]{:S(2)}) collective-permute-start(f32[32,256]{1,0:T(8,128)S(1)} %get-tuple-element.56.refs_0_), channel_id=1, source_target_pairs={{0,12},{1,13},{2,14},{3,15},{4,8},{5,9},{6,10},{7,11},{8,4},{9,5},... | collective-permute-start | bytes 98312 | tf_op jit(solution)/shard_map/ppermute | solution.py:229
  84.3 6.1 %collective-permute-start.81 = (f32[32,256]{1,0:T(8,128)S(1)}, f32[32,256]{1,0:T(8,128)S(1)}, u32[]{:S(2)}, u32[]{:S(2)}) collective-permute-start(f32[32,256]{1,0:T(8,128)S(1)} %get-tuple-element.53), channel_id=1, source_target_pairs={{0,16},{16,0},{1,17},{17,1},{2,18},{18,2},{3,19},{19,3},{4,20},{20... | collective-permute-start | bytes 98312 | tf_op jit(solution)/shard_map/ppermute | solution.py:229
  85.9 5.8 %collective-permute-start.104 = (f32[32,256]{1,0:T(8,128)S(1)}, f32[32,256]{1,0:T(8,128)S(1)}, u32[]{:S(2)}, u32[]{:S(2)}) collective-permute-start(f32[32,256]{1,0:T(8,128)S(1)} %get-tuple-element.54.refs_0_), channel_id=1, source_target_pairs={{0,12},{1,13},{2,14},{3,15},{4,8},{5,9},{6,10},{7,11},{8,4},{9,5},... | collective-permute-start | bytes 98312 | tf_op jit(solution)/shard_map/ppermute | solution.py:229
  90.4 5.8 %collective-permute-start.84 = (f32[32,256]{1,0:T(8,128)S(1)}, f32[32,256]{1,0:T(8,128)S(1)}, u32[]{:S(2)}, u32[]{:S(2)}) collective-permute-start(f32[32,256]{1,0:T(8,128)S(1)} %get-tuple-element.54.refs_0_), channel_id=1, source_target_pairs={{0,2},{1,3},{2,0},{3,1},{4,6},{5,7},{6,4},{7,5},{8,10},{9,11},{10,... | collective-permute-start | bytes 98312 | tf_op jit(solution)/shard_map/ppermute | solution.py:229
  93.4 6.0 %collective-permute-start.141 = (f32[32,256]{1,0:T(8,128)S(1)}, f32[32,256]{1,0:T(8,128)S(1)}, u32[]{:S(2)}, u32[]{:S(2)}) collective-permute-start(f32[32,256]{1,0:T(8,128)S(1)} %get-tuple-element.52.refs_0_), channel_id=1, source_target_pairs={{0,12},{1,13},{2,14},{3,15},{4,8},{5,9},{6,10},{7,11},{8,4},{9,5},... | collective-permute-start | bytes 98312 | tf_op jit(solution)/shard_map/ppermute | solution.py:229
  96.2 6.4 %collective-permute-start.125 = (f32[32,256]{1,0:T(8,128)S(1)}, f32[32,256]{1,0:T(8,128)S(1)}, u32[]{:S(2)}, u32[]{:S(2)}) collective-permute-start(f32[32,256]{1,0:T(8,128)S(1)} %get-tuple-element.52.refs_0_), channel_id=1, source_target_pairs={{0,4},{1,5},{2,6},{3,7},{4,0},{5,1},{6,2},{7,3},{8,12},{9,13},{10,... | collective-permute-start | bytes 98312 | tf_op jit(solution)/shard_map/ppermute | solution.py:229
  99.4 6.0 %collective-permute-start.119 = (f32[32,256]{1,0:T(8,128)S(1)}, f32[32,256]{1,0:T(8,128)S(1)}, u32[]{:S(2)}, u32[]{:S(2)}) collective-permute-start(f32[32,256]{1,0:T(8,128)S(1)} %get-tuple-element.52.refs_0_), channel_id=1, source_target_pairs={{0,1},{1,0},{2,3},{3,2},{4,5},{5,4},{6,7},{7,6},{8,9},{9,8},{10,11... | collective-permute-start | bytes 98312 | tf_op jit(solution)/shard_map/ppermute | solution.py:229
  113.5 6.0 %collective-permute-start.68 = (f32[32,256]{1,0:T(8,128)S(1)}, f32[32,256]{1,0:T(8,128)S(1)}, u32[]{:S(2)}, u32[]{:S(2)}) collective-permute-start(f32[32,256]{1,0:T(8,128)S(1)} %collective-permute-done.44.refs_1_), channel_id=1, source_target_pairs={{0,12},{1,13},{2,14},{3,15},{4,8},{5,9},{6,10},{7,11},{8,4},{9,5},... | collective-permute-start | bytes 98312 | tf_op jit(solution)/shard_map/ppermute | solution.py:229
  126.0 6.0 %collective-permute-start.105 = (f32[32,256]{1,0:T(8,128)S(1)}, f32[32,256]{1,0:T(8,128)S(1)}, u32[]{:S(2)}, u32[]{:S(2)}) collective-permute-start(f32[32,256]{1,0:T(8,128)S(1)} %collective-permute-done.81.refs_1_), channel_id=1, source_target_pairs={{0,12},{1,13},{2,14},{3,15},{4,8},{5,9},{6,10},{7,11},{8,4},{9,5},... | collective-permute-start | bytes 98312 | tf_op jit(solution)/shard_map/ppermute | solution.py:229
  138.7 6.0 %collective-permute-start.142 = (f32[32,256]{1,0:T(8,128)S(1)}, f32[32,256]{1,0:T(8,128)S(1)}, u32[]{:S(2)}, u32[]{:S(2)}) collective-permute-start(f32[32,256]{1,0:T(8,128)S(1)} %collective-permute-done.118.refs_1_), channel_id=1, source_target_pairs={{0,12},{1,13},{2,14},{3,15},{4,8},{5,9},{6,10},{7,11},{8,4},{9,5},... | collective-permute-start | bytes 98312 | tf_op jit(solution)/shard_map/ppermute | solution.py:229
  184.4 19.6 %collective-permute-start.102 = (f32[32,256]{1,0:T(8,128)S(1)}, f32[32,256]{1,0:T(8,128)S(1)}, u32[]{:S(2)}, u32[]{:S(2)}) collective-permute-start(f32[32,256]{1,0:T(8,128)S(1)} %collective-permute-done.100.refs_20_), channel_id=1, source_target_pairs={{0,1},{1,0},{2,3},{3,2},{4,5},{5,4},{6,7},{7,6},{8,9},{9,8},{10,11... | collective-permute-start | bytes 98312 | tf_op jit(solution)/shard_map/ppermute | solution.py:229
  184.7 19.3 %collective-permute-start.94 = (f32[32,256]{1,0:T(8,128)S(1)}, f32[32,256]{1,0:T(8,128)S(1)}, u32[]{:S(2)}, u32[]{:S(2)}) collective-permute-start(f32[32,256]{1,0:T(8,128)S(1)} %collective-permute-done.92.refs_12_), channel_id=1, source_target_pairs={{0,1},{1,0},{2,3},{3,2},{4,5},{5,4},{6,7},{7,6},{8,9},{9,8},{10,11... | collective-permute-start | bytes 98312 | tf_op jit(solution)/shard_map/ppermute | solution.py:229
  184.9 19.6 %collective-permute-start.111 = (f32[32,256]{1,0:T(8,128)S(1)}, f32[32,256]{1,0:T(8,128)S(1)}, u32[]{:S(2)}, u32[]{:S(2)}) collective-permute-start(f32[32,256]{1,0:T(8,128)S(1)} %collective-permute-done.109.refs_29_), channel_id=1, source_target_pairs={{0,1},{1,0},{2,3},{3,2},{4,5},{5,4},{6,7},{7,6},{8,9},{9,8},{10,11... | collective-permute-start | bytes 98312 | tf_op jit(solution)/shard_map/ppermute | solution.py:229
  185.4 19.2 %collective-permute-start.103 = (f32[32,256]{1,0:T(8,128)S(1)}, f32[32,256]{1,0:T(8,128)S(1)}, u32[]{:S(2)}, u32[]{:S(2)}) collective-permute-start(f32[32,256]{1,0:T(8,128)S(1)} %collective-permute-done.101.refs_21_), channel_id=1, source_target_pairs={{0,1},{1,0},{2,3},{3,2},{4,5},{5,4},{6,7},{7,6},{8,9},{9,8},{10,11... | collective-permute-start | bytes 98312 | tf_op jit(solution)/shard_map/ppermute | solution.py:229
  185.6 19.4 %collective-permute-start.95 = (f32[32,256]{1,0:T(8,128)S(1)}, f32[32,256]{1,0:T(8,128)S(1)}, u32[]{:S(2)}, u32[]{:S(2)}) collective-permute-start(f32[32,256]{1,0:T(8,128)S(1)} %collective-permute-done.93.refs_13_), channel_id=1, source_target_pairs={{0,1},{1,0},{2,3},{3,2},{4,5},{5,4},{6,7},{7,6},{8,9},{9,8},{10,11... | collective-permute-start | bytes 98312 | tf_op jit(solution)/shard_map/ppermute | solution.py:229
  203.9 17.2 %collective-permute-start.65 = (f32[32,256]{1,0:T(8,128)S(1)}, f32[32,256]{1,0:T(8,128)S(1)}, u32[]{:S(2)}, u32[]{:S(2)}) collective-permute-start(f32[32,256]{1,0:T(8,128)S(1)} %collective-permute-done.63.refs_20_), channel_id=1, source_target_pairs={{0,1},{1,0},{2,3},{3,2},{4,5},{5,4},{6,7},{7,6},{8,9},{9,8},{10,11... | collective-permute-start | bytes 98312 | tf_op jit(solution)/shard_map/ppermute | solution.py:229
  204.1 17.5 %collective-permute-start.57 = (f32[32,256]{1,0:T(8,128)S(1)}, f32[32,256]{1,0:T(8,128)S(1)}, u32[]{:S(2)}, u32[]{:S(2)}) collective-permute-start(f32[32,256]{1,0:T(8,128)S(1)} %collective-permute-done.55.refs_12_), channel_id=1, source_target_pairs={{0,1},{1,0},{2,3},{3,2},{4,5},{5,4},{6,7},{7,6},{8,9},{9,8},{10,11... | collective-permute-start | bytes 98312 | tf_op jit(solution)/shard_map/ppermute | solution.py:229
  204.5 17.2 %collective-permute-start.74 = (f32[32,256]{1,0:T(8,128)S(1)}, f32[32,256]{1,0:T(8,128)S(1)}, u32[]{:S(2)}, u32[]{:S(2)}) collective-permute-start(f32[32,256]{1,0:T(8,128)S(1)} %collective-permute-done.72.refs_29_), channel_id=1, source_target_pairs={{0,1},{1,0},{2,3},{3,2},{4,5},{5,4},{6,7},{7,6},{8,9},{9,8},{10,11... | collective-permute-start | bytes 98312 | tf_op jit(solution)/shard_map/ppermute | solution.py:229
  204.6 17.5 %collective-permute-start.66 = (f32[32,256]{1,0:T(8,128)S(1)}, f32[32,256]{1,0:T(8,128)S(1)}, u32[]{:S(2)}, u32[]{:S(2)}) collective-permute-start(f32[32,256]{1,0:T(8,128)S(1)} %collective-permute-done.64.refs_21_), channel_id=1, source_target_pairs={{0,1},{1,0},{2,3},{3,2},{4,5},{5,4},{6,7},{7,6},{8,9},{9,8},{10,11... | collective-permute-start | bytes 98312 | tf_op jit(solution)/shard_map/ppermute | solution.py:229
  205.0 17.2 %collective-permute-start.58 = (f32[32,256]{1,0:T(8,128)S(1)}, f32[32,256]{1,0:T(8,128)S(1)}, u32[]{:S(2)}, u32[]{:S(2)}) collective-permute-start(f32[32,256]{1,0:T(8,128)S(1)} %collective-permute-done.56.refs_13_), channel_id=1, source_target_pairs={{0,1},{1,0},{2,3},{3,2},{4,5},{5,4},{6,7},{7,6},{8,9},{9,8},{10,11... | collective-permute-start | bytes 98312 | tf_op jit(solution)/shard_map/ppermute | solution.py:229
  221.2 17.5 %collective-permute-start.28 = (f32[32,256]{1,0:T(8,128)S(1)}, f32[32,256]{1,0:T(8,128)S(1)}, u32[]{:S(2)}, u32[]{:S(2)}) collective-permute-start(f32[32,256]{1,0:T(8,128)S(1)} %collective-permute-done.26.refs_20_), channel_id=1, source_target_pairs={{0,1},{1,0},{2,3},{3,2},{4,5},{5,4},{6,7},{7,6},{8,9},{9,8},{10,11... | collective-permute-start | bytes 98312 | tf_op jit(solution)/shard_map/ppermute | solution.py:229
  221.6 17.1 %collective-permute-start.20 = (f32[32,256]{1,0:T(8,128)S(1)}, f32[32,256]{1,0:T(8,128)S(1)}, u32[]{:S(2)}, u32[]{:S(2)}) collective-permute-start(f32[32,256]{1,0:T(8,128)S(1)} %collective-permute-done.18.refs_12_), channel_id=1, source_target_pairs={{0,1},{1,0},{2,3},{3,2},{4,5},{5,4},{6,7},{7,6},{8,9},{9,8},{10,11... | collective-permute-start | bytes 98312 | tf_op jit(solution)/shard_map/ppermute | solution.py:229
  221.7 17.0 %collective-permute-start.37 = (f32[32,256]{1,0:T(8,128)S(1)}, f32[32,256]{1,0:T(8,128)S(1)}, u32[]{:S(2)}, u32[]{:S(2)}) collective-permute-start(f32[32,256]{1,0:T(8,128)S(1)} %collective-permute-done.35.refs_29_), channel_id=1, source_target_pairs={{0,1},{1,0},{2,3},{3,2},{4,5},{5,4},{6,7},{7,6},{8,9},{9,8},{10,11... | collective-permute-start | bytes 98312 | tf_op jit(solution)/shard_map/ppermute | solution.py:229
  222.1 16.6 %collective-permute-start.29 = (f32[32,256]{1,0:T(8,128)S(1)}, f32[32,256]{1,0:T(8,128)S(1)}, u32[]{:S(2)}, u32[]{:S(2)}) collective-permute-start(f32[32,256]{1,0:T(8,128)S(1)} %collective-permute-done.27.refs_21_), channel_id=1, source_target_pairs={{0,1},{1,0},{2,3},{3,2},{4,5},{5,4},{6,7},{7,6},{8,9},{9,8},{10,11... | collective-permute-start | bytes 98312 | tf_op jit(solution)/shard_map/ppermute | solution.py:229
  222.2 16.5 %collective-permute-start.21 = (f32[32,256]{1,0:T(8,128)S(1)}, f32[32,256]{1,0:T(8,128)S(1)}, u32[]{:S(2)}, u32[]{:S(2)}) collective-permute-start(f32[32,256]{1,0:T(8,128)S(1)} %collective-permute-done.19.refs_13_), channel_id=1, source_target_pairs={{0,1},{1,0},{2,3},{3,2},{4,5},{5,4},{6,7},{7,6},{8,9},{9,8},{10,11... | collective-permute-start | bytes 98312 | tf_op jit(solution)/shard_map/ppermute | solution.py:229
  (105 other events, 400.7 us)

commit v2 on v1

v2 whole, which is shorter than its diff:
```python
import functools

import jax
import jax.numpy as jnp
import numpy as np
from jax import lax
from jax.experimental import pallas as pl
from jax.experimental.pallas import tpu as pltpu
from jax.sharding import PartitionSpec as P

F = 128
LAGS = 512
SMOOTH = 2
SEG = 32
CHUNKS = 1
CAP = 32

water_level = 0.2
epsilon = 1e-05

BF16 = jnp.bfloat16
F32 = jnp.float32


def forward_table(samples):
    bins = np.arange(F, dtype=np.int64) + 1
    times = np.arange(samples, dtype=np.int64)
    angle = 2.0 * np.pi * (bins[:, None] * times[None, :] % samples) / samples
    taper = 0.5 - 0.5 * np.cos(2.0 * np.pi * times / samples)
    return np.concatenate((np.cos(angle) * taper, -np.sin(angle) * taper)).astype(np.float32)


def inverse_table(samples):
    bins = np.arange(F, dtype=np.int64) + 1
    shifts = np.arange(LAGS, dtype=np.int64) - LAGS // 2
    angle = 2.0 * np.pi * (bins[:, None] * shifts[None, :] % samples) / samples
    scale = 1.0 / np.sqrt(float(SEG * F))
    return np.concatenate((np.cos(angle) * scale, -np.sin(angle) * scale)).astype(np.float32)


def split_const(table):
    high = table.astype(jnp.bfloat16)
    low = (table - high.astype(np.float32)).astype(jnp.bfloat16)
    return high, low


def split(x):
    high = x.astype(BF16)
    low = (x - high.astype(F32)).astype(BF16)
    return high, low


def dot_nt(a, b):
    return lax.dot_general(a, b, (((1,), (1,)), ((), ())), preferred_element_type=F32)


def dot_nn(a, b):
    return lax.dot_general(a, b, (((1,), (0,)), ((), ())), preferred_element_type=F32)


def whiten_tile(real, imag):
    magnitude = jnp.sqrt(real * real + imag * imag)
    row = lax.broadcasted_iota(jnp.int32, magnitude.shape, 0)
    smoothed = magnitude
    for offset in range(1, SMOOTH + 1):
        smoothed = smoothed + jnp.where(row >= offset, pltpu.roll(magnitude, offset, 0), 0.0)
        smoothed = smoothed + jnp.where(row < F - offset, pltpu.roll(magnitude, F - offset, 0), 0.0)
    water_mark = jnp.mean(magnitude, axis=0, keepdims=True)
    divisor = smoothed * (1.0 / (2 * SMOOTH + 1)) + water_level * water_mark + epsilon
    return real / divisor, imag / divisor


def as_column(row):
    n = row.shape[1]
    here = lax.broadcasted_iota(jnp.int32, (n, n), 0) == lax.broadcasted_iota(jnp.int32, (n, n), 1)
    return jnp.sum(jnp.where(here, row.astype(F32), 0.0), axis=1, keepdims=True).astype(jnp.int32)


def ranks(col, row, channels, axis):
    same = col // channels == row // channels
    first = lax.broadcasted_iota(jnp.int32, same.shape, axis) < lax.broadcasted_iota(jnp.int32, same.shape, 1 - axis)
    return jnp.sum(jnp.where(same & first, 1.0, 0.0), axis=axis, keepdims=True).astype(jnp.int32)


def spectra_kernel(place_ref, rec_ref, hi_ref, lo_ref, row_ref, first_ref, second_ref, held_ref, *, segs):
    step = pl.program_id(0)
    per, channels, samples = rec_ref.shape
    high, low = split(rec_ref[...].reshape(per * channels, samples))
    spectra = dot_nt(hi_ref[...], high) + (dot_nt(lo_ref[...], high) + dot_nt(hi_ref[...], low))
    for i in range(per):
        lanes = slice(i * channels, (i + 1) * channels)
        real, imag = whiten_tile(spectra[:F, lanes], spectra[F:, lanes])
        seg = step * per + i
        for ref, start in ((first_ref, 0), (second_ref, first_ref.shape[0] // (2 * segs))):
            count = ref.shape[0] // (2 * segs)
            ref[pl.ds(seg, count, stride=2 * segs), :] = real[start : start + count]
            ref[pl.ds(seg + segs, count, stride=2 * segs), :] = imag[start : start + count]

    @pl.when(step == pl.num_programs(0) - 1)
    def _():
        shards, cap, rows = held_ref.shape
        shard = place_ref[0]
        row = row_ref[...]
        col = as_column(row)
        nsrc = col.shape[0]
        rank = jnp.where(row // channels == shard, ranks(col, row, channels, 0), -1)
        chosen = (lax.broadcasted_iota(jnp.int32, (cap, nsrc), 0) == rank).astype(F32).astype(BF16)
        lane = lax.broadcasted_iota(jnp.int32, (nsrc, channels), 1)
        where = (col - shard * channels == lane).astype(F32).astype(BF16)
        hot = dot_nn(chosen, where).astype(BF16)
        hot = jnp.concatenate((hot, hot), axis=1)
        for d in range(shards):
            cut = first_ref.shape[0] // rows
            ref, at = (first_ref, d) if d < cut else (second_ref, d - cut)
            high, low = split(ref[at * rows : (at + 1) * rows, :])
            held_ref[d] = dot_nt(hot, jnp.concatenate((high, low), axis=1))


def whole(shape):
    return pl.BlockSpec(shape, lambda *_: (0,) * len(shape))


def first_blocks(shards):
    return 3 * shards // 8


def forward(recording, row, shard, shards):
    segs, channels, samples = recording.shape
    per = 4
    nsrc = row.shape[1]
    rows = F // shards * 2 * segs
    held = (shards, CAP, rows)
    cut = first_blocks(shards)
    white = [(cut * rows, channels), ((shards - cut) * rows, channels)]
    high, low = split_const(forward_table(samples))
    return pl.pallas_call(
        functools.partial(spectra_kernel, segs=segs),
        grid_spec=pltpu.PrefetchScalarGridSpec(
            num_scalar_prefetch=1,
            grid=(segs // per,),
            in_specs=[
                pl.BlockSpec((per, channels, samples), lambda s, p: (s, 0, 0)),
                whole((2 * F, samples)),
                whole((2 * F, samples)),
                whole((1, nsrc)),
            ],
            out_specs=[whole(x) for x in (*white, held)],
        ),
        out_shape=[jax.ShapeDtypeStruct(x, F32) for x in (*white, held)],
        compiler_params=pltpu.CompilerParams(vmem_limit_bytes=60 * 2**20, dimension_semantics=("arbitrary",)),
        cost_estimate=pl.CostEstimate(flops=6 * 10**9, bytes_accessed=16 * 2**20, transcendentals=0),
        name="forward_whiten",
    )(shard[None], recording, high, low, row)


def order_kernel(place_ref, got_ref, row_ref, *outs, channels):
    row = row_ref[...]
    col = as_column(row)
    nsrc = col.shape[0]
    entries = got_ref.shape[0]
    at = col // channels * CAP + ranks(col, row, channels, 1)
    hot = (at == lax.broadcasted_iota(jnp.int32, (nsrc, entries), 1)).astype(F32).astype(BF16)
    high, low = split(got_ref[...])
    rows = dot_nn(hot, high) + dot_nn(hot, low)
    size = outs[0].shape[0]
    per_half = nsrc // 2
    for h in range(2):

        @pl.when(place_ref[1] == h)
        def _():
            for k, out in enumerate(outs):
                start = ((k // CHUNKS) ^ h) * per_half + k % CHUNKS * size
                out[...] = rows[start : start + size]


def in_order(got, row, shard, half, channels):
    nsrc = row.shape[1]
    size = nsrc // 2 // CHUNKS
    shape = (size, got.shape[1])
    return pl.pallas_call(
        functools.partial(order_kernel, channels=channels),
        grid_spec=pltpu.PrefetchScalarGridSpec(
            num_scalar_prefetch=1,
            grid=(1,),
            in_specs=[whole(got.shape), whole((1, nsrc))],
            out_specs=[whole(shape)] * (2 * CHUNKS),
        ),
        out_shape=[jax.ShapeDtypeStruct(shape, F32)] * (2 * CHUNKS),
        compiler_params=pltpu.CompilerParams(vmem_limit_bytes=16 * 2**20),
        cost_estimate=pl.CostEstimate(flops=10**8, bytes_accessed=2**20, transcendentals=0),
        name="order_sources",
    )(jnp.stack((shard, half)), got, row)


def any_order(white, source_channels, half, shards):
    channels = white.shape[1]
    bins = white.reshape(shards, -1, channels)
    bins = lax.all_to_all(bins, "shard", split_axis=0, concat_axis=2, tiled=True)[0]
    rows = jnp.take(bins, source_channels, axis=1).T
    per_half = rows.shape[0] // 2
    mine = lax.dynamic_slice_in_dim(rows, half * per_half, per_half)
    others = lax.dynamic_slice_in_dim(rows, (1 - half) * per_half, per_half)
    return [*jnp.split(mine, CHUNKS), *jnp.split(others, CHUNKS)]


def pair_kernel(own_ref, oth_ref, out_ref, *, width):
    own, oth = own_ref[...], oth_ref[...]
    parts = []
    for i in range(own.shape[1] // width):
        lanes = slice(i * width, (i + 1) * width)
        parts += [own[:, lanes], oth[:, lanes]]
    out_ref[...] = jnp.concatenate(parts, axis=1)


def pair_halves(own, other, width):
    size, lanes = own.shape
    return pl.pallas_call(
        functools.partial(pair_kernel, width=width),
        out_shape=jax.ShapeDtypeStruct((size, 2 * lanes), F32),
        cost_estimate=pl.CostEstimate(flops=10**6, bytes_accessed=2**20, transcendentals=0),
        name="pair_halves",
    )(own, other)


def stack_kernel(place_ref, own0_ref, own1_ref, oth0_ref, oth1_ref, hi_ref, lo_ref, *refs, shards, pitch):
    blocks = refs[:shards]
    out_ref, real_ref, imag_ref, src_ref = refs[-4:]
    step = pl.program_id(0)
    per, channels, lags = out_ref.shape
    size, lanes = blocks[0].shape
    bins = F // shards
    width = lanes // bins // 2
    segs = width // 2
    cut = own0_ref.shape[0] // (bins * width)

    def turn(v):
        return jnp.concatenate((v[segs : 2 * segs], -v[:segs], v[3 * segs :], -v[2 * segs : 3 * segs]))

    def block(owner, own_ref, oth_ref, skip):
        zero = jnp.zeros((2 * width, channels), BF16)
        for two in range(0, bins, 2):
            shigh, slow = split(src_ref[place_ref[0] ^ owner, :, two * 2 * width : (two + 2) * 2 * width])
            for i in range(two, two + 2):
                rows = pl.ds(pl.multiple_of(((owner - skip) * bins + i) * width, width), width)
                high, low = split(jnp.concatenate((own_ref[rows, :], oth_ref[rows, :])))
                order = lambda h, l: jnp.concatenate((h, h, l, zero) if i == two else (h, h, zero, l))
                rhs = jnp.concatenate((order(high, low), order(turn(high), turn(low))), axis=1)
                at = slice((i - two) * 2 * width, (i - two + 1) * 2 * width)
                cross = dot_nn(jnp.concatenate((shigh[:, at], slow[:, at], shigh), axis=1), rhs)
                to = pl.ds(pl.multiple_of((owner * bins + i) * pitch, 8), size)
                real_ref[to, :] = cross[:, :channels]
                imag_ref[to, :] = cross[:, channels:]

    @pl.when(step == 0)
    def _():
        for r in range(shards):
            src_ref[r] = blocks[r][...]

        def first(owner, carry):
            block(owner, own0_ref, oth0_ref, 0)
            return carry

        def second(owner, carry):
            block(owner, own1_ref, oth1_ref, cut)
            return carry

        lax.fori_loop(0, cut, first, 0, unroll=2)
        lax.fori_loop(cut, shards, second, 0, unroll=2)

    table = jnp.concatenate((hi_ref[...], hi_ref[...], lo_ref[...]))
    rows = []
    for i in range(per):
        n = step * per + i
        both = [jnp.transpose(ref[pl.ds(n, F, stride=pitch), :]) for ref in (real_ref, imag_ref)]
        high, low = split(jnp.concatenate(both, axis=1))
        rows.append(jnp.concatenate((high, low, high), axis=1))
    out_ref[...] = dot_nn(jnp.concatenate(rows), table).reshape(per, channels, lags)


def correlate(j, previous, shard, own, other, blocks, samples, sources):
    size, lanes = blocks[0].shape
    shards = len(blocks)
    channels = own[0].shape[1]
    per = 16
    steps = size // per
    pitch = size + 8
    high, low = split_const(inverse_table(samples))
    operands = [*own, *other, high, low, *blocks]
    in_specs = [whole(x.shape) for x in operands]
    aliases = {}
    if previous is not None:
        aliases = {1 + len(operands): 0}
        operands.append(previous)
        in_specs.append(pl.BlockSpec(memory_space=pl.ANY))
    return pl.pallas_call(
        functools.partial(stack_kernel, shards=shards, pitch=pitch),
        grid_spec=pltpu.PrefetchScalarGridSpec(
            num_scalar_prefetch=1,
            grid=(steps,),
            in_specs=in_specs,
            out_specs=pl.BlockSpec((per, channels, LAGS), lambda s, p: (j * steps + s, 0, 0)),
            scratch_shapes=[
                pltpu.VMEM((F * pitch, channels), F32),
                pltpu.VMEM((F * pitch, channels), F32),
                pltpu.VMEM((shards, size, lanes), F32),
            ],
        ),
        out_shape=jax.ShapeDtypeStruct((sources, channels, LAGS), F32),
        input_output_aliases=aliases,
        compiler_params=pltpu.CompilerParams(vmem_limit_bytes=48 * 2**20, dimension_semantics=("arbitrary",)),
        cost_estimate=pl.CostEstimate(flops=20 * 10**9 // CHUNKS, bytes_accessed=48 * 2**20 // CHUNKS, transcendentals=0),
        name="stack_lags",
    )(shard[None], *operands)


def swap(x, axis, bits):
    return lax.ppermute(x, axis, [(i, i ^ bits) for i in range(lax.axis_size(axis))])


def body(recording, source_channels):
    segs, channels, samples = recording.shape
    shards = lax.axis_size("shard")
    shard, half = lax.axis_index("shard"), lax.axis_index("half")
    nsrc = source_channels.shape[0]
    row = source_channels[None, :]
    first, second, held = forward(recording, row, shard, shards)
    other_first = swap(first, "half", 1)

    got = lax.all_to_all(held, "shard", split_axis=0, concat_axis=0, tiled=True)
    mine = in_order(got.reshape(-1, got.shape[2]), row, shard, half, channels)
    counts = jnp.sum(source_channels[:, None] // channels == jnp.arange(shards)[None, :], axis=0)
    mine = lax.cond(
        jnp.max(counts) > CAP,
        lambda m: any_order(jnp.concatenate((first, second)), source_channels, half, shards),
        lambda m: list(m),
        list(mine),
    )
    other_first, *crossing = lax.optimization_barrier((other_first, *mine[CHUNKS:]))
    crossed = [swap(x, "half", 1) for x in crossing]
    second, *crossed = lax.optimization_barrier((second, *crossed))
    own, other = (first, second), (other_first, swap(second, "half", 1))

    result = None
    for j in range(CHUNKS):
        blocks = {0: pair_halves(mine[j], crossed[j], 2 * segs)}
        for k in range(1, shards // 4):
            blocks[4 * k] = swap(blocks[0], "shard", 4 * k)
        for bit in (2, 1):
            for r, x in list(blocks.items()):
                blocks[r ^ bit] = swap(x, "shard", bit)
        group = [blocks[r] for r in range(shards)]
        result = correlate(j, result, shard, own, other, group, samples, nsrc // 2)
    return result


def plain_forward_table(samples, freq_count):
    table = forward_table(samples)
    return jnp.stack((table[:freq_count], table[freq_count:]), axis=1)


def plain_inverse_table(samples, freq_count):
    table = inverse_table(samples)
    return jnp.stack((table[:freq_count], table[freq_count:]), axis=1)


def plain_whiten(spectra):
    magnitude = jnp.sqrt(spectra[:, 0] * spectra[:, 0] + spectra[:, 1] * spectra[:, 1])
    freq_count = magnitude.shape[0]
    padded = jnp.pad(magnitude, ((SMOOTH, SMOOTH), (0, 0), (0, 0)))
    smoothed = padded[0:freq_count]
    for offset in range(1, 2 * SMOOTH + 1):
        smoothed = smoothed + padded[offset : offset + freq_count]
    smoothed = smoothed / (2 * SMOOTH + 1)
    water_mark = jnp.mean(magnitude, axis=0, keepdims=True)
    divisor = smoothed + water_level * water_mark + epsilon
    return spectra / divisor[:, None]


def plain_correlate(whitened, indices):
    sources = jnp.take(whitened, indices, axis=2)
    src_real, src_imag = (sources[:, 0], sources[:, 1])
    rec_real, rec_imag = (whitened[:, 0], whitened[:, 1])
    high = lax.Precision.HIGHEST
    cross_real = jnp.einsum("fnx,fcx->fnc", src_real, rec_real, precision=high) + jnp.einsum(
        "fnx,fcx->fnc", src_imag, rec_imag, precision=high
    )
    cross_imag = jnp.einsum("fnx,fcx->fnc", src_real, rec_imag, precision=high) - jnp.einsum(
        "fnx,fcx->fnc", src_imag, rec_real, precision=high
    )
    return jnp.stack((cross_real, cross_imag), axis=1)


def plain_body(recording, source_channels):
    samples = recording.shape[2]
    high = lax.Precision.HIGHEST
    spectra = jnp.einsum("fqt,sct->fqcs", plain_forward_table(samples, F), recording, precision=high)
    whitened = plain_whiten(spectra)
    by_freq = lax.all_to_all(whitened, "shard", split_axis=0, concat_axis=2, tiled=True)
    per_half = source_channels.shape[0] // lax.axis_size("half")
    own_sources = lax.dynamic_slice_in_dim(source_channels, lax.axis_index("half") * per_half, per_half)
    combined = jnp.concatenate((by_freq, swap(by_freq, "half", 1)), axis=3)
    cross = plain_correlate(combined, own_sources)
    cross = lax.all_to_all(cross, "shard", split_axis=3, concat_axis=0, tiled=True)
    return jnp.einsum("fqnc,fql->ncl", cross, plain_inverse_table(samples, F), precision=high)


def solution(mesh):
    def run(recording, source_channels):
        shards = lax.axis_size("shard")
        fits = recording.shape[1] % 128 == 0 and shards == 16
        return (body if fits else plain_body)(recording, source_channels)

    return jax.shard_map(
        run,
        mesh=mesh,
        in_specs=(P("half", "shard", None), P()),
        out_specs=P("half", "shard", None),
        check_vma=False,
    )
```

time: 255 us -> 118 us (0.46)
  starting transfers between devices: 113 us -> 22.8 us
  Pallas kernels: 75.4 us -> 37.7 us
  waiting for transfers between devices: 60.7 us -> 53.2 us
  local copies, waits for them, and re-layouts: 4.87 us -> 2.04 us
    ppermute x149 -> x18, starting transfers between devices: 113 us -> 15.4 us  [swap(): lax.ppermute(x, axis, [(i, i ^ bits) for i in range(lax.axis_size(axis))])]
    pallas_call x5 -> x4, Pallas kernels: 75.4 us -> 37.7 us  [the longest x1 23.6 us: correlate(): pl.pallas_call(functools.partial(stack_kernel, shards=shards, pitch=pitch...]
    ppermute x149 -> x18, waiting for transfers between devices: 60.7 us -> 42 us  [swap(): lax.ppermute(x, axis, [(i, i ^ bits) for i in range(lax.axis_size(axis))])]
    all_to_all x0 -> x1, waiting for transfers between devices: none -> 11.3 us  [body(): got = lax.all_to_all(held, 'shard', split_axis=0, concat_axis=0, tiled=True)]
    all_to_all x0 -> x1, starting transfers between devices: none -> 7.36 us  [body(): got = lax.all_to_all(held, 'shard', split_axis=0, concat_axis=0, tiled=True)]
  transfers between devices with their start and end apart: 149 -> 19, of which waited for: 49 -> 10; matrix products, arithmetic and copies ran while one was open for 0% -> 1% of each run, Pallas kernels for 19% -> 3%
where the time goes in v2:
time: 118 us; the launch traced here: 117 us
  waiting for transfers between devices  53.2 us (45%)
  Pallas kernels  37.7 us (32%)
  starting transfers between devices  22.8 us (19%)
  local copies, waits for them, and re-layouts  2.04 us (2%)
    ppermute x18, waiting for transfers between devices, swap(): lax.ppermute(x, axis, [(i, i ^ bits) for i in range(lax.axis_size(axis))])  42 us
    pallas_call x1, Pallas kernels, correlate(): pl.pallas_call(functools.partial(stack_kernel, shards=shards, pitch=pitch...  23.6 us
    ppermute x18, starting transfers between devices, swap(): lax.ppermute(x, axis, [(i, i ^ bits) for i in range(lax.axis_size(axis))])  15.4 us
    all_to_all x1, waiting for transfers between devices, body(): got = lax.all_to_all(held, 'shard', split_axis=0, concat_axis=0, tiled=True)  11.3 us
    pallas_call x1, Pallas kernels, forward(): pl.pallas_call(functools.partial(spectra_kernel, segs=segs), grid_spec=pl...  11.2 us
    all_to_all x1, starting transfers between devices, body(): got = lax.all_to_all(held, 'shard', split_axis=0, concat_axis=0, tiled=True)  7.36 us
  transfers between devices with their start and end apart: 19, of which 10 were waited for; matrix products, arithmetic and copies ran while one was open for 1% of the time, Pallas kernels for 3%

profile of v2, /device:TPU:0, one launch (start us, length us, event | category | flops | bytes accessed | tf_op | source)
XLA Modules:
  0.0 117.4 jit_solution(865769480380827606)
XLA Ops:
  0.0 11.2 %forward_whiten.1 = (f32[1536,128]{1,0:T(8,128)}, f32[2560,128]{1,0:T(8,128)}, f32[16,32,256]{2,1,0:T(8,128)}) custom-call(s32[1]{0:T(128)} %bitcast.6.place_ref, f32[16,128,1024]{2,1,0:T(8,128)} %rec_ref.1, bf16[256,1024]{1,0:T(8,128)(2,1)} %constant.61.clone.hi_ref, bf16[256,1024]{1,0:T(8,128)(2,1)} %constant.62.clone.lo_ref, s32[1,256]{1,0:T(1,128)} %bitcast.13), custom_call_target="tpu_custom_call" | custom-call | flops 6000000000 | bytes 16777216 | tf_op jit(solution)/shard_map/forward_whiten/pallas_call | solution.py:136
  11.2 7.4 %all-to-all-start.1 = ((f32[16,32,256]{2,1,0:T(8,128)}), f32[16,32,256]{2,1,0:T(8,128)S(1)}, u32[]{:S(2)}, u32[]{:S(2)}) async-start(f32[16,32,256]{2,1,0:T(8,128)} %get-tuple-element.32), calls=%async_computation.1 | async-start | bytes 1048576 | tf_op jit(solution)/shard_map/all_to_all | solution.py:329
  18.5 1.6 %collective-permute-start = (f32[1536,128]{1,0:T(8,128)}, f32[1536,128]{1,0:T(8,128)S(1)}, u32[]{:S(2)}, u32[]{:S(2)}) collective-permute-start(f32[1536,128]{1,0:T(8,128)} %get-tuple-element.30.own0_ref), channel_id=1, source_target_pairs={{0,16},{16,0},{1,17},{17,1},{2,18},{18,2},{3,19},{19,3},{4,20},{20... | collective-permute-start | bytes 2359304 | tf_op jit(solution)/shard_map/ppermute | solution.py:317
  20.1 0.1 convert_reduce_fusion
  20.3 0.7 reduce_max.9
  21.7 0.1 pad_add_fusion.place_ref
  21.8 11.3 %all-to-all-done.1 = f32[16,32,256]{2,1,0:T(8,128)S(1)} async-done(((f32[16,32,256]{2,1,0:T(8,128)}), f32[16,32,256]{2,1,0:T(8,128)S(1)}, u32[]{:S(2)}, u32[]{:S(2)}) %all-to-all-start.1) | async-done | bytes 524320 | tf_op jit(solution)/shard_map/all_to_all | solution.py:329
  33.0 1.1 order_sources.1
  34.1 0.0 copy-start.1
  34.1 0.0 copy-start.2
  34.1 0.0 copy-start.6
  34.1 4.5 %collective-permute-done.oth0_ref = f32[1536,128]{1,0:T(8,128)S(1)} collective-permute-done((f32[1536,128]{1,0:T(8,128)}, f32[1536,128]{1,0:T(8,128)S(1)}, u32[]{:S(2)}, u32[]{:S(2)}) %collective-permute-start) | collective-permute-done | bytes 786464 | tf_op jit(solution)/shard_map/ppermute | solution.py:317
  38.6 1.5 %collective-permute-start.1 = (f32[128,256]{1,0:T(8,128)}, f32[128,256]{1,0:T(8,128)S(1)}, u32[]{:S(2)}, u32[]{:S(2)}) collective-permute-start(f32[128,256]{1,0:T(8,128)} %copy-done.6), channel_id=1, source_target_pairs={{0,16},{16,0},{1,17},{17,1},{2,18},{18,2},{3,19},{19,3},{4,20},{20... | collective-permute-start | bytes 393224 | tf_op jit(solution)/shard_map/ppermute | solution.py:317
  40.1 3.7 %collective-permute-done.1.oth_ref = f32[128,256]{1,0:T(8,128)S(1)} collective-permute-done((f32[128,256]{1,0:T(8,128)}, f32[128,256]{1,0:T(8,128)S(1)}, u32[]{:S(2)}, u32[]{:S(2)}) %collective-permute-start.1) | collective-permute-done | bytes 131104 | tf_op jit(solution)/shard_map/ppermute | solution.py:317
  43.8 1.5 %collective-permute-start.2 = (f32[2560,128]{1,0:T(8,128)}, f32[2560,128]{1,0:T(8,128)S(1)}, u32[]{:S(2)}, u32[]{:S(2)}) collective-permute-start(f32[2560,128]{1,0:T(8,128)} %get-tuple-element.35.own1_ref), channel_id=1, source_target_pairs={{0,16},{16,0},{1,17},{17,1},{2,18},{18,2},{3,19},{19,3},{4,20},{20... | collective-permute-start | bytes 3932168 | tf_op jit(solution)/shard_map/ppermute | solution.py:317
  45.3 1.9 %pair_halves.1.refs_0_ = f32[128,512]{1,0:T(8,128)} custom-call(f32[128,256]{1,0:T(8,128)S(1)} %get-tuple-element.37.own_ref, f32[128,256]{1,0:T(8,128)} %copy-done.3), custom_call_target="tpu_custom_call" | custom-call | flops 1000000 | bytes 1048576 | tf_op jit(solution)/shard_map/pair_halves/pallas_call | solution.py:217
  47.2 3.5 %collective-permute-start.14 = (f32[128,512]{1,0:T(8,128)}, f32[128,512]{1,0:T(8,128)S(1)}, u32[]{:S(2)}, u32[]{:S(2)}) collective-permute-start(f32[128,512]{1,0:T(8,128)} %pair_halves.1.refs_0_), channel_id=1, source_target_pairs={{0,12},{1,13},{2,14},{3,15},{4,8},{5,9},{6,10},{7,11},{8,4},{9,5},... | collective-permute-start | bytes 786440 | tf_op jit(solution)/shard_map/ppermute | solution.py:317
  50.7 0.0 collective-permute-start.10
  50.7 0.9 collective-permute-start.6
  51.6 1.7 %collective-permute-start.4 = (f32[128,512]{1,0:T(8,128)}, f32[128,512]{1,0:T(8,128)S(1)}, u32[]{:S(2)}, u32[]{:S(2)}) collective-permute-start(f32[128,512]{1,0:T(8,128)} %pair_halves.1.refs_0_), channel_id=1, source_target_pairs={{0,2},{1,3},{2,0},{3,1},{4,6},{5,7},{6,4},{7,5},{8,10},{9,11},{10,... | collective-permute-start | bytes 786440 | tf_op jit(solution)/shard_map/ppermute | solution.py:317
  53.2 5.2 %collective-permute-done.14.refs_12_ = f32[128,512]{1,0:T(8,128)S(1)} collective-permute-done((f32[128,512]{1,0:T(8,128)}, f32[128,512]{1,0:T(8,128)S(1)}, u32[]{:S(2)}, u32[]{:S(2)}) %collective-permute-start.14) | collective-permute-done | bytes 262176 | tf_op jit(solution)/shard_map/ppermute | solution.py:317
  58.5 13.0 %collective-permute-done.10.refs_8_ = f32[128,512]{1,0:T(8,128)S(1)} collective-permute-done((f32[128,512]{1,0:T(8,128)}, f32[128,512]{1,0:T(8,128)S(1)}, u32[]{:S(2)}, u32[]{:S(2)}) %collective-permute-start.10) | collective-permute-done | bytes 262176 | tf_op jit(solution)/shard_map/ppermute | solution.py:317
  71.5 1.5 %collective-permute-start.16 = (f32[128,512]{1,0:T(8,128)S(1)}, f32[128,512]{1,0:T(8,128)S(1)}, u32[]{:S(2)}, u32[]{:S(2)}) collective-permute-start(f32[128,512]{1,0:T(8,128)S(1)} %collective-permute-done.14.refs_12_), channel_id=1, source_target_pairs={{0,2},{1,3},{2,0},{3,1},{4,6},{5,7},{6,4},{7,5},{8,10},{9,11},{10,... | collective-permute-start | bytes 786440 | tf_op jit(solution)/shard_map/ppermute | solution.py:317
  72.9 0.0 collective-permute-done.6.refs_4_
  72.9 0.0 collective-permute-start.15
  72.9 0.0 collective-permute-done.4.refs_2_
  72.9 0.6 collective-permute-start.12
  73.6 0.0 collective-permute-done.3.refs_1_
  73.6 0.2 collective-permute-start.11
  73.7 7.0 %collective-permute-done.16.refs_14_ = f32[128,512]{1,0:T(8,128)S(1)} collective-permute-done((f32[128,512]{1,0:T(8,128)S(1)}, f32[128,512]{1,0:T(8,128)S(1)}, u32[]{:S(2)}, u32[]{:S(2)}) %collective-permute-start.16) | collective-permute-done | bytes 262176 | tf_op jit(solution)/shard_map/ppermute | solution.py:317
  80.7 1.5 %collective-permute-start.8 = (f32[128,512]{1,0:T(8,128)S(1)}, f32[128,512]{1,0:T(8,128)S(1)}, u32[]{:S(2)}, u32[]{:S(2)}) collective-permute-start(f32[128,512]{1,0:T(8,128)S(1)} %collective-permute-done.6.refs_4_), channel_id=1, source_target_pairs={{0,2},{1,3},{2,0},{3,1},{4,6},{5,7},{6,4},{7,5},{8,10},{9,11},{10,... | collective-permute-start | bytes 786440 | tf_op jit(solution)/shard_map/ppermute | solution.py:317
  82.2 0.0 collective-permute-done.15.refs_13_
  82.2 0.0 collective-permute-start.7
  82.2 4.1 %collective-permute-done.12.refs_10_ = f32[128,512]{1,0:T(8,128)S(1)} collective-permute-done((f32[128,512]{1,0:T(8,128)S(1)}, f32[128,512]{1,0:T(8,128)S(1)}, u32[]{:S(2)}, u32[]{:S(2)}) %collective-permute-start.12) | collective-permute-done | bytes 262176 | tf_op jit(solution)/shard_map/ppermute | solution.py:317
  86.3 0.0 collective-permute-start.5
  86.3 0.0 collective-permute-done.11.refs_9_
  86.3 0.5 collective-permute-start.17
  86.8 3.1 %collective-permute-done.8.refs_6_ = f32[128,512]{1,0:T(8,128)S(1)} collective-permute-done((f32[128,512]{1,0:T(8,128)S(1)}, f32[128,512]{1,0:T(8,128)S(1)}, u32[]{:S(2)}, u32[]{:S(2)}) %collective-permute-start.8) | collective-permute-done | bytes 262176 | tf_op jit(solution)/shard_map/ppermute | solution.py:317
  89.9 0.0 collective-permute-start.13
  89.9 0.0 collective-permute-done.7.refs_5_
  89.9 0.5 collective-permute-start.9
  90.5 0.0 collective-permute-done.5.refs_3_
  90.5 0.0 collective-permute-done.17.refs_15_
  90.5 1.0 collective-permute-done.13.refs_11_
  91.5 0.4 collective-permute-done.9.refs_7_
  91.9 1.1 copy-done.5
  92.9 0.9 copy-done
  93.9 23.6 %stack_lags.1 = f32[128,128,512]{2,1,0:T(8,128)} custom-call(s32[1]{0:T(128)} %bitcast.6.place_ref, f32[1536,128]{1,0:T(8,128)} %get-tuple-element.30.own0_ref, f32[2560,128]{1,0:T(8,128)} %get-tuple-element.35.own1_ref, f32[1536,128]{1,0:T(8,128)S(1)} %collective-permute-done.oth0_ref, f32[2560,128]{1,0:T(8,128)} %copy-done.5, ...), custom_call_target="tpu_custom_call" | custom-call | flops 20000000000 | bytes 50331648 | tf_op jit(solution)/shard_map/stack_lags/pallas_call | solution.py:295
  (13 shorter events, 0.0 us)
Async XLA Ops:
  0.0 20.1 %copy-start.4 = (s32[256]{0:T(256)S(1)}, s32[256]{0:T(256)}, u32[]{:S(2)}) copy-start(s32[256]{0:T(256)} %param.9) | copy-start | bytes 3076
  11.2 21.8 %all-to-all-start.1 = ((f32[16,32,256]{2,1,0:T(8,128)}), f32[16,32,256]{2,1,0:T(8,128)S(1)}, u32[]{:S(2)}, u32[]{:S(2)}) async-start(f32[16,32,256]{2,1,0:T(8,128)} %get-tuple-element.32), calls=%async_computation.1 | async-start | bytes 1048576 | tf_op jit(solution)/shard_map/all_to_all | solution.py:329
  18.5 20.1 %collective-permute-start = (f32[1536,128]{1,0:T(8,128)}, f32[1536,128]{1,0:T(8,128)S(1)}, u32[]{:S(2)}, u32[]{:S(2)}) collective-permute-start(f32[1536,128]{1,0:T(8,128)} %get-tuple-element.30.own0_ref), channel_id=1, source_target_pairs={{0,16},{16,0},{1,17},{17,1},{2,18},{18,2},{3,19},{19,3},{4,20},{20... | collective-permute-start | bytes 2359304 | tf_op jit(solution)/shard_map/ppermute | solution.py:317
  34.1 58.8 %copy-start.1 = (bf16[256,512]{1,0:T(8,128)(2,1)S(1)}, bf16[256,512]{1,0:T(8,128)(2,1)}, u32[]{:S(2)}) copy-start(bf16[256,512]{1,0:T(8,128)(2,1)} %constant.64.clone.lo_ref) | copy-start | bytes 786436
  34.1 58.8 %copy-start.2 = (bf16[256,512]{1,0:T(8,128)(2,1)S(1)}, bf16[256,512]{1,0:T(8,128)(2,1)}, u32[]{:S(2)}) copy-start(bf16[256,512]{1,0:T(8,128)(2,1)} %constant.63.clone.hi_ref) | copy-start | bytes 786436
  34.1 4.5 %copy-start.6 = (f32[128,256]{1,0:T(8,128)}, f32[128,256]{1,0:T(8,128)S(1)}, u32[]{:S(2)}) copy-start(f32[128,256]{1,0:T(8,128)S(1)} %get-tuple-element.34) | copy-start | bytes 393220
  38.6 5.2 %collective-permute-start.1 = (f32[128,256]{1,0:T(8,128)}, f32[128,256]{1,0:T(8,128)S(1)}, u32[]{:S(2)}, u32[]{:S(2)}) collective-permute-start(f32[128,256]{1,0:T(8,128)} %copy-done.6), channel_id=1, source_target_pairs={{0,16},{16,0},{1,17},{17,1},{2,18},{18,2},{3,19},{19,3},{4,20},{20... | collective-permute-start | bytes 393224 | tf_op jit(solution)/shard_map/ppermute | solution.py:317
  43.8 1.5 %copy-start.3 = (f32[128,256]{1,0:T(8,128)}, f32[128,256]{1,0:T(8,128)S(1)}, u32[]{:S(2)}) copy-start(f32[128,256]{1,0:T(8,128)S(1)} %collective-permute-done.1.oth_ref) | copy-start | bytes 393220
  43.8 48.1 %collective-permute-start.2 = (f32[2560,128]{1,0:T(8,128)}, f32[2560,128]{1,0:T(8,128)S(1)}, u32[]{:S(2)}, u32[]{:S(2)}) collective-permute-start(f32[2560,128]{1,0:T(8,128)} %get-tuple-element.35.own1_ref), channel_id=1, source_target_pairs={{0,16},{16,0},{1,17},{17,1},{2,18},{18,2},{3,19},{19,3},{4,20},{20... | collective-permute-start | bytes 3932168 | tf_op jit(solution)/shard_map/ppermute | solution.py:317
  47.2 11.3 %collective-permute-start.14 = (f32[128,512]{1,0:T(8,128)}, f32[128,512]{1,0:T(8,128)S(1)}, u32[]{:S(2)}, u32[]{:S(2)}) collective-permute-start(f32[128,512]{1,0:T(8,128)} %pair_halves.1.refs_0_), channel_id=1, source_target_pairs={{0,12},{1,13},{2,14},{3,15},{4,8},{5,9},{6,10},{7,11},{8,4},{9,5},... | collective-permute-start | bytes 786440 | tf_op jit(solution)/shard_map/ppermute | solution.py:317
  50.7 20.8 %collective-permute-start.10 = (f32[128,512]{1,0:T(8,128)}, f32[128,512]{1,0:T(8,128)S(1)}, u32[]{:S(2)}, u32[]{:S(2)}) collective-permute-start(f32[128,512]{1,0:T(8,128)} %pair_halves.1.refs_0_), channel_id=1, source_target_pairs={{0,8},{1,9},{2,10},{3,11},{4,12},{5,13},{6,14},{7,15},{8,0},{9,1},... | collective-permute-start | bytes 786440 | tf_op jit(solution)/shard_map/ppermute | solution.py:317
  50.7 22.3 %collective-permute-start.6 = (f32[128,512]{1,0:T(8,128)}, f32[128,512]{1,0:T(8,128)S(1)}, u32[]{:S(2)}, u32[]{:S(2)}) collective-permute-start(f32[128,512]{1,0:T(8,128)} %pair_halves.1.refs_0_), channel_id=1, source_target_pairs={{0,4},{1,5},{2,6},{3,7},{4,0},{5,1},{6,2},{7,3},{8,12},{9,13},{10,... | collective-permute-start | bytes 786440 | tf_op jit(solution)/shard_map/ppermute | solution.py:317
  51.6 21.4 %collective-permute-start.4 = (f32[128,512]{1,0:T(8,128)}, f32[128,512]{1,0:T(8,128)S(1)}, u32[]{:S(2)}, u32[]{:S(2)}) collective-permute-start(f32[128,512]{1,0:T(8,128)} %pair_halves.1.refs_0_), channel_id=1, source_target_pairs={{0,2},{1,3},{2,0},{3,1},{4,6},{5,7},{6,4},{7,5},{8,10},{9,11},{10,... | collective-permute-start | bytes 786440 | tf_op jit(solution)/shard_map/ppermute | solution.py:317
  58.5 15.1 %collective-permute-start.3 = (f32[128,512]{1,0:T(8,128)}, f32[128,512]{1,0:T(8,128)S(1)}, u32[]{:S(2)}, u32[]{:S(2)}) collective-permute-start(f32[128,512]{1,0:T(8,128)} %pair_halves.1.refs_0_), channel_id=1, source_target_pairs={{0,1},{1,0},{2,3},{3,2},{4,5},{5,4},{6,7},{7,6},{8,9},{9,8},{10,11... | collective-permute-start | bytes 786440 | tf_op jit(solution)/shard_map/ppermute | solution.py:317
  71.5 9.2 %collective-permute-start.16 = (f32[128,512]{1,0:T(8,128)S(1)}, f32[128,512]{1,0:T(8,128)S(1)}, u32[]{:S(2)}, u32[]{:S(2)}) collective-permute-start(f32[128,512]{1,0:T(8,128)S(1)} %collective-permute-done.14.refs_12_), channel_id=1, source_target_pairs={{0,2},{1,3},{2,0},{3,1},{4,6},{5,7},{6,4},{7,5},{8,10},{9,11},{10,... | collective-permute-start | bytes 786440 | tf_op jit(solution)/shard_map/ppermute | solution.py:317
  72.9 9.2 %collective-permute-start.15 = (f32[128,512]{1,0:T(8,128)S(1)}, f32[128,512]{1,0:T(8,128)S(1)}, u32[]{:S(2)}, u32[]{:S(2)}) collective-permute-start(f32[128,512]{1,0:T(8,128)S(1)} %collective-permute-done.14.refs_12_), channel_id=1, source_target_pairs={{0,1},{1,0},{2,3},{3,2},{4,5},{5,4},{6,7},{7,6},{8,9},{9,8},{10,11... | collective-permute-start | bytes 786440 | tf_op jit(solution)/shard_map/ppermute | solution.py:317
  72.9 13.4 %collective-permute-start.12 = (f32[128,512]{1,0:T(8,128)S(1)}, f32[128,512]{1,0:T(8,128)S(1)}, u32[]{:S(2)}, u32[]{:S(2)}) collective-permute-start(f32[128,512]{1,0:T(8,128)S(1)} %collective-permute-done.10.refs_8_), channel_id=1, source_target_pairs={{0,2},{1,3},{2,0},{3,1},{4,6},{5,7},{6,4},{7,5},{8,10},{9,11},{10,... | collective-permute-start | bytes 786440 | tf_op jit(solution)/shard_map/ppermute | solution.py:317
  73.6 12.8 %collective-permute-start.11 = (f32[128,512]{1,0:T(8,128)S(1)}, f32[128,512]{1,0:T(8,128)S(1)}, u32[]{:S(2)}, u32[]{:S(2)}) collective-permute-start(f32[128,512]{1,0:T(8,128)S(1)} %collective-permute-done.10.refs_8_), channel_id=1, source_target_pairs={{0,1},{1,0},{2,3},{3,2},{4,5},{5,4},{6,7},{7,6},{8,9},{9,8},{10,11... | collective-permute-start | bytes 786440 | tf_op jit(solution)/shard_map/ppermute | solution.py:317
  80.7 9.2 %collective-permute-start.8 = (f32[128,512]{1,0:T(8,128)S(1)}, f32[128,512]{1,0:T(8,128)S(1)}, u32[]{:S(2)}, u32[]{:S(2)}) collective-permute-start(f32[128,512]{1,0:T(8,128)S(1)} %collective-permute-done.6.refs_4_), channel_id=1, source_target_pairs={{0,2},{1,3},{2,0},{3,1},{4,6},{5,7},{6,4},{7,5},{8,10},{9,11},{10,... | collective-permute-start | bytes 786440 | tf_op jit(solution)/shard_map/ppermute | solution.py:317
  82.2 7.8 %collective-permute-start.7 = (f32[128,512]{1,0:T(8,128)S(1)}, f32[128,512]{1,0:T(8,128)S(1)}, u32[]{:S(2)}, u32[]{:S(2)}) collective-permute-start(f32[128,512]{1,0:T(8,128)S(1)} %collective-permute-done.6.refs_4_), channel_id=1, source_target_pairs={{0,1},{1,0},{2,3},{3,2},{4,5},{5,4},{6,7},{7,6},{8,9},{9,8},{10,11... | collective-permute-start | bytes 786440 | tf_op jit(solution)/shard_map/ppermute | solution.py:317
  86.3 4.1 %collective-permute-start.5 = (f32[128,512]{1,0:T(8,128)S(1)}, f32[128,512]{1,0:T(8,128)S(1)}, u32[]{:S(2)}, u32[]{:S(2)}) collective-permute-start(f32[128,512]{1,0:T(8,128)S(1)} %collective-permute-done.4.refs_2_), channel_id=1, source_target_pairs={{0,1},{1,0},{2,3},{3,2},{4,5},{5,4},{6,7},{7,6},{8,9},{9,8},{10,11... | collective-permute-start | bytes 786440 | tf_op jit(solution)/shard_map/ppermute | solution.py:317
  86.3 4.1 %collective-permute-start.17 = (f32[128,512]{1,0:T(8,128)S(1)}, f32[128,512]{1,0:T(8,128)S(1)}, u32[]{:S(2)}, u32[]{:S(2)}) collective-permute-start(f32[128,512]{1,0:T(8,128)S(1)} %collective-permute-done.16.refs_14_), channel_id=1, source_target_pairs={{0,1},{1,0},{2,3},{3,2},{4,5},{5,4},{6,7},{7,6},{8,9},{9,8},{10,11... | collective-permute-start | bytes 786440 | tf_op jit(solution)/shard_map/ppermute | solution.py:317
  89.9 1.5 %collective-permute-start.13 = (f32[128,512]{1,0:T(8,128)S(1)}, f32[128,512]{1,0:T(8,128)S(1)}, u32[]{:S(2)}, u32[]{:S(2)}) collective-permute-start(f32[128,512]{1,0:T(8,128)S(1)} %collective-permute-done.12.refs_10_), channel_id=1, source_target_pairs={{0,1},{1,0},{2,3},{3,2},{4,5},{5,4},{6,7},{7,6},{8,9},{9,8},{10,11... | collective-permute-start | bytes 786440 | tf_op jit(solution)/shard_map/ppermute | solution.py:317
  89.9 1.9 %collective-permute-start.9 = (f32[128,512]{1,0:T(8,128)S(1)}, f32[128,512]{1,0:T(8,128)S(1)}, u32[]{:S(2)}, u32[]{:S(2)}) collective-permute-start(f32[128,512]{1,0:T(8,128)S(1)} %collective-permute-done.8.refs_6_), channel_id=1, source_target_pairs={{0,1},{1,0},{2,3},{3,2},{4,5},{5,4},{6,7},{7,6},{8,9},{9,8},{10,11... | collective-permute-start | bytes 786440 | tf_op jit(solution)/shard_map/ppermute | solution.py:317
  91.9 1.1 copy-start.5
  92.9 1.0 copy-start

commit v3 on v2

--- a/solution.py
+++ b/solution.py
@@ -121,7 +121,7 @@
 
 
 def first_blocks(shards):
-    return 3 * shards // 8
+    return 5 * shards // 16
 
 
 def forward(recording, row, shard, shards):
@@ -203,58 +203,42 @@
     return [*jnp.split(mine, CHUNKS), *jnp.split(others, CHUNKS)]
 
 
-def pair_kernel(own_ref, oth_ref, out_ref, *, width):
-    own, oth = own_ref[...], oth_ref[...]
-    parts = []
-    for i in range(own.shape[1] // width):
-        lanes = slice(i * width, (i + 1) * width)
-        parts += [own[:, lanes], oth[:, lanes]]
-    out_ref[...] = jnp.concatenate(parts, axis=1)
-
-
-def pair_halves(own, other, width):
-    size, lanes = own.shape
-    return pl.pallas_call(
-        functools.partial(pair_kernel, width=width),
-        out_shape=jax.ShapeDtypeStruct((size, 2 * lanes), F32),
-        cost_estimate=pl.CostEstimate(flops=10**6, bytes_accessed=2**20, transcendentals=0),
-        name="pair_halves",
-    )(own, other)
-
-
-def stack_kernel(place_ref, own0_ref, own1_ref, oth0_ref, oth1_ref, hi_ref, lo_ref, *refs, shards, pitch):
-    blocks = refs[:shards]
+def stack_kernel(place_ref, own0_ref, own1_ref, oth0_ref, oth1_ref, hi_ref, lo_ref, *refs, stacked, pitch):
+    stacks = refs[: len(stacked)]
     out_ref, real_ref, imag_ref, src_ref = refs[-4:]
     step = pl.program_id(0)
     per, channels, lags = out_ref.shape
-    size, lanes = blocks[0].shape
+    _, shards, size, lanes = src_ref.shape
     bins = F // shards
-    width = lanes // bins // 2
+    width = lanes // bins
     segs = width // 2
     cut = own0_ref.shape[0] // (bins * width)
 
     def turn(v):
-        return jnp.concatenate((v[segs : 2 * segs], -v[:segs], v[3 * segs :], -v[2 * segs : 3 * segs]))
+        return jnp.concatenate((v[segs:], -v[:segs]))
 
     def block(owner, own_ref, oth_ref, skip):
-        zero = jnp.zeros((2 * width, channels), BF16)
-        for two in range(0, bins, 2):
-            shigh, slow = split(src_ref[place_ref[0] ^ owner, :, two * 2 * width : (two + 2) * 2 * width])
-            for i in range(two, two + 2):
+        for group in range(0, bins, 4):
+            lanes = slice(group * width, (group + 4) * width)
+            source = [split(src_ref[h, place_ref[0] ^ owner, :, lanes]) for h in range(2)]
+            for i in range(group, group + 4):
                 rows = pl.ds(pl.multiple_of(((owner - skip) * bins + i) * width, width), width)
-                high, low = split(jnp.concatenate((own_ref[rows, :], oth_ref[rows, :])))
-                order = lambda h, l: jnp.concatenate((h, h, l, zero) if i == two else (h, h, zero, l))
-                rhs = jnp.concatenate((order(high, low), order(turn(high), turn(low))), axis=1)
-                at = slice((i - two) * 2 * width, (i - two + 1) * 2 * width)
-                cross = dot_nn(jnp.concatenate((shigh[:, at], slow[:, at], shigh), axis=1), rhs)
+                (ah, al), (bh, bl) = split(own_ref[rows, :]), split(oth_ref[rows, :])
+                right = (ah, bh, ah, bh, al, bl)
+                rhs = jnp.concatenate((jnp.concatenate(right), jnp.concatenate([turn(v) for v in right])), axis=1)
+                at = slice((i - group) * width, (i - group + 1) * width)
+                (ah, al), (bh, bl) = source
+                lhs = jnp.concatenate([v[:, at] for v in (ah, bh, al, bl, ah, bh)], axis=1)
+                cross = dot_nn(lhs, rhs)
                 to = pl.ds(pl.multiple_of((owner * bins + i) * pitch, 8), size)
                 real_ref[to, :] = cross[:, :channels]
                 imag_ref[to, :] = cross[:, channels:]
 
     @pl.when(step == 0)
     def _():
-        for r in range(shards):
-            src_ref[r] = blocks[r][...]
+        for held, ref in zip(stacked, stacks):
+            for k, (h, r) in enumerate(held):
+                src_ref[h, r] = ref[k]
 
         def first(owner, carry):
             block(owner, own0_ref, oth0_ref, 0)
@@ -264,8 +248,8 @@
             block(owner, own1_ref, oth1_ref, cut)
             return carry
 
-        lax.fori_loop(0, cut, first, 0, unroll=2)
-        lax.fori_loop(cut, shards, second, 0, unroll=2)
+        lax.fori_loop(0, cut, first, 0, unroll=4)
+        lax.fori_loop(cut, shards, second, 0, unroll=4)
 
     table = jnp.concatenate((hi_ref[...], hi_ref[...], lo_ref[...]))
     rows = []
@@ -277,15 +261,16 @@
     out_ref[...] = dot_nn(jnp.concatenate(rows), table).reshape(per, channels, lags)
 
 
-def correlate(j, previous, shard, own, other, blocks, samples, sources):
-    size, lanes = blocks[0].shape
-    shards = len(blocks)
+def correlate(j, previous, shard, own, other, stacks, samples, sources):
+    stacked = [held for held, _ in stacks]
+    shards = sum(map(len, stacked)) // 2
+    size, lanes = stacks[0][1].shape[1:]
     channels = own[0].shape[1]
     per = 16
     steps = size // per
     pitch = size + 8
     high, low = split_const(inverse_table(samples))
-    operands = [*own, *other, high, low, *blocks]
+    operands = [*own, *other, high, low, *(x for _, x in stacks)]
     in_specs = [whole(x.shape) for x in operands]
     aliases = {}
     if previous is not None:
@@ -293,7 +278,7 @@
         operands.append(previous)
         in_specs.append(pl.BlockSpec(memory_space=pl.ANY))
     return pl.pallas_call(
-        functools.partial(stack_kernel, shards=shards, pitch=pitch),
+        functools.partial(stack_kernel, stacked=stacked, pitch=pitch),
         grid_spec=pltpu.PrefetchScalarGridSpec(
             num_scalar_prefetch=1,
             grid=(steps,),
@@ -302,12 +287,12 @@
             scratch_shapes=[
                 pltpu.VMEM((F * pitch, channels), F32),
                 pltpu.VMEM((F * pitch, channels), F32),
-                pltpu.VMEM((shards, size, lanes), F32),
+                pltpu.VMEM((2, shards, size, lanes), F32),
             ],
         ),
         out_shape=jax.ShapeDtypeStruct((sources, channels, LAGS), F32),
         input_output_aliases=aliases,
-        compiler_params=pltpu.CompilerParams(vmem_limit_bytes=48 * 2**20, dimension_semantics=("arbitrary",)),
+        compiler_params=pltpu.CompilerParams(vmem_limit_bytes=36 * 2**20, dimension_semantics=("arbitrary",)),
         cost_estimate=pl.CostEstimate(flops=20 * 10**9 // CHUNKS, bytes_accessed=48 * 2**20 // CHUNKS, transcendentals=0),
         name="stack_lags",
     )(shard[None], *operands)
@@ -315,6 +300,31 @@
 
 def swap(x, axis, bits):
     return lax.ppermute(x, axis, [(i, i ^ bits) for i in range(lax.axis_size(axis))])
+
+
+def gather(own, crossing, passed):
+    crossing, passed = lax.optimization_barrier((crossing, passed))
+    other = swap(crossing, "half", 1)
+    first = [swap(own, "shard", r) for r in (8, 4, 2)]
+    *first, after = lax.optimization_barrier((*first, other))
+    second = [swap(after, "shard", r) for r in (8, 4, 2)]
+    *two, own, after = lax.optimization_barrier((*first, *second, own, after))
+    first, second = two[:3], two[3:]
+    mine = jnp.stack((own, after))
+    line = jnp.stack((first[0], second[0], first[1], second[1]))
+    far = swap(mine, "shard", 12)
+    across = swap(line, "shard", 2)
+    far_across = swap(far, "shard", 2)
+    stacks = []
+    for relative, blocks in (
+        ((8, 4), line),
+        ((0, 2), jnp.concatenate((mine, jnp.stack((first[2], second[2]))))),
+        ((10, 6), across),
+        ((12, 14), jnp.concatenate((far, far_across))),
+    ):
+        held = [(h, r) for r in relative for h in range(2)]
+        stacks += [(held, blocks), ([(h, r + 1) for h, r in held], swap(blocks, "shard", 1))]
+    return stacks, passed, other
 
 
 def body(recording, source_channels):
@@ -335,22 +345,10 @@
         lambda m: list(m),
         list(mine),
     )
-    other_first, *crossing = lax.optimization_barrier((other_first, *mine[CHUNKS:]))
-    crossed = [swap(x, "half", 1) for x in crossing]
-    second, *crossed = lax.optimization_barrier((second, *crossed))
+    stacks, other_first, crossed = gather(mine[0], mine[1], other_first)
+    second, crossed = lax.optimization_barrier((second, crossed))
     own, other = (first, second), (other_first, swap(second, "half", 1))
-
-    result = None
-    for j in range(CHUNKS):
-        blocks = {0: pair_halves(mine[j], crossed[j], 2 * segs)}
-        for k in range(1, shards // 4):
-            blocks[4 * k] = swap(blocks[0], "shard", 4 * k)
-        for bit in (2, 1):
-            for r, x in list(blocks.items()):
-                blocks[r ^ bit] = swap(x, "shard", bit)
-        group = [blocks[r] for r in range(shards)]
-        result = correlate(j, result, shard, own, other, group, samples, nsrc // 2)
-    return result
+    return correlate(0, None, shard, own, other, stacks, samples, nsrc // 2)
 
 
 def plain_forward_table(samples, freq_count):

time: 118 us -> 101 us (0.86)
  waiting for transfers between devices: 53.2 us -> 35.5 us
  starting transfers between devices: 22.8 us -> 27.7 us
  Pallas kernels: 37.7 us -> 35.6 us
  local copies, waits for them, and re-layouts: 2.04 us -> 0.06 us
    ppermute x18 -> x16, waiting for transfers between devices: 42 us -> 24.2 us  [swap(): lax.ppermute(x, axis, [(i, i ^ bits) for i in range(lax.axis_size(axis))])]
    ppermute x18 -> x16, starting transfers between devices: 15.4 us -> 20.4 us  [swap(): lax.ppermute(x, axis, [(i, i ^ bits) for i in range(lax.axis_size(axis))])]
    pallas_call x2 -> x1, Pallas kernels: 25.4 us -> 23.3 us  [correlate(): pl.pallas_call(functools.partial(stack_kernel, stacked=stacked, pitch=pit...]
    unnamed x14 -> x9, local copies, waits for them, and re-layouts: 2.04 us -> 0.04 us
  transfers between devices with their start and end apart: 19 -> 17, of which waited for: 10 -> 11; matrix products, arithmetic and copies ran while one was open for 1% -> 1% of each run, Pallas kernels for 3% -> 1%
where the time goes in v3:
time: 101 us
  Pallas kernels  35.6 us (35%)
  waiting for transfers between devices  35.5 us (35%)
  starting transfers between devices  27.7 us (27%)
    ppermute x16, waiting for transfers between devices, swap(): lax.ppermute(x, axis, [(i, i ^ bits) for i in range(lax.axis_size(axis))])  24.2 us
    pallas_call x1, Pallas kernels, correlate(): pl.pallas_call(functools.partial(stack_kernel, stacked=stacked, pitch=pit...  23.3 us
    ppermute x16, starting transfers between devices, swap(): lax.ppermute(x, axis, [(i, i ^ bits) for i in range(lax.axis_size(axis))])  20.4 us
    all_to_all x1, waiting for transfers between devices, body(): got = lax.all_to_all(held, 'shard', split_axis=0, concat_axis=0, tiled=True)  11.3 us
    pallas_call x1, Pallas kernels, forward(): pl.pallas_call(functools.partial(spectra_kernel, segs=segs), grid_spec=pl...  11.2 us
    all_to_all x1, starting transfers between devices, body(): got = lax.all_to_all(held, 'shard', split_axis=0, concat_axis=0, tiled=True)  7.33 us
  transfers between devices with their start and end apart: 17, of which 11 were waited for; matrix products, arithmetic and copies ran while one was open for 1% of the time, Pallas kernels for 1%

profile of v3, /device:TPU:0, one launch (start us, length us, event | category | flops | bytes accessed | tf_op | source)
XLA Modules:
  0.0 100.6 jit_solution(8595920974221483273)
XLA Ops:
  0.0 0.0 copy-start.3
  0.0 11.2 %forward_whiten.1 = (f32[1280,128]{1,0:T(8,128)}, f32[2816,128]{1,0:T(8,128)}, f32[16,32,256]{2,1,0:T(8,128)}) custom-call(s32[1]{0:T(128)} %bitcast.6.place_ref, f32[16,128,1024]{2,1,0:T(8,128)} %rec_ref.1, bf16[256,1024]{1,0:T(8,128)(2,1)} %constant.61.clone.hi_ref, bf16[256,1024]{1,0:T(8,128)(2,1)} %constant.62.clone.lo_ref, s32[1,256]{1,0:T(1,128)} %bitcast.31), custom_call_target="tpu_custom_call" | custom-call | flops 6000000000 | bytes 16777216 | tf_op jit(solution)/shard_map/forward_whiten/pallas_call | solution.py:136
  11.2 7.3 %all-to-all-start.1 = ((f32[16,32,256]{2,1,0:T(8,128)}), f32[16,32,256]{2,1,0:T(8,128)S(1)}, u32[]{:S(2)}, u32[]{:S(2)}) async-start(f32[16,32,256]{2,1,0:T(8,128)} %get-tuple-element.43), calls=%async_computation.1 | async-start | bytes 1048576 | tf_op jit(solution)/shard_map/all_to_all | solution.py:339
  18.6 1.6 %collective-permute-start = (f32[1280,128]{1,0:T(8,128)}, f32[1280,128]{1,0:T(8,128)S(1)}, u32[]{:S(2)}, u32[]{:S(2)}) collective-permute-start(f32[1280,128]{1,0:T(8,128)} %get-tuple-element.41.own0_ref), channel_id=1, source_target_pairs={{0,16},{16,0},{1,17},{17,1},{2,18},{18,2},{3,19},{19,3},{4,20},{20... | collective-permute-start | bytes 1966088 | tf_op jit(solution)/shard_map/ppermute | solution.py:302
  20.2 0.0 copy-done.3
  20.2 0.1 convert_reduce_fusion
  20.3 0.7 reduce_max.9
  21.6 0.1 pad_add_fusion.place_ref
  21.7 11.3 %all-to-all-done.1 = f32[16,32,256]{2,1,0:T(8,128)S(1)} async-done(((f32[16,32,256]{2,1,0:T(8,128)}), f32[16,32,256]{2,1,0:T(8,128)S(1)}, u32[]{:S(2)}, u32[]{:S(2)}) %all-to-all-start.1) | async-done | bytes 524320 | tf_op jit(solution)/shard_map/all_to_all | solution.py:339
  33.0 1.1 %order_sources.1 = (f32[128,256]{1,0:T(8,128)S(1)}, f32[128,256]{1,0:T(8,128)S(1)}) custom-call(s32[2]{0:T(128)S(1)} %pad_add_fusion.place_ref, f32[512,256]{1,0:T(8,128)S(1)} %bitcast.18, s32[1,256]{1,0:T(1,128)S(1)} %bitcast.32), custom_call_target="tpu_custom_call" | custom-call | flops 100000000 | bytes 1048576 | tf_op jit(solution)/shard_map/order_sources/pallas_call | solution.py:180
  34.1 0.0 copy-start
  34.2 0.0 copy-start.1
  34.2 0.0 copy-start.2
  34.2 1.7 %collective-permute-done.oth0_ref = f32[1280,128]{1,0:T(8,128)S(1)} collective-permute-done((f32[1280,128]{1,0:T(8,128)}, f32[1280,128]{1,0:T(8,128)S(1)}, u32[]{:S(2)}, u32[]{:S(2)}) %collective-permute-start) | collective-permute-done | bytes 655392 | tf_op jit(solution)/shard_map/ppermute | solution.py:302
  35.8 1.5 %collective-permute-start.1 = (f32[128,256]{1,0:T(8,128)S(1)}, f32[128,256]{1,0:T(8,128)S(1)}, u32[]{:S(2)}, u32[]{:S(2)}) collective-permute-start(f32[128,256]{1,0:T(8,128)S(1)} %get-tuple-element.45), channel_id=1, source_target_pairs={{0,16},{16,0},{1,17},{17,1},{2,18},{18,2},{3,19},{19,3},{4,20},{20... | collective-permute-start | bytes 393224 | tf_op jit(solution)/shard_map/ppermute | solution.py:302
  37.4 1.7 %collective-permute-start.5 = (f32[128,256]{1,0:T(8,128)S(1)}, f32[128,256]{1,0:T(8,128)S(1)}, u32[]{:S(2)}, u32[]{:S(2)}) collective-permute-start(f32[128,256]{1,0:T(8,128)S(1)} %get-tuple-element.57), channel_id=1, source_target_pairs={{0,2},{1,3},{2,0},{3,1},{4,6},{5,7},{6,4},{7,5},{8,10},{9,11},{10,... | collective-permute-start | bytes 393224 | tf_op jit(solution)/shard_map/ppermute | solution.py:302
  39.0 1.5 %collective-permute-start.4 = (f32[128,256]{1,0:T(8,128)S(1)}, f32[128,256]{1,0:T(8,128)S(1)}, u32[]{:S(2)}, u32[]{:S(2)}) collective-permute-start(f32[128,256]{1,0:T(8,128)S(1)} %get-tuple-element.57), channel_id=1, source_target_pairs={{0,4},{1,5},{2,6},{3,7},{4,0},{5,1},{6,2},{7,3},{8,12},{9,13},{10,... | collective-permute-start | bytes 393224 | tf_op jit(solution)/shard_map/ppermute | solution.py:302
  40.5 2.4 %collective-permute-start.3 = (f32[128,256]{1,0:T(8,128)S(1)}, f32[128,256]{1,0:T(8,128)S(1)}, u32[]{:S(2)}, u32[]{:S(2)}) collective-permute-start(f32[128,256]{1,0:T(8,128)S(1)} %get-tuple-element.57), channel_id=1, source_target_pairs={{0,8},{1,9},{2,10},{3,11},{4,12},{5,13},{6,14},{7,15},{8,0},{9,1},... | collective-permute-start | bytes 393224 | tf_op jit(solution)/shard_map/ppermute | solution.py:302
  42.9 0.0 collective-permute-done.1
  42.9 0.5 collective-permute-start.2
  43.4 0.0 collective-permute-done.5
  43.4 2.2 %collective-permute-done.4 = f32[128,256]{1,0:T(8,128)S(1)} collective-permute-done((f32[128,256]{1,0:T(8,128)S(1)}, f32[128,256]{1,0:T(8,128)S(1)}, u32[]{:S(2)}, u32[]{:S(2)}) %collective-permute-start.4) | collective-permute-done | bytes 131104 | tf_op jit(solution)/shard_map/ppermute | solution.py:302
  45.5 2.6 %collective-permute-done.3 = f32[128,256]{1,0:T(8,128)S(1)} collective-permute-done((f32[128,256]{1,0:T(8,128)S(1)}, f32[128,256]{1,0:T(8,128)S(1)}, u32[]{:S(2)}, u32[]{:S(2)}) %collective-permute-start.3) | collective-permute-done | bytes 131104 | tf_op jit(solution)/shard_map/ppermute | solution.py:302
  48.1 0.6 collective-permute-start.8
  48.7 0.3 collective-permute-start.7
  49.1 2.8 %collective-permute-start.6 = (f32[128,256]{1,0:T(8,128)S(1)}, f32[128,256]{1,0:T(8,128)S(1)}, u32[]{:S(2)}, u32[]{:S(2)}) collective-permute-start(f32[128,256]{1,0:T(8,128)S(1)} %collective-permute-done.1), channel_id=1, source_target_pairs={{0,8},{1,9},{2,10},{3,11},{4,12},{5,13},{6,14},{7,15},{8,0},{9,1},... | collective-permute-start | bytes 393224 | tf_op jit(solution)/shard_map/ppermute | solution.py:302
  51.8 1.2 %collective-permute-done.8 = f32[128,256]{1,0:T(8,128)S(1)} collective-permute-done((f32[128,256]{1,0:T(8,128)S(1)}, f32[128,256]{1,0:T(8,128)S(1)}, u32[]{:S(2)}, u32[]{:S(2)}) %collective-permute-start.8) | collective-permute-done | bytes 131104 | tf_op jit(solution)/shard_map/ppermute | solution.py:302
  53.1 1.8 %collective-permute-done.7 = f32[128,256]{1,0:T(8,128)S(1)} collective-permute-done((f32[128,256]{1,0:T(8,128)S(1)}, f32[128,256]{1,0:T(8,128)S(1)}, u32[]{:S(2)}, u32[]{:S(2)}) %collective-permute-start.7) | collective-permute-done | bytes 131104 | tf_op jit(solution)/shard_map/ppermute | solution.py:302
  54.9 4.5 %collective-permute-done.6 = f32[128,256]{1,0:T(8,128)S(1)} collective-permute-done((f32[128,256]{1,0:T(8,128)S(1)}, f32[128,256]{1,0:T(8,128)S(1)}, u32[]{:S(2)}, u32[]{:S(2)}) %collective-permute-start.6) | collective-permute-done | bytes 131104 | tf_op jit(solution)/shard_map/ppermute | solution.py:302
  59.4 3.1 %collective-permute-start.13 = (f32[2,128,256]{2,1,0:T(8,128)S(1)}, f32[2,128,256]{2,1,0:T(8,128)S(1)}, u32[]{:S(2)}, u32[]{:S(2)}) collective-permute-start(f32[2,128,256]{2,1,0:T(8,128)S(1)} %pad_maximum_fusion.3), channel_id=1, source_target_pairs={{0,12},{1,13},{2,14},{3,15},{4,8},{5,9},{6,10},{7,11},{8,4},{9,5},... | collective-permute-start | bytes 786440 | tf_op jit(solution)/shard_map/ppermute | solution.py:302
  62.5 1.7 %collective-permute-start.11 = (f32[4,128,256]{2,1,0:T(8,128)S(1)}, f32[4,128,256]{2,1,0:T(8,128)S(1)}, u32[]{:S(2)}, u32[]{:S(2)}) collective-permute-start(f32[4,128,256]{2,1,0:T(8,128)S(1)} %pad_maximum_fusion.1.refs_0_), channel_id=1, source_target_pairs={{0,2},{1,3},{2,0},{3,1},{4,6},{5,7},{6,4},{7,5},{8,10},{9,11},{10,... | collective-permute-start | bytes 1572872 | tf_op jit(solution)/shard_map/ppermute | solution.py:302
  64.2 3.4 %collective-permute-done.13 = f32[2,128,256]{2,1,0:T(8,128)S(1)} collective-permute-done((f32[2,128,256]{2,1,0:T(8,128)S(1)}, f32[2,128,256]{2,1,0:T(8,128)S(1)}, u32[]{:S(2)}, u32[]{:S(2)}) %collective-permute-start.13) | collective-permute-done | bytes 262176 | tf_op jit(solution)/shard_map/ppermute | solution.py:302
  67.6 1.6 %collective-permute-start.14 = (f32[2,128,256]{2,1,0:T(8,128)S(1)}, f32[2,128,256]{2,1,0:T(8,128)S(1)}, u32[]{:S(2)}, u32[]{:S(2)}) collective-permute-start(f32[2,128,256]{2,1,0:T(8,128)S(1)} %collective-permute-done.13), channel_id=1, source_target_pairs={{0,2},{1,3},{2,0},{3,1},{4,6},{5,7},{6,4},{7,5},{8,10},{9,11},{10,... | collective-permute-start | bytes 786440 | tf_op jit(solution)/shard_map/ppermute | solution.py:302
  69.2 0.0 collective-permute-start.9
  69.3 0.6 collective-permute-start.10
  69.9 4.7 %collective-permute-done.14 = f32[2,128,256]{2,1,0:T(8,128)S(1)} collective-permute-done((f32[2,128,256]{2,1,0:T(8,128)S(1)}, f32[2,128,256]{2,1,0:T(8,128)S(1)}, u32[]{:S(2)}, u32[]{:S(2)}) %collective-permute-start.14) | collective-permute-done | bytes 262176 | tf_op jit(solution)/shard_map/ppermute | solution.py:302
  74.6 0.1 collective-permute-start.15
  74.7 0.0 collective-permute-done.11.refs_4_
  74.7 0.5 collective-permute-start.12
  75.2 0.0 collective-permute-done.10.refs_3_
  75.2 0.0 collective-permute-done.9.refs_1_
  75.2 1.4 %collective-permute-done.15.refs_7_ = f32[4,128,256]{2,1,0:T(8,128)S(1)} collective-permute-done((f32[4,128,256]{2,1,0:T(8,128)S(1)}, f32[4,128,256]{2,1,0:T(8,128)S(1)}, u32[]{:S(2)}, u32[]{:S(2)}) %collective-permute-start.15) | collective-permute-done | bytes 524320 | tf_op jit(solution)/shard_map/ppermute | solution.py:302
  76.6 0.7 collective-permute-done.12.refs_5_
  77.3 0.0 collective-permute-done.2.oth1_ref
  77.3 0.0 copy-done
  77.3 0.0 copy-done.1
  77.3 0.0 copy-done.2
  77.3 23.3 %stack_lags.1 = f32[128,128,512]{2,1,0:T(8,128)} custom-call(s32[1]{0:T(128)} %bitcast.6.place_ref, f32[1280,128]{1,0:T(8,128)} %get-tuple-element.41.own0_ref, f32[2816,128]{1,0:T(8,128)S(1)} %copy-done.2, f32[1280,128]{1,0:T(8,128)S(1)} %collective-permute-done.oth0_ref, f32[2816,128]{1,0:T(8,128)S(1)} %collective-permute-done.2.oth1_ref, ...), custom_call_target="tpu_custom_call" | custom-call | flops 20000000000 | bytes 50331648 | tf_op jit(solution)/shard_map/stack_lags/pallas_call | solution.py:280
  (7 shorter events, 0.1 us)
Async XLA Ops:
  0.0 20.2 %copy-start.3 = (s32[256]{0:T(256)S(1)}, s32[256]{0:T(256)}, u32[]{:S(2)}) copy-start(s32[256]{0:T(256)} %param.9) | copy-start | bytes 3076
  11.2 21.8 %all-to-all-start.1 = ((f32[16,32,256]{2,1,0:T(8,128)}), f32[16,32,256]{2,1,0:T(8,128)S(1)}, u32[]{:S(2)}, u32[]{:S(2)}) async-start(f32[16,32,256]{2,1,0:T(8,128)} %get-tuple-element.43), calls=%async_computation.1 | async-start | bytes 1048576 | tf_op jit(solution)/shard_map/all_to_all | solution.py:339
  18.6 17.3 %collective-permute-start = (f32[1280,128]{1,0:T(8,128)}, f32[1280,128]{1,0:T(8,128)S(1)}, u32[]{:S(2)}, u32[]{:S(2)}) collective-permute-start(f32[1280,128]{1,0:T(8,128)} %get-tuple-element.41.own0_ref), channel_id=1, source_target_pairs={{0,16},{16,0},{1,17},{17,1},{2,18},{18,2},{3,19},{19,3},{4,20},{20... | collective-permute-start | bytes 1966088 | tf_op jit(solution)/shard_map/ppermute | solution.py:302
  34.1 43.2 %copy-start = (bf16[256,512]{1,0:T(8,128)(2,1)S(1)}, bf16[256,512]{1,0:T(8,128)(2,1)}, u32[]{:S(2)}) copy-start(bf16[256,512]{1,0:T(8,128)(2,1)} %constant.64.clone.lo_ref) | copy-start | bytes 786436
  34.2 43.2 %copy-start.1 = (bf16[256,512]{1,0:T(8,128)(2,1)S(1)}, bf16[256,512]{1,0:T(8,128)(2,1)}, u32[]{:S(2)}) copy-start(bf16[256,512]{1,0:T(8,128)(2,1)} %constant.63.clone.hi_ref) | copy-start | bytes 786436
  34.2 43.2 %copy-start.2 = (f32[2816,128]{1,0:T(8,128)S(1)}, f32[2816,128]{1,0:T(8,128)}, u32[]{:S(2)}) copy-start(f32[2816,128]{1,0:T(8,128)} %get-tuple-element.46.own1_ref) | copy-start | bytes 4325380
  35.8 7.0 %collective-permute-start.1 = (f32[128,256]{1,0:T(8,128)S(1)}, f32[128,256]{1,0:T(8,128)S(1)}, u32[]{:S(2)}, u32[]{:S(2)}) collective-permute-start(f32[128,256]{1,0:T(8,128)S(1)} %get-tuple-element.45), channel_id=1, source_target_pairs={{0,16},{16,0},{1,17},{17,1},{2,18},{18,2},{3,19},{19,3},{4,20},{20... | collective-permute-start | bytes 393224 | tf_op jit(solution)/shard_map/ppermute | solution.py:302
  37.4 6.0 %collective-permute-start.5 = (f32[128,256]{1,0:T(8,128)S(1)}, f32[128,256]{1,0:T(8,128)S(1)}, u32[]{:S(2)}, u32[]{:S(2)}) collective-permute-start(f32[128,256]{1,0:T(8,128)S(1)} %get-tuple-element.57), channel_id=1, source_target_pairs={{0,2},{1,3},{2,0},{3,1},{4,6},{5,7},{6,4},{7,5},{8,10},{9,11},{10,... | collective-permute-start | bytes 393224 | tf_op jit(solution)/shard_map/ppermute | solution.py:302
  39.0 6.5 %collective-permute-start.4 = (f32[128,256]{1,0:T(8,128)S(1)}, f32[128,256]{1,0:T(8,128)S(1)}, u32[]{:S(2)}, u32[]{:S(2)}) collective-permute-start(f32[128,256]{1,0:T(8,128)S(1)} %get-tuple-element.57), channel_id=1, source_target_pairs={{0,4},{1,5},{2,6},{3,7},{4,0},{5,1},{6,2},{7,3},{8,12},{9,13},{10,... | collective-permute-start | bytes 393224 | tf_op jit(solution)/shard_map/ppermute | solution.py:302
  40.5 7.6 %collective-permute-start.3 = (f32[128,256]{1,0:T(8,128)S(1)}, f32[128,256]{1,0:T(8,128)S(1)}, u32[]{:S(2)}, u32[]{:S(2)}) collective-permute-start(f32[128,256]{1,0:T(8,128)S(1)} %get-tuple-element.57), channel_id=1, source_target_pairs={{0,8},{1,9},{2,10},{3,11},{4,12},{5,13},{6,14},{7,15},{8,0},{9,1},... | collective-permute-start | bytes 393224 | tf_op jit(solution)/shard_map/ppermute | solution.py:302
  42.9 34.4 %collective-permute-start.2 = (f32[2816,128]{1,0:T(8,128)}, f32[2816,128]{1,0:T(8,128)S(1)}, u32[]{:S(2)}, u32[]{:S(2)}) collective-permute-start(f32[2816,128]{1,0:T(8,128)} %get-tuple-element.46.own1_ref), channel_id=1, source_target_pairs={{0,16},{16,0},{1,17},{17,1},{2,18},{18,2},{3,19},{19,3},{4,20},{20... | collective-permute-start | bytes 4325384 | tf_op jit(solution)/shard_map/ppermute | solution.py:302
  48.1 5.0 %collective-permute-start.8 = (f32[128,256]{1,0:T(8,128)S(1)}, f32[128,256]{1,0:T(8,128)S(1)}, u32[]{:S(2)}, u32[]{:S(2)}) collective-permute-start(f32[128,256]{1,0:T(8,128)S(1)} %collective-permute-done.1), channel_id=1, source_target_pairs={{0,2},{1,3},{2,0},{3,1},{4,6},{5,7},{6,4},{7,5},{8,10},{9,11},{10,... | collective-permute-start | bytes 393224 | tf_op jit(solution)/shard_map/ppermute | solution.py:302
  48.7 6.1 %collective-permute-start.7 = (f32[128,256]{1,0:T(8,128)S(1)}, f32[128,256]{1,0:T(8,128)S(1)}, u32[]{:S(2)}, u32[]{:S(2)}) collective-permute-start(f32[128,256]{1,0:T(8,128)S(1)} %collective-permute-done.1), channel_id=1, source_target_pairs={{0,4},{1,5},{2,6},{3,7},{4,0},{5,1},{6,2},{7,3},{8,12},{9,13},{10,... | collective-permute-start | bytes 393224 | tf_op jit(solution)/shard_map/ppermute | solution.py:302
  49.1 10.3 %collective-permute-start.6 = (f32[128,256]{1,0:T(8,128)S(1)}, f32[128,256]{1,0:T(8,128)S(1)}, u32[]{:S(2)}, u32[]{:S(2)}) collective-permute-start(f32[128,256]{1,0:T(8,128)S(1)} %collective-permute-done.1), channel_id=1, source_target_pairs={{0,8},{1,9},{2,10},{3,11},{4,12},{5,13},{6,14},{7,15},{8,0},{9,1},... | collective-permute-start | bytes 393224 | tf_op jit(solution)/shard_map/ppermute | solution.py:302
  59.4 8.2 %collective-permute-start.13 = (f32[2,128,256]{2,1,0:T(8,128)S(1)}, f32[2,128,256]{2,1,0:T(8,128)S(1)}, u32[]{:S(2)}, u32[]{:S(2)}) collective-permute-start(f32[2,128,256]{2,1,0:T(8,128)S(1)} %pad_maximum_fusion.3), channel_id=1, source_target_pairs={{0,12},{1,13},{2,14},{3,15},{4,8},{5,9},{6,10},{7,11},{8,4},{9,5},... | collective-permute-start | bytes 786440 | tf_op jit(solution)/shard_map/ppermute | solution.py:302
  62.5 12.2 %collective-permute-start.11 = (f32[4,128,256]{2,1,0:T(8,128)S(1)}, f32[4,128,256]{2,1,0:T(8,128)S(1)}, u32[]{:S(2)}, u32[]{:S(2)}) collective-permute-start(f32[4,128,256]{2,1,0:T(8,128)S(1)} %pad_maximum_fusion.1.refs_0_), channel_id=1, source_target_pairs={{0,2},{1,3},{2,0},{3,1},{4,6},{5,7},{6,4},{7,5},{8,10},{9,11},{10,... | collective-permute-start | bytes 1572872 | tf_op jit(solution)/shard_map/ppermute | solution.py:302
  67.6 7.0 %collective-permute-start.14 = (f32[2,128,256]{2,1,0:T(8,128)S(1)}, f32[2,128,256]{2,1,0:T(8,128)S(1)}, u32[]{:S(2)}, u32[]{:S(2)}) collective-permute-start(f32[2,128,256]{2,1,0:T(8,128)S(1)} %collective-permute-done.13), channel_id=1, source_target_pairs={{0,2},{1,3},{2,0},{3,1},{4,6},{5,7},{6,4},{7,5},{8,10},{9,11},{10,... | collective-permute-start | bytes 786440 | tf_op jit(solution)/shard_map/ppermute | solution.py:302
  69.2 6.0 %collective-permute-start.9 = (f32[4,128,256]{2,1,0:T(8,128)S(1)}, f32[4,128,256]{2,1,0:T(8,128)S(1)}, u32[]{:S(2)}, u32[]{:S(2)}) collective-permute-start(f32[4,128,256]{2,1,0:T(8,128)S(1)} %pad_maximum_fusion.1.refs_0_), channel_id=1, source_target_pairs={{0,1},{1,0},{2,3},{3,2},{4,5},{5,4},{6,7},{7,6},{8,9},{9,8},{10,11... | collective-permute-start | bytes 1572872 | tf_op jit(solution)/shard_map/ppermute | solution.py:302
  69.3 5.9 %collective-permute-start.10 = (f32[4,128,256]{2,1,0:T(8,128)S(1)}, f32[4,128,256]{2,1,0:T(8,128)S(1)}, u32[]{:S(2)}, u32[]{:S(2)}) collective-permute-start(f32[4,128,256]{2,1,0:T(8,128)S(1)} %pad_maximum_fusion.2.refs_2_), channel_id=1, source_target_pairs={{0,1},{1,0},{2,3},{3,2},{4,5},{5,4},{6,7},{7,6},{8,9},{9,8},{10,11... | collective-permute-start | bytes 1572872 | tf_op jit(solution)/shard_map/ppermute | solution.py:302
  74.6 2.0 %collective-permute-start.15 = (f32[4,128,256]{2,1,0:T(8,128)S(1)}, f32[4,128,256]{2,1,0:T(8,128)S(1)}, u32[]{:S(2)}, u32[]{:S(2)}) collective-permute-start(f32[4,128,256]{2,1,0:T(8,128)S(1)} %constant_dynamic-update-slice_fusion.refs_6_), channel_id=1, source_target_pairs={{0,1},{1,0},{2,3},{3,2},{4,5},{5,4},{6,7},{7,6},{8,9},{9,8},{10,11... | collective-permute-start | bytes 1572872 | tf_op jit(solution)/shard_map/ppermute | solution.py:302
  74.7 2.6 %collective-permute-start.12 = (f32[4,128,256]{2,1,0:T(8,128)S(1)}, f32[4,128,256]{2,1,0:T(8,128)S(1)}, u32[]{:S(2)}, u32[]{:S(2)}) collective-permute-start(f32[4,128,256]{2,1,0:T(8,128)S(1)} %collective-permute-done.11.refs_4_), channel_id=1, source_target_pairs={{0,1},{1,0},{2,3},{3,2},{4,5},{5,4},{6,7},{7,6},{8,9},{9,8},{10,11... | collective-permute-start | bytes 1572872 | tf_op jit(solution)/shard_map/ppermute | solution.py:302

commit v4 on v3

--- a/solution.py
+++ b/solution.py
@@ -27,7 +27,7 @@
     times = np.arange(samples, dtype=np.int64)
     angle = 2.0 * np.pi * (bins[:, None] * times[None, :] % samples) / samples
     taper = 0.5 - 0.5 * np.cos(2.0 * np.pi * times / samples)
-    return np.concatenate((np.cos(angle) * taper, -np.sin(angle) * taper)).astype(np.float32)
+    return np.concatenate((np.cos(angle) * taper, -np.sin(angle) * taper)).T.astype(np.float32)
 
 
 def inverse_table(samples):
@@ -85,11 +85,10 @@
 def spectra_kernel(place_ref, rec_ref, hi_ref, lo_ref, row_ref, first_ref, second_ref, held_ref, *, segs):
     step = pl.program_id(0)
     per, channels, samples = rec_ref.shape
-    high, low = split(rec_ref[...].reshape(per * channels, samples))
-    spectra = dot_nt(hi_ref[...], high) + (dot_nt(lo_ref[...], high) + dot_nt(hi_ref[...], low))
     for i in range(per):
-        lanes = slice(i * channels, (i + 1) * channels)
-        real, imag = whiten_tile(spectra[:F, lanes], spectra[F:, lanes])
+        high, low = split(rec_ref[i])
+        spectra = dot_nn(high, hi_ref[...]) + (dot_nn(low, hi_ref[...]) + dot_nn(high, lo_ref[...]))
+        real, imag = whiten_tile(jnp.transpose(spectra[:, :F]), jnp.transpose(spectra[:, F:]))
         seg = step * per + i
         for ref, start in ((first_ref, 0), (second_ref, first_ref.shape[0] // (2 * segs))):
             count = ref.shape[0] // (2 * segs)
@@ -140,8 +139,8 @@
             grid=(segs // per,),
             in_specs=[
                 pl.BlockSpec((per, channels, samples), lambda s, p: (s, 0, 0)),
-                whole((2 * F, samples)),
-                whole((2 * F, samples)),
+                whole((samples, 2 * F)),
+                whole((samples, 2 * F)),
                 whole((1, nsrc)),
             ],
             out_specs=[whole(x) for x in (*white, held)],
@@ -240,16 +239,17 @@
             for k, (h, r) in enumerate(held):
                 src_ref[h, r] = ref[k]
 
-        def first(owner, carry):
-            block(owner, own0_ref, oth0_ref, 0)
+        def four(group, carry, parts):
+            for k, (own_ref, oth_ref, skip) in enumerate(parts):
+                block(4 * group + k, own_ref, oth_ref, skip)
             return carry
 
-        def second(owner, carry):
-            block(owner, own1_ref, oth1_ref, cut)
-            return carry
-
-        lax.fori_loop(0, cut, first, 0, unroll=4)
-        lax.fori_loop(cut, shards, second, 0, unroll=4)
+        for group in range(shards // 4):
+            parts = [
+                (own0_ref, oth0_ref, 0) if owner < cut else (own1_ref, oth1_ref, cut)
+                for owner in range(4 * group, 4 * group + 4)
+            ]
+            lax.fori_loop(group, group + 1, functools.partial(four, parts=parts), 0)
 
     table = jnp.concatenate((hi_ref[...], hi_ref[...], lo_ref[...]))
     rows = []
@@ -314,6 +314,7 @@
     line = jnp.stack((first[0], second[0], first[1], second[1]))
     far = swap(mine, "shard", 12)
     across = swap(line, "shard", 2)
+    far, mine, line = lax.optimization_barrier((far, mine, line))
     far_across = swap(far, "shard", 2)
     stacks = []
     for relative, blocks in (
@@ -352,7 +353,7 @@
 
 
 def plain_forward_table(samples, freq_count):
-    table = forward_table(samples)
+    table = forward_table(samples).T
     return jnp.stack((table[:freq_count], table[freq_count:]), axis=1)
 
 

time: 101 us -> 99.5 us (0.985)
  Pallas kernels: 35.6 us -> 34.2 us
where the time goes in v4:
time: 99.5 us; the launch traced here: 99.2 us
  waiting for transfers between devices  35.5 us (36%)
  Pallas kernels  34.2 us (34%)
  starting transfers between devices  27.7 us (28%)
    ppermute x16, waiting for transfers between devices, swap(): lax.ppermute(x, axis, [(i, i ^ bits) for i in range(lax.axis_size(axis))])  24.2 us
    pallas_call x1, Pallas kernels, correlate(): pl.pallas_call(functools.partial(stack_kernel, stacked=stacked, pitch=pit...  22.3 us
    ppermute x16, starting transfers between devices, swap(): lax.ppermute(x, axis, [(i, i ^ bits) for i in range(lax.axis_size(axis))])  20.4 us
    all_to_all x1, waiting for transfers between devices, body(): got = lax.all_to_all(held, 'shard', split_axis=0, concat_axis=0, tiled=True)  11.4 us
    pallas_call x1, Pallas kernels, forward(): pl.pallas_call(functools.partial(spectra_kernel, segs=segs), grid_spec=pl...  10.8 us
    all_to_all x1, starting transfers between devices, body(): got = lax.all_to_all(held, 'shard', split_axis=0, concat_axis=0, tiled=True)  7.37 us
  transfers between devices with their start and end apart: 17, of which 11 were waited for; matrix products, arithmetic and copies ran while one was open for 1% of the time, Pallas kernels for 1%

profile of v4, /device:TPU:0, one launch (start us, length us, event | category | flops | bytes accessed | tf_op | source)
XLA Modules:
  0.0 99.2 jit_solution(1957737793494813474)
XLA Ops:
  0.0 0.0 copy-start.3
  0.0 10.8 %forward_whiten.1 = (f32[1280,128]{1,0:T(8,128)}, f32[2816,128]{1,0:T(8,128)}, f32[16,32,256]{2,1,0:T(8,128)}) custom-call(s32[1]{0:T(128)} %bitcast.6.place_ref, f32[16,128,1024]{2,1,0:T(8,128)} %rec_ref.1, bf16[1024,256]{1,0:T(8,128)(2,1)} %constant.61.clone.hi_ref, bf16[1024,256]{1,0:T(8,128)(2,1)} %constant.62.clone.lo_ref, s32[1,256]{1,0:T(1,128)} %bitcast.29), custom_call_target="tpu_custom_call" | custom-call | flops 6000000000 | bytes 16777216 | tf_op jit(solution)/shard_map/forward_whiten/pallas_call | solution.py:135
  10.8 7.4 %all-to-all-start.1 = ((f32[16,32,256]{2,1,0:T(8,128)}), f32[16,32,256]{2,1,0:T(8,128)S(1)}, u32[]{:S(2)}, u32[]{:S(2)}) async-start(f32[16,32,256]{2,1,0:T(8,128)} %get-tuple-element.46), calls=%async_computation.1 | async-start | bytes 1048576 | tf_op jit(solution)/shard_map/all_to_all | solution.py:340
  18.2 1.6 %collective-permute-start = (f32[1280,128]{1,0:T(8,128)}, f32[1280,128]{1,0:T(8,128)S(1)}, u32[]{:S(2)}, u32[]{:S(2)}) collective-permute-start(f32[1280,128]{1,0:T(8,128)} %get-tuple-element.44.own0_ref), channel_id=1, source_target_pairs={{0,16},{16,0},{1,17},{17,1},{2,18},{18,2},{3,19},{19,3},{4,20},{20... | collective-permute-start | bytes 1966088 | tf_op jit(solution)/shard_map/ppermute | solution.py:302
  19.8 0.0 copy-done.3
  19.8 0.1 convert_reduce_fusion
  19.9 0.7 reduce_max.9
  21.2 0.1 pad_add_fusion.place_ref
  21.3 11.4 %all-to-all-done.1 = f32[16,32,256]{2,1,0:T(8,128)S(1)} async-done(((f32[16,32,256]{2,1,0:T(8,128)}), f32[16,32,256]{2,1,0:T(8,128)S(1)}, u32[]{:S(2)}, u32[]{:S(2)}) %all-to-all-start.1) | async-done | bytes 524320 | tf_op jit(solution)/shard_map/all_to_all | solution.py:340
  32.7 1.1 %order_sources.1 = (f32[128,256]{1,0:T(8,128)S(1)}, f32[128,256]{1,0:T(8,128)S(1)}) custom-call(s32[2]{0:T(128)S(1)} %pad_add_fusion.place_ref, f32[512,256]{1,0:T(8,128)S(1)} %bitcast.18, s32[1,256]{1,0:T(1,128)S(1)} %bitcast.30), custom_call_target="tpu_custom_call" | custom-call | flops 100000000 | bytes 1048576 | tf_op jit(solution)/shard_map/order_sources/pallas_call | solution.py:179
  33.8 0.0 copy-start
  33.8 0.0 copy-start.1
  33.8 0.0 copy-start.2
  33.8 1.7 %collective-permute-done.oth0_ref = f32[1280,128]{1,0:T(8,128)S(1)} collective-permute-done((f32[1280,128]{1,0:T(8,128)}, f32[1280,128]{1,0:T(8,128)S(1)}, u32[]{:S(2)}, u32[]{:S(2)}) %collective-permute-start) | collective-permute-done | bytes 655392 | tf_op jit(solution)/shard_map/ppermute | solution.py:302
  35.5 1.5 %collective-permute-start.1 = (f32[128,256]{1,0:T(8,128)S(1)}, f32[128,256]{1,0:T(8,128)S(1)}, u32[]{:S(2)}, u32[]{:S(2)}) collective-permute-start(f32[128,256]{1,0:T(8,128)S(1)} %get-tuple-element.48), channel_id=1, source_target_pairs={{0,16},{16,0},{1,17},{17,1},{2,18},{18,2},{3,19},{19,3},{4,20},{20... | collective-permute-start | bytes 393224 | tf_op jit(solution)/shard_map/ppermute | solution.py:302
  37.0 1.7 %collective-permute-start.5 = (f32[128,256]{1,0:T(8,128)S(1)}, f32[128,256]{1,0:T(8,128)S(1)}, u32[]{:S(2)}, u32[]{:S(2)}) collective-permute-start(f32[128,256]{1,0:T(8,128)S(1)} %get-tuple-element.56), channel_id=1, source_target_pairs={{0,2},{1,3},{2,0},{3,1},{4,6},{5,7},{6,4},{7,5},{8,10},{9,11},{10,... | collective-permute-start | bytes 393224 | tf_op jit(solution)/shard_map/ppermute | solution.py:302
  38.6 1.5 %collective-permute-start.4 = (f32[128,256]{1,0:T(8,128)S(1)}, f32[128,256]{1,0:T(8,128)S(1)}, u32[]{:S(2)}, u32[]{:S(2)}) collective-permute-start(f32[128,256]{1,0:T(8,128)S(1)} %get-tuple-element.56), channel_id=1, source_target_pairs={{0,4},{1,5},{2,6},{3,7},{4,0},{5,1},{6,2},{7,3},{8,12},{9,13},{10,... | collective-permute-start | bytes 393224 | tf_op jit(solution)/shard_map/ppermute | solution.py:302
  40.1 2.4 %collective-permute-start.3 = (f32[128,256]{1,0:T(8,128)S(1)}, f32[128,256]{1,0:T(8,128)S(1)}, u32[]{:S(2)}, u32[]{:S(2)}) collective-permute-start(f32[128,256]{1,0:T(8,128)S(1)} %get-tuple-element.56), channel_id=1, source_target_pairs={{0,8},{1,9},{2,10},{3,11},{4,12},{5,13},{6,14},{7,15},{8,0},{9,1},... | collective-permute-start | bytes 393224 | tf_op jit(solution)/shard_map/ppermute | solution.py:302
  42.5 0.0 collective-permute-done.1
  42.5 0.5 collective-permute-start.2
  43.0 0.0 collective-permute-done.5
  43.0 2.2 %collective-permute-done.4 = f32[128,256]{1,0:T(8,128)S(1)} collective-permute-done((f32[128,256]{1,0:T(8,128)S(1)}, f32[128,256]{1,0:T(8,128)S(1)}, u32[]{:S(2)}, u32[]{:S(2)}) %collective-permute-start.4) | collective-permute-done | bytes 131104 | tf_op jit(solution)/shard_map/ppermute | solution.py:302
  45.1 2.6 %collective-permute-done.3 = f32[128,256]{1,0:T(8,128)S(1)} collective-permute-done((f32[128,256]{1,0:T(8,128)S(1)}, f32[128,256]{1,0:T(8,128)S(1)}, u32[]{:S(2)}, u32[]{:S(2)}) %collective-permute-start.3) | collective-permute-done | bytes 131104 | tf_op jit(solution)/shard_map/ppermute | solution.py:302
  47.7 0.6 collective-permute-start.8
  48.3 0.3 collective-permute-start.7
  48.7 2.8 %collective-permute-start.6 = (f32[128,256]{1,0:T(8,128)S(1)}, f32[128,256]{1,0:T(8,128)S(1)}, u32[]{:S(2)}, u32[]{:S(2)}) collective-permute-start(f32[128,256]{1,0:T(8,128)S(1)} %collective-permute-done.1), channel_id=1, source_target_pairs={{0,8},{1,9},{2,10},{3,11},{4,12},{5,13},{6,14},{7,15},{8,0},{9,1},... | collective-permute-start | bytes 393224 | tf_op jit(solution)/shard_map/ppermute | solution.py:302
  51.4 1.2 %collective-permute-done.8 = f32[128,256]{1,0:T(8,128)S(1)} collective-permute-done((f32[128,256]{1,0:T(8,128)S(1)}, f32[128,256]{1,0:T(8,128)S(1)}, u32[]{:S(2)}, u32[]{:S(2)}) %collective-permute-start.8) | collective-permute-done | bytes 131104 | tf_op jit(solution)/shard_map/ppermute | solution.py:302
  52.7 1.8 %collective-permute-done.7 = f32[128,256]{1,0:T(8,128)S(1)} collective-permute-done((f32[128,256]{1,0:T(8,128)S(1)}, f32[128,256]{1,0:T(8,128)S(1)}, u32[]{:S(2)}, u32[]{:S(2)}) %collective-permute-start.7) | collective-permute-done | bytes 131104 | tf_op jit(solution)/shard_map/ppermute | solution.py:302
  54.5 4.5 %collective-permute-done.6 = f32[128,256]{1,0:T(8,128)S(1)} collective-permute-done((f32[128,256]{1,0:T(8,128)S(1)}, f32[128,256]{1,0:T(8,128)S(1)}, u32[]{:S(2)}, u32[]{:S(2)}) %collective-permute-start.6) | collective-permute-done | bytes 131104 | tf_op jit(solution)/shard_map/ppermute | solution.py:302
  59.0 3.1 %collective-permute-start.9 = (f32[2,128,256]{2,1,0:T(8,128)S(1)}, f32[2,128,256]{2,1,0:T(8,128)S(1)}, u32[]{:S(2)}, u32[]{:S(2)}) collective-permute-start(f32[2,128,256]{2,1,0:T(8,128)S(1)} %pad_maximum_fusion.3), channel_id=1, source_target_pairs={{0,12},{1,13},{2,14},{3,15},{4,8},{5,9},{6,10},{7,11},{8,4},{9,5},... | collective-permute-start | bytes 786440 | tf_op jit(solution)/shard_map/ppermute | solution.py:302
  62.1 1.7 %collective-permute-start.12 = (f32[4,128,256]{2,1,0:T(8,128)S(1)}, f32[4,128,256]{2,1,0:T(8,128)S(1)}, u32[]{:S(2)}, u32[]{:S(2)}) collective-permute-start(f32[4,128,256]{2,1,0:T(8,128)S(1)} %pad_maximum_fusion.1.refs_0_), channel_id=1, source_target_pairs={{0,2},{1,3},{2,0},{3,1},{4,6},{5,7},{6,4},{7,5},{8,10},{9,11},{10,... | collective-permute-start | bytes 1572872 | tf_op jit(solution)/shard_map/ppermute | solution.py:302
  63.8 3.4 %collective-permute-done.9 = f32[2,128,256]{2,1,0:T(8,128)S(1)} collective-permute-done((f32[2,128,256]{2,1,0:T(8,128)S(1)}, f32[2,128,256]{2,1,0:T(8,128)S(1)}, u32[]{:S(2)}, u32[]{:S(2)}) %collective-permute-start.9) | collective-permute-done | bytes 262176 | tf_op jit(solution)/shard_map/ppermute | solution.py:302
  67.2 1.6 %collective-permute-start.14 = (f32[2,128,256]{2,1,0:T(8,128)S(1)}, f32[2,128,256]{2,1,0:T(8,128)S(1)}, u32[]{:S(2)}, u32[]{:S(2)}) collective-permute-start(f32[2,128,256]{2,1,0:T(8,128)S(1)} %collective-permute-done.9), channel_id=1, source_target_pairs={{0,2},{1,3},{2,0},{3,1},{4,6},{5,7},{6,4},{7,5},{8,10},{9,11},{10,... | collective-permute-start | bytes 786440 | tf_op jit(solution)/shard_map/ppermute | solution.py:302
  68.8 0.1 collective-permute-start.11
  68.9 0.5 collective-permute-start.10
  69.4 4.7 %collective-permute-done.14 = f32[2,128,256]{2,1,0:T(8,128)S(1)} collective-permute-done((f32[2,128,256]{2,1,0:T(8,128)S(1)}, f32[2,128,256]{2,1,0:T(8,128)S(1)}, u32[]{:S(2)}, u32[]{:S(2)}) %collective-permute-start.14) | collective-permute-done | bytes 262176 | tf_op jit(solution)/shard_map/ppermute | solution.py:302
  74.2 0.1 collective-permute-start.15
  74.3 0.0 collective-permute-done.12.refs_4_
  74.3 0.5 collective-permute-start.13
  74.8 0.0 collective-permute-done.11.refs_3_
  74.8 0.0 collective-permute-done.10.refs_1_
  74.8 1.4 %collective-permute-done.15.refs_7_ = f32[4,128,256]{2,1,0:T(8,128)S(1)} collective-permute-done((f32[4,128,256]{2,1,0:T(8,128)S(1)}, f32[4,128,256]{2,1,0:T(8,128)S(1)}, u32[]{:S(2)}, u32[]{:S(2)}) %collective-permute-start.15) | collective-permute-done | bytes 524320 | tf_op jit(solution)/shard_map/ppermute | solution.py:302
  76.2 0.7 collective-permute-done.13.refs_5_
  76.9 0.0 collective-permute-done.2.oth1_ref
  76.9 0.0 copy-done
  76.9 0.0 copy-done.1
  76.9 0.0 copy-done.2
  76.9 22.3 %stack_lags.1 = f32[128,128,512]{2,1,0:T(8,128)} custom-call(s32[1]{0:T(128)} %bitcast.6.place_ref, f32[1280,128]{1,0:T(8,128)} %get-tuple-element.44.own0_ref, f32[2816,128]{1,0:T(8,128)S(1)} %copy-done.2, f32[1280,128]{1,0:T(8,128)S(1)} %collective-permute-done.oth0_ref, f32[2816,128]{1,0:T(8,128)S(1)} %collective-permute-done.2.oth1_ref, ...), custom_call_target="tpu_custom_call" | custom-call | flops 20000000000 | bytes 50331648 | tf_op jit(solution)/shard_map/stack_lags/pallas_call | solution.py:280
  (7 shorter events, 0.1 us)
Async XLA Ops:
  0.0 19.8 %copy-start.3 = (s32[256]{0:T(256)S(1)}, s32[256]{0:T(256)}, u32[]{:S(2)}) copy-start(s32[256]{0:T(256)} %param.9) | copy-start | bytes 3076
  10.8 21.8 %all-to-all-start.1 = ((f32[16,32,256]{2,1,0:T(8,128)}), f32[16,32,256]{2,1,0:T(8,128)S(1)}, u32[]{:S(2)}, u32[]{:S(2)}) async-start(f32[16,32,256]{2,1,0:T(8,128)} %get-tuple-element.46), calls=%async_computation.1 | async-start | bytes 1048576 | tf_op jit(solution)/shard_map/all_to_all | solution.py:340
  18.2 17.3 %collective-permute-start = (f32[1280,128]{1,0:T(8,128)}, f32[1280,128]{1,0:T(8,128)S(1)}, u32[]{:S(2)}, u32[]{:S(2)}) collective-permute-start(f32[1280,128]{1,0:T(8,128)} %get-tuple-element.44.own0_ref), channel_id=1, source_target_pairs={{0,16},{16,0},{1,17},{17,1},{2,18},{18,2},{3,19},{19,3},{4,20},{20... | collective-permute-start | bytes 1966088 | tf_op jit(solution)/shard_map/ppermute | solution.py:302
  33.8 43.2 %copy-start = (bf16[256,512]{1,0:T(8,128)(2,1)S(1)}, bf16[256,512]{1,0:T(8,128)(2,1)}, u32[]{:S(2)}) copy-start(bf16[256,512]{1,0:T(8,128)(2,1)} %constant.64.clone.lo_ref) | copy-start | bytes 786436
  33.8 43.1 %copy-start.1 = (bf16[256,512]{1,0:T(8,128)(2,1)S(1)}, bf16[256,512]{1,0:T(8,128)(2,1)}, u32[]{:S(2)}) copy-start(bf16[256,512]{1,0:T(8,128)(2,1)} %constant.63.clone.hi_ref) | copy-start | bytes 786436
  33.8 43.1 %copy-start.2 = (f32[2816,128]{1,0:T(8,128)S(1)}, f32[2816,128]{1,0:T(8,128)}, u32[]{:S(2)}) copy-start(f32[2816,128]{1,0:T(8,128)} %get-tuple-element.49.own1_ref) | copy-start | bytes 4325380
  35.5 7.0 %collective-permute-start.1 = (f32[128,256]{1,0:T(8,128)S(1)}, f32[128,256]{1,0:T(8,128)S(1)}, u32[]{:S(2)}, u32[]{:S(2)}) collective-permute-start(f32[128,256]{1,0:T(8,128)S(1)} %get-tuple-element.48), channel_id=1, source_target_pairs={{0,16},{16,0},{1,17},{17,1},{2,18},{18,2},{3,19},{19,3},{4,20},{20... | collective-permute-start | bytes 393224 | tf_op jit(solution)/shard_map/ppermute | solution.py:302
  37.0 6.0 %collective-permute-start.5 = (f32[128,256]{1,0:T(8,128)S(1)}, f32[128,256]{1,0:T(8,128)S(1)}, u32[]{:S(2)}, u32[]{:S(2)}) collective-permute-start(f32[128,256]{1,0:T(8,128)S(1)} %get-tuple-element.56), channel_id=1, source_target_pairs={{0,2},{1,3},{2,0},{3,1},{4,6},{5,7},{6,4},{7,5},{8,10},{9,11},{10,... | collective-permute-start | bytes 393224 | tf_op jit(solution)/shard_map/ppermute | solution.py:302
  38.6 6.5 %collective-permute-start.4 = (f32[128,256]{1,0:T(8,128)S(1)}, f32[128,256]{1,0:T(8,128)S(1)}, u32[]{:S(2)}, u32[]{:S(2)}) collective-permute-start(f32[128,256]{1,0:T(8,128)S(1)} %get-tuple-element.56), channel_id=1, source_target_pairs={{0,4},{1,5},{2,6},{3,7},{4,0},{5,1},{6,2},{7,3},{8,12},{9,13},{10,... | collective-permute-start | bytes 393224 | tf_op jit(solution)/shard_map/ppermute | solution.py:302
  40.1 7.6 %collective-permute-start.3 = (f32[128,256]{1,0:T(8,128)S(1)}, f32[128,256]{1,0:T(8,128)S(1)}, u32[]{:S(2)}, u32[]{:S(2)}) collective-permute-start(f32[128,256]{1,0:T(8,128)S(1)} %get-tuple-element.56), channel_id=1, source_target_pairs={{0,8},{1,9},{2,10},{3,11},{4,12},{5,13},{6,14},{7,15},{8,0},{9,1},... | collective-permute-start | bytes 393224 | tf_op jit(solution)/shard_map/ppermute | solution.py:302
  42.5 34.4 %collective-permute-start.2 = (f32[2816,128]{1,0:T(8,128)}, f32[2816,128]{1,0:T(8,128)S(1)}, u32[]{:S(2)}, u32[]{:S(2)}) collective-permute-start(f32[2816,128]{1,0:T(8,128)} %get-tuple-element.49.own1_ref), channel_id=1, source_target_pairs={{0,16},{16,0},{1,17},{17,1},{2,18},{18,2},{3,19},{19,3},{4,20},{20... | collective-permute-start | bytes 4325384 | tf_op jit(solution)/shard_map/ppermute | solution.py:302
  47.7 5.0 %collective-permute-start.8 = (f32[128,256]{1,0:T(8,128)S(1)}, f32[128,256]{1,0:T(8,128)S(1)}, u32[]{:S(2)}, u32[]{:S(2)}) collective-permute-start(f32[128,256]{1,0:T(8,128)S(1)} %collective-permute-done.1), channel_id=1, source_target_pairs={{0,2},{1,3},{2,0},{3,1},{4,6},{5,7},{6,4},{7,5},{8,10},{9,11},{10,... | collective-permute-start | bytes 393224 | tf_op jit(solution)/shard_map/ppermute | solution.py:302
  48.3 6.1 %collective-permute-start.7 = (f32[128,256]{1,0:T(8,128)S(1)}, f32[128,256]{1,0:T(8,128)S(1)}, u32[]{:S(2)}, u32[]{:S(2)}) collective-permute-start(f32[128,256]{1,0:T(8,128)S(1)} %collective-permute-done.1), channel_id=1, source_target_pairs={{0,4},{1,5},{2,6},{3,7},{4,0},{5,1},{6,2},{7,3},{8,12},{9,13},{10,... | collective-permute-start | bytes 393224 | tf_op jit(solution)/shard_map/ppermute | solution.py:302
  48.7 10.3 %collective-permute-start.6 = (f32[128,256]{1,0:T(8,128)S(1)}, f32[128,256]{1,0:T(8,128)S(1)}, u32[]{:S(2)}, u32[]{:S(2)}) collective-permute-start(f32[128,256]{1,0:T(8,128)S(1)} %collective-permute-done.1), channel_id=1, source_target_pairs={{0,8},{1,9},{2,10},{3,11},{4,12},{5,13},{6,14},{7,15},{8,0},{9,1},... | collective-permute-start | bytes 393224 | tf_op jit(solution)/shard_map/ppermute | solution.py:302
  59.0 8.2 %collective-permute-start.9 = (f32[2,128,256]{2,1,0:T(8,128)S(1)}, f32[2,128,256]{2,1,0:T(8,128)S(1)}, u32[]{:S(2)}, u32[]{:S(2)}) collective-permute-start(f32[2,128,256]{2,1,0:T(8,128)S(1)} %pad_maximum_fusion.3), channel_id=1, source_target_pairs={{0,12},{1,13},{2,14},{3,15},{4,8},{5,9},{6,10},{7,11},{8,4},{9,5},... | collective-permute-start | bytes 786440 | tf_op jit(solution)/shard_map/ppermute | solution.py:302
  62.1 12.2 %collective-permute-start.12 = (f32[4,128,256]{2,1,0:T(8,128)S(1)}, f32[4,128,256]{2,1,0:T(8,128)S(1)}, u32[]{:S(2)}, u32[]{:S(2)}) collective-permute-start(f32[4,128,256]{2,1,0:T(8,128)S(1)} %pad_maximum_fusion.1.refs_0_), channel_id=1, source_target_pairs={{0,2},{1,3},{2,0},{3,1},{4,6},{5,7},{6,4},{7,5},{8,10},{9,11},{10,... | collective-permute-start | bytes 1572872 | tf_op jit(solution)/shard_map/ppermute | solution.py:302
  67.2 7.0 %collective-permute-start.14 = (f32[2,128,256]{2,1,0:T(8,128)S(1)}, f32[2,128,256]{2,1,0:T(8,128)S(1)}, u32[]{:S(2)}, u32[]{:S(2)}) collective-permute-start(f32[2,128,256]{2,1,0:T(8,128)S(1)} %collective-permute-done.9), channel_id=1, source_target_pairs={{0,2},{1,3},{2,0},{3,1},{4,6},{5,7},{6,4},{7,5},{8,10},{9,11},{10,... | collective-permute-start | bytes 786440 | tf_op jit(solution)/shard_map/ppermute | solution.py:302
  68.8 5.9 %collective-permute-start.11 = (f32[4,128,256]{2,1,0:T(8,128)S(1)}, f32[4,128,256]{2,1,0:T(8,128)S(1)}, u32[]{:S(2)}, u32[]{:S(2)}) collective-permute-start(f32[4,128,256]{2,1,0:T(8,128)S(1)} %pad_maximum_fusion.2.refs_2_), channel_id=1, source_target_pairs={{0,1},{1,0},{2,3},{3,2},{4,5},{5,4},{6,7},{7,6},{8,9},{9,8},{10,11... | collective-permute-start | bytes 1572872 | tf_op jit(solution)/shard_map/ppermute | solution.py:302
  68.9 5.8 %collective-permute-start.10 = (f32[4,128,256]{2,1,0:T(8,128)S(1)}, f32[4,128,256]{2,1,0:T(8,128)S(1)}, u32[]{:S(2)}, u32[]{:S(2)}) collective-permute-start(f32[4,128,256]{2,1,0:T(8,128)S(1)} %pad_maximum_fusion.1.refs_0_), channel_id=1, source_target_pairs={{0,1},{1,0},{2,3},{3,2},{4,5},{5,4},{6,7},{7,6},{8,9},{9,8},{10,11... | collective-permute-start | bytes 1572872 | tf_op jit(solution)/shard_map/ppermute | solution.py:302
  74.2 2.0 %collective-permute-start.15 = (f32[4,128,256]{2,1,0:T(8,128)S(1)}, f32[4,128,256]{2,1,0:T(8,128)S(1)}, u32[]{:S(2)}, u32[]{:S(2)}) collective-permute-start(f32[4,128,256]{2,1,0:T(8,128)S(1)} %constant_dynamic-update-slice_fusion.refs_6_), channel_id=1, source_target_pairs={{0,1},{1,0},{2,3},{3,2},{4,5},{5,4},{6,7},{7,6},{8,9},{9,8},{10,11... | collective-permute-start | bytes 1572872 | tf_op jit(solution)/shard_map/ppermute | solution.py:302
  74.3 2.6 %collective-permute-start.13 = (f32[4,128,256]{2,1,0:T(8,128)S(1)}, f32[4,128,256]{2,1,0:T(8,128)S(1)}, u32[]{:S(2)}, u32[]{:S(2)}) collective-permute-start(f32[4,128,256]{2,1,0:T(8,128)S(1)} %collective-permute-done.12.refs_4_), channel_id=1, source_target_pairs={{0,1},{1,0},{2,3},{3,2},{4,5},{5,4},{6,7},{7,6},{8,9},{9,8},{10,11... | collective-permute-start | bytes 1572872 | tf_op jit(solution)/shard_map/ppermute | solution.py:302

commit v5 on v4

--- a/solution.py
+++ b/solution.py
@@ -202,7 +202,7 @@
     return [*jnp.split(mine, CHUNKS), *jnp.split(others, CHUNKS)]
 
 
-def stack_kernel(place_ref, own0_ref, own1_ref, oth0_ref, oth1_ref, hi_ref, lo_ref, *refs, stacked, pitch):
+def stack_kernel(place_ref, own0_ref, own1_ref, oth0_ref, oth1_ref, table_ref, *refs, stacked, pitch):
     stacks = refs[: len(stacked)]
     out_ref, real_ref, imag_ref, src_ref = refs[-4:]
     step = pl.program_id(0)
@@ -251,14 +251,13 @@
             ]
             lax.fori_loop(group, group + 1, functools.partial(four, parts=parts), 0)
 
-    table = jnp.concatenate((hi_ref[...], hi_ref[...], lo_ref[...]))
     rows = []
     for i in range(per):
         n = step * per + i
         both = [jnp.transpose(ref[pl.ds(n, F, stride=pitch), :]) for ref in (real_ref, imag_ref)]
         high, low = split(jnp.concatenate(both, axis=1))
         rows.append(jnp.concatenate((high, low, high), axis=1))
-    out_ref[...] = dot_nn(jnp.concatenate(rows), table).reshape(per, channels, lags)
+    out_ref[...] = dot_nn(jnp.concatenate(rows), table_ref[...]).reshape(per, channels, lags)
 
 
 def correlate(j, previous, shard, own, other, stacks, samples, sources):
@@ -270,7 +269,8 @@
     steps = size // per
     pitch = size + 8
     high, low = split_const(inverse_table(samples))
-    operands = [*own, *other, high, low, *(x for _, x in stacks)]
+    table = np.concatenate((high, high, low))
+    operands = [*own, *other, table, *(x for _, x in stacks)]
     in_specs = [whole(x.shape) for x in operands]
     aliases = {}
     if previous is not None:

time: 99.5 us -> 99.5 us (level)
  no operation moved by 1% of the time
where the time goes in v5:
time: 99.5 us; the launch traced here: 99.2 us
  waiting for transfers between devices  35.4 us (36%)
  Pallas kernels  34.1 us (34%)
  starting transfers between devices  27.7 us (28%)
  other arithmetic  1.01 us (1%)
    ppermute x16, waiting for transfers between devices, swap(): lax.ppermute(x, axis, [(i, i ^ bits) for i in range(lax.axis_size(axis))])  24.2 us
    pallas_call x1, Pallas kernels, correlate(): pl.pallas_call(functools.partial(stack_kernel, stacked=stacked, pitch=pit...  22.3 us
    ppermute x16, starting transfers between devices, swap(): lax.ppermute(x, axis, [(i, i ^ bits) for i in range(lax.axis_size(axis))])  20.3 us
    all_to_all x1, waiting for transfers between devices, body(): got = lax.all_to_all(held, 'shard', split_axis=0, concat_axis=0, tiled=True)  11.3 us
    pallas_call x1, Pallas kernels, forward(): pl.pallas_call(functools.partial(spectra_kernel, segs=segs), grid_spec=pl...  10.8 us
    all_to_all x1, starting transfers between devices, body(): got = lax.all_to_all(held, 'shard', split_axis=0, concat_axis=0, tiled=True)  7.38 us
  transfers between devices with their start and end apart: 17, of which 11 were waited for; matrix products, arithmetic and copies ran while one was open for 1% of the time, Pallas kernels for 1%

profile of v5, /device:TPU:0, one launch (start us, length us, event | category | flops | bytes accessed | tf_op | source)
XLA Modules:
  0.0 99.2 jit_solution(14170173307324695263)
XLA Ops:
  0.0 0.0 copy-start.2
  0.0 10.8 %forward_whiten.1 = (f32[1280,128]{1,0:T(8,128)}, f32[2816,128]{1,0:T(8,128)}, f32[16,32,256]{2,1,0:T(8,128)}) custom-call(s32[1]{0:T(128)} %bitcast.6.place_ref, f32[16,128,1024]{2,1,0:T(8,128)} %rec_ref.1, bf16[1024,256]{1,0:T(8,128)(2,1)} %constant.59.clone.hi_ref, bf16[1024,256]{1,0:T(8,128)(2,1)} %constant.60.clone.lo_ref, s32[1,256]{1,0:T(1,128)} %bitcast.29), custom_call_target="tpu_custom_call" | custom-call | flops 6000000000 | bytes 16777216 | tf_op jit(solution)/shard_map/forward_whiten/pallas_call | solution.py:135
  10.8 7.4 %all-to-all-start.1 = ((f32[16,32,256]{2,1,0:T(8,128)}), f32[16,32,256]{2,1,0:T(8,128)S(1)}, u32[]{:S(2)}, u32[]{:S(2)}) async-start(f32[16,32,256]{2,1,0:T(8,128)} %get-tuple-element.46), calls=%async_computation.1 | async-start | bytes 1048576 | tf_op jit(solution)/shard_map/all_to_all | solution.py:340
  18.2 1.6 %collective-permute-start = (f32[1280,128]{1,0:T(8,128)}, f32[1280,128]{1,0:T(8,128)S(1)}, u32[]{:S(2)}, u32[]{:S(2)}) collective-permute-start(f32[1280,128]{1,0:T(8,128)} %get-tuple-element.44.own0_ref), channel_id=1, source_target_pairs={{0,16},{16,0},{1,17},{17,1},{2,18},{18,2},{3,19},{19,3},{4,20},{20... | collective-permute-start | bytes 1966088 | tf_op jit(solution)/shard_map/ppermute | solution.py:302
  19.8 0.0 copy-done.2
  19.8 0.1 convert_reduce_fusion
  19.9 0.7 reduce_max.9
  21.3 0.1 pad_add_fusion.place_ref
  21.4 11.3 %all-to-all-done.1 = f32[16,32,256]{2,1,0:T(8,128)S(1)} async-done(((f32[16,32,256]{2,1,0:T(8,128)}), f32[16,32,256]{2,1,0:T(8,128)S(1)}, u32[]{:S(2)}, u32[]{:S(2)}) %all-to-all-start.1) | async-done | bytes 524320 | tf_op jit(solution)/shard_map/all_to_all | solution.py:340
  32.7 1.1 %order_sources.1 = (f32[128,256]{1,0:T(8,128)S(1)}, f32[128,256]{1,0:T(8,128)S(1)}) custom-call(s32[2]{0:T(128)S(1)} %pad_add_fusion.place_ref, f32[512,256]{1,0:T(8,128)S(1)} %bitcast.18, s32[1,256]{1,0:T(1,128)S(1)} %bitcast.30), custom_call_target="tpu_custom_call" | custom-call | flops 100000000 | bytes 1048576 | tf_op jit(solution)/shard_map/order_sources/pallas_call | solution.py:179
  33.8 0.0 copy-start
  33.8 0.0 copy-start.1
  33.8 1.7 %collective-permute-done.oth0_ref = f32[1280,128]{1,0:T(8,128)S(1)} collective-permute-done((f32[1280,128]{1,0:T(8,128)}, f32[1280,128]{1,0:T(8,128)S(1)}, u32[]{:S(2)}, u32[]{:S(2)}) %collective-permute-start) | collective-permute-done | bytes 655392 | tf_op jit(solution)/shard_map/ppermute | solution.py:302
  35.5 1.5 %collective-permute-start.1 = (f32[128,256]{1,0:T(8,128)S(1)}, f32[128,256]{1,0:T(8,128)S(1)}, u32[]{:S(2)}, u32[]{:S(2)}) collective-permute-start(f32[128,256]{1,0:T(8,128)S(1)} %get-tuple-element.48), channel_id=1, source_target_pairs={{0,16},{16,0},{1,17},{17,1},{2,18},{18,2},{3,19},{19,3},{4,20},{20... | collective-permute-start | bytes 393224 | tf_op jit(solution)/shard_map/ppermute | solution.py:302
  37.0 1.7 %collective-permute-start.5 = (f32[128,256]{1,0:T(8,128)S(1)}, f32[128,256]{1,0:T(8,128)S(1)}, u32[]{:S(2)}, u32[]{:S(2)}) collective-permute-start(f32[128,256]{1,0:T(8,128)S(1)} %get-tuple-element.56), channel_id=1, source_target_pairs={{0,2},{1,3},{2,0},{3,1},{4,6},{5,7},{6,4},{7,5},{8,10},{9,11},{10,... | collective-permute-start | bytes 393224 | tf_op jit(solution)/shard_map/ppermute | solution.py:302
  38.7 1.5 %collective-permute-start.4 = (f32[128,256]{1,0:T(8,128)S(1)}, f32[128,256]{1,0:T(8,128)S(1)}, u32[]{:S(2)}, u32[]{:S(2)}) collective-permute-start(f32[128,256]{1,0:T(8,128)S(1)} %get-tuple-element.56), channel_id=1, source_target_pairs={{0,4},{1,5},{2,6},{3,7},{4,0},{5,1},{6,2},{7,3},{8,12},{9,13},{10,... | collective-permute-start | bytes 393224 | tf_op jit(solution)/shard_map/ppermute | solution.py:302
  40.1 2.4 %collective-permute-start.3 = (f32[128,256]{1,0:T(8,128)S(1)}, f32[128,256]{1,0:T(8,128)S(1)}, u32[]{:S(2)}, u32[]{:S(2)}) collective-permute-start(f32[128,256]{1,0:T(8,128)S(1)} %get-tuple-element.56), channel_id=1, source_target_pairs={{0,8},{1,9},{2,10},{3,11},{4,12},{5,13},{6,14},{7,15},{8,0},{9,1},... | collective-permute-start | bytes 393224 | tf_op jit(solution)/shard_map/ppermute | solution.py:302
  42.5 0.0 collective-permute-done.1
  42.5 0.5 collective-permute-start.2
  43.0 0.0 collective-permute-done.5
  43.0 2.2 %collective-permute-done.4 = f32[128,256]{1,0:T(8,128)S(1)} collective-permute-done((f32[128,256]{1,0:T(8,128)S(1)}, f32[128,256]{1,0:T(8,128)S(1)}, u32[]{:S(2)}, u32[]{:S(2)}) %collective-permute-start.4) | collective-permute-done | bytes 131104 | tf_op jit(solution)/shard_map/ppermute | solution.py:302
  45.2 2.6 %collective-permute-done.3 = f32[128,256]{1,0:T(8,128)S(1)} collective-permute-done((f32[128,256]{1,0:T(8,128)S(1)}, f32[128,256]{1,0:T(8,128)S(1)}, u32[]{:S(2)}, u32[]{:S(2)}) %collective-permute-start.3) | collective-permute-done | bytes 131104 | tf_op jit(solution)/shard_map/ppermute | solution.py:302
  47.7 0.6 collective-permute-start.8
  48.3 0.3 collective-permute-start.7
  48.7 2.8 %collective-permute-start.6 = (f32[128,256]{1,0:T(8,128)S(1)}, f32[128,256]{1,0:T(8,128)S(1)}, u32[]{:S(2)}, u32[]{:S(2)}) collective-permute-start(f32[128,256]{1,0:T(8,128)S(1)} %collective-permute-done.1), channel_id=1, source_target_pairs={{0,8},{1,9},{2,10},{3,11},{4,12},{5,13},{6,14},{7,15},{8,0},{9,1},... | collective-permute-start | bytes 393224 | tf_op jit(solution)/shard_map/ppermute | solution.py:302
  51.4 1.2 %collective-permute-done.8 = f32[128,256]{1,0:T(8,128)S(1)} collective-permute-done((f32[128,256]{1,0:T(8,128)S(1)}, f32[128,256]{1,0:T(8,128)S(1)}, u32[]{:S(2)}, u32[]{:S(2)}) %collective-permute-start.8) | collective-permute-done | bytes 131104 | tf_op jit(solution)/shard_map/ppermute | solution.py:302
  52.7 1.8 %collective-permute-done.7 = f32[128,256]{1,0:T(8,128)S(1)} collective-permute-done((f32[128,256]{1,0:T(8,128)S(1)}, f32[128,256]{1,0:T(8,128)S(1)}, u32[]{:S(2)}, u32[]{:S(2)}) %collective-permute-start.7) | collective-permute-done | bytes 131104 | tf_op jit(solution)/shard_map/ppermute | solution.py:302
  54.5 4.5 %collective-permute-done.6 = f32[128,256]{1,0:T(8,128)S(1)} collective-permute-done((f32[128,256]{1,0:T(8,128)S(1)}, f32[128,256]{1,0:T(8,128)S(1)}, u32[]{:S(2)}, u32[]{:S(2)}) %collective-permute-start.6) | collective-permute-done | bytes 131104 | tf_op jit(solution)/shard_map/ppermute | solution.py:302
  59.0 3.1 %collective-permute-start.9 = (f32[2,128,256]{2,1,0:T(8,128)S(1)}, f32[2,128,256]{2,1,0:T(8,128)S(1)}, u32[]{:S(2)}, u32[]{:S(2)}) collective-permute-start(f32[2,128,256]{2,1,0:T(8,128)S(1)} %pad_maximum_fusion.3), channel_id=1, source_target_pairs={{0,12},{1,13},{2,14},{3,15},{4,8},{5,9},{6,10},{7,11},{8,4},{9,5},... | collective-permute-start | bytes 786440 | tf_op jit(solution)/shard_map/ppermute | solution.py:302
  62.1 1.7 %collective-permute-start.12 = (f32[4,128,256]{2,1,0:T(8,128)S(1)}, f32[4,128,256]{2,1,0:T(8,128)S(1)}, u32[]{:S(2)}, u32[]{:S(2)}) collective-permute-start(f32[4,128,256]{2,1,0:T(8,128)S(1)} %pad_maximum_fusion.1.refs_0_), channel_id=1, source_target_pairs={{0,2},{1,3},{2,0},{3,1},{4,6},{5,7},{6,4},{7,5},{8,10},{9,11},{10,... | collective-permute-start | bytes 1572872 | tf_op jit(solution)/shard_map/ppermute | solution.py:302
  63.8 3.4 %collective-permute-done.9 = f32[2,128,256]{2,1,0:T(8,128)S(1)} collective-permute-done((f32[2,128,256]{2,1,0:T(8,128)S(1)}, f32[2,128,256]{2,1,0:T(8,128)S(1)}, u32[]{:S(2)}, u32[]{:S(2)}) %collective-permute-start.9) | collective-permute-done | bytes 262176 | tf_op jit(solution)/shard_map/ppermute | solution.py:302
  67.2 1.6 %collective-permute-start.14 = (f32[2,128,256]{2,1,0:T(8,128)S(1)}, f32[2,128,256]{2,1,0:T(8,128)S(1)}, u32[]{:S(2)}, u32[]{:S(2)}) collective-permute-start(f32[2,128,256]{2,1,0:T(8,128)S(1)} %collective-permute-done.9), channel_id=1, source_target_pairs={{0,2},{1,3},{2,0},{3,1},{4,6},{5,7},{6,4},{7,5},{8,10},{9,11},{10,... | collective-permute-start | bytes 786440 | tf_op jit(solution)/shard_map/ppermute | solution.py:302
  68.9 0.1 collective-permute-start.11
  68.9 0.5 collective-permute-start.10
  69.5 4.7 %collective-permute-done.14 = f32[2,128,256]{2,1,0:T(8,128)S(1)} collective-permute-done((f32[2,128,256]{2,1,0:T(8,128)S(1)}, f32[2,128,256]{2,1,0:T(8,128)S(1)}, u32[]{:S(2)}, u32[]{:S(2)}) %collective-permute-start.14) | collective-permute-done | bytes 262176 | tf_op jit(solution)/shard_map/ppermute | solution.py:302
  74.2 0.1 collective-permute-start.15
  74.3 0.0 collective-permute-done.12.refs_4_
  74.3 0.5 collective-permute-start.13
  74.8 0.0 collective-permute-done.11.refs_3_
  74.8 0.0 collective-permute-done.10.refs_1_
  74.8 1.4 %collective-permute-done.15.refs_7_ = f32[4,128,256]{2,1,0:T(8,128)S(1)} collective-permute-done((f32[4,128,256]{2,1,0:T(8,128)S(1)}, f32[4,128,256]{2,1,0:T(8,128)S(1)}, u32[]{:S(2)}, u32[]{:S(2)}) %collective-permute-start.15) | collective-permute-done | bytes 524320 | tf_op jit(solution)/shard_map/ppermute | solution.py:302
  76.2 0.7 collective-permute-done.13.refs_5_
  76.9 0.0 collective-permute-done.2.oth1_ref
  76.9 0.0 copy-done
  76.9 0.0 copy-done.1
  76.9 22.3 %stack_lags.1 = f32[128,128,512]{2,1,0:T(8,128)} custom-call(s32[1]{0:T(128)} %bitcast.6.place_ref, f32[1280,128]{1,0:T(8,128)} %get-tuple-element.44.own0_ref, f32[2816,128]{1,0:T(8,128)S(1)} %copy-done.1, f32[1280,128]{1,0:T(8,128)S(1)} %collective-permute-done.oth0_ref, f32[2816,128]{1,0:T(8,128)S(1)} %collective-permute-done.2.oth1_ref, ...), custom_call_target="tpu_custom_call" | custom-call | flops 20000000000 | bytes 50331648 | tf_op jit(solution)/shard_map/stack_lags/pallas_call | solution.py:280
  (7 shorter events, 0.1 us)
Async XLA Ops:
  0.0 19.8 %copy-start.2 = (s32[256]{0:T(256)S(1)}, s32[256]{0:T(256)}, u32[]{:S(2)}) copy-start(s32[256]{0:T(256)} %param.8) | copy-start | bytes 3076
  10.8 21.9 %all-to-all-start.1 = ((f32[16,32,256]{2,1,0:T(8,128)}), f32[16,32,256]{2,1,0:T(8,128)S(1)}, u32[]{:S(2)}, u32[]{:S(2)}) async-start(f32[16,32,256]{2,1,0:T(8,128)} %get-tuple-element.46), calls=%async_computation.1 | async-start | bytes 1048576 | tf_op jit(solution)/shard_map/all_to_all | solution.py:340
  18.2 17.3 %collective-permute-start = (f32[1280,128]{1,0:T(8,128)}, f32[1280,128]{1,0:T(8,128)S(1)}, u32[]{:S(2)}, u32[]{:S(2)}) collective-permute-start(f32[1280,128]{1,0:T(8,128)} %get-tuple-element.44.own0_ref), channel_id=1, source_target_pairs={{0,16},{16,0},{1,17},{17,1},{2,18},{18,2},{3,19},{19,3},{4,20},{20... | collective-permute-start | bytes 1966088 | tf_op jit(solution)/shard_map/ppermute | solution.py:302
  33.8 43.2 %copy-start = (bf16[768,512]{1,0:T(8,128)(2,1)S(1)}, bf16[768,512]{1,0:T(8,128)(2,1)}, u32[]{:S(2)}) copy-start(bf16[768,512]{1,0:T(8,128)(2,1)} %constant.61.clone.table_ref) | copy-start | bytes 2359300
  33.8 43.1 %copy-start.1 = (f32[2816,128]{1,0:T(8,128)S(1)}, f32[2816,128]{1,0:T(8,128)}, u32[]{:S(2)}) copy-start(f32[2816,128]{1,0:T(8,128)} %get-tuple-element.49.own1_ref) | copy-start | bytes 4325380
  35.5 7.0 %collective-permute-start.1 = (f32[128,256]{1,0:T(8,128)S(1)}, f32[128,256]{1,0:T(8,128)S(1)}, u32[]{:S(2)}, u32[]{:S(2)}) collective-permute-start(f32[128,256]{1,0:T(8,128)S(1)} %get-tuple-element.48), channel_id=1, source_target_pairs={{0,16},{16,0},{1,17},{17,1},{2,18},{18,2},{3,19},{19,3},{4,20},{20... | collective-permute-start | bytes 393224 | tf_op jit(solution)/shard_map/ppermute | solution.py:302
  37.0 6.0 %collective-permute-start.5 = (f32[128,256]{1,0:T(8,128)S(1)}, f32[128,256]{1,0:T(8,128)S(1)}, u32[]{:S(2)}, u32[]{:S(2)}) collective-permute-start(f32[128,256]{1,0:T(8,128)S(1)} %get-tuple-element.56), channel_id=1, source_target_pairs={{0,2},{1,3},{2,0},{3,1},{4,6},{5,7},{6,4},{7,5},{8,10},{9,11},{10,... | collective-permute-start | bytes 393224 | tf_op jit(solution)/shard_map/ppermute | solution.py:302
  38.7 6.5 %collective-permute-start.4 = (f32[128,256]{1,0:T(8,128)S(1)}, f32[128,256]{1,0:T(8,128)S(1)}, u32[]{:S(2)}, u32[]{:S(2)}) collective-permute-start(f32[128,256]{1,0:T(8,128)S(1)} %get-tuple-element.56), channel_id=1, source_target_pairs={{0,4},{1,5},{2,6},{3,7},{4,0},{5,1},{6,2},{7,3},{8,12},{9,13},{10,... | collective-permute-start | bytes 393224 | tf_op jit(solution)/shard_map/ppermute | solution.py:302
  40.1 7.6 %collective-permute-start.3 = (f32[128,256]{1,0:T(8,128)S(1)}, f32[128,256]{1,0:T(8,128)S(1)}, u32[]{:S(2)}, u32[]{:S(2)}) collective-permute-start(f32[128,256]{1,0:T(8,128)S(1)} %get-tuple-element.56), channel_id=1, source_target_pairs={{0,8},{1,9},{2,10},{3,11},{4,12},{5,13},{6,14},{7,15},{8,0},{9,1},... | collective-permute-start | bytes 393224 | tf_op jit(solution)/shard_map/ppermute | solution.py:302
  42.5 34.4 %collective-permute-start.2 = (f32[2816,128]{1,0:T(8,128)}, f32[2816,128]{1,0:T(8,128)S(1)}, u32[]{:S(2)}, u32[]{:S(2)}) collective-permute-start(f32[2816,128]{1,0:T(8,128)} %get-tuple-element.49.own1_ref), channel_id=1, source_target_pairs={{0,16},{16,0},{1,17},{17,1},{2,18},{18,2},{3,19},{19,3},{4,20},{20... | collective-permute-start | bytes 4325384 | tf_op jit(solution)/shard_map/ppermute | solution.py:302
  47.7 5.0 %collective-permute-start.8 = (f32[128,256]{1,0:T(8,128)S(1)}, f32[128,256]{1,0:T(8,128)S(1)}, u32[]{:S(2)}, u32[]{:S(2)}) collective-permute-start(f32[128,256]{1,0:T(8,128)S(1)} %collective-permute-done.1), channel_id=1, source_target_pairs={{0,2},{1,3},{2,0},{3,1},{4,6},{5,7},{6,4},{7,5},{8,10},{9,11},{10,... | collective-permute-start | bytes 393224 | tf_op jit(solution)/shard_map/ppermute | solution.py:302
  48.3 6.1 %collective-permute-start.7 = (f32[128,256]{1,0:T(8,128)S(1)}, f32[128,256]{1,0:T(8,128)S(1)}, u32[]{:S(2)}, u32[]{:S(2)}) collective-permute-start(f32[128,256]{1,0:T(8,128)S(1)} %collective-permute-done.1), channel_id=1, source_target_pairs={{0,4},{1,5},{2,6},{3,7},{4,0},{5,1},{6,2},{7,3},{8,12},{9,13},{10,... | collective-permute-start | bytes 393224 | tf_op jit(solution)/shard_map/ppermute | solution.py:302
  48.7 10.3 %collective-permute-start.6 = (f32[128,256]{1,0:T(8,128)S(1)}, f32[128,256]{1,0:T(8,128)S(1)}, u32[]{:S(2)}, u32[]{:S(2)}) collective-permute-start(f32[128,256]{1,0:T(8,128)S(1)} %collective-permute-done.1), channel_id=1, source_target_pairs={{0,8},{1,9},{2,10},{3,11},{4,12},{5,13},{6,14},{7,15},{8,0},{9,1},... | collective-permute-start | bytes 393224 | tf_op jit(solution)/shard_map/ppermute | solution.py:302
  59.0 8.2 %collective-permute-start.9 = (f32[2,128,256]{2,1,0:T(8,128)S(1)}, f32[2,128,256]{2,1,0:T(8,128)S(1)}, u32[]{:S(2)}, u32[]{:S(2)}) collective-permute-start(f32[2,128,256]{2,1,0:T(8,128)S(1)} %pad_maximum_fusion.3), channel_id=1, source_target_pairs={{0,12},{1,13},{2,14},{3,15},{4,8},{5,9},{6,10},{7,11},{8,4},{9,5},... | collective-permute-start | bytes 786440 | tf_op jit(solution)/shard_map/ppermute | solution.py:302
  62.1 12.2 %collective-permute-start.12 = (f32[4,128,256]{2,1,0:T(8,128)S(1)}, f32[4,128,256]{2,1,0:T(8,128)S(1)}, u32[]{:S(2)}, u32[]{:S(2)}) collective-permute-start(f32[4,128,256]{2,1,0:T(8,128)S(1)} %pad_maximum_fusion.1.refs_0_), channel_id=1, source_target_pairs={{0,2},{1,3},{2,0},{3,1},{4,6},{5,7},{6,4},{7,5},{8,10},{9,11},{10,... | collective-permute-start | bytes 1572872 | tf_op jit(solution)/shard_map/ppermute | solution.py:302
  67.2 7.0 %collective-permute-start.14 = (f32[2,128,256]{2,1,0:T(8,128)S(1)}, f32[2,128,256]{2,1,0:T(8,128)S(1)}, u32[]{:S(2)}, u32[]{:S(2)}) collective-permute-start(f32[2,128,256]{2,1,0:T(8,128)S(1)} %collective-permute-done.9), channel_id=1, source_target_pairs={{0,2},{1,3},{2,0},{3,1},{4,6},{5,7},{6,4},{7,5},{8,10},{9,11},{10,... | collective-permute-start | bytes 786440 | tf_op jit(solution)/shard_map/ppermute | solution.py:302
  68.9 5.9 %collective-permute-start.11 = (f32[4,128,256]{2,1,0:T(8,128)S(1)}, f32[4,128,256]{2,1,0:T(8,128)S(1)}, u32[]{:S(2)}, u32[]{:S(2)}) collective-permute-start(f32[4,128,256]{2,1,0:T(8,128)S(1)} %pad_maximum_fusion.2.refs_2_), channel_id=1, source_target_pairs={{0,1},{1,0},{2,3},{3,2},{4,5},{5,4},{6,7},{7,6},{8,9},{9,8},{10,11... | collective-permute-start | bytes 1572872 | tf_op jit(solution)/shard_map/ppermute | solution.py:302
  68.9 5.8 %collective-permute-start.10 = (f32[4,128,256]{2,1,0:T(8,128)S(1)}, f32[4,128,256]{2,1,0:T(8,128)S(1)}, u32[]{:S(2)}, u32[]{:S(2)}) collective-permute-start(f32[4,128,256]{2,1,0:T(8,128)S(1)} %pad_maximum_fusion.1.refs_0_), channel_id=1, source_target_pairs={{0,1},{1,0},{2,3},{3,2},{4,5},{5,4},{6,7},{7,6},{8,9},{9,8},{10,11... | collective-permute-start | bytes 1572872 | tf_op jit(solution)/shard_map/ppermute | solution.py:302
  74.2 2.0 %collective-permute-start.15 = (f32[4,128,256]{2,1,0:T(8,128)S(1)}, f32[4,128,256]{2,1,0:T(8,128)S(1)}, u32[]{:S(2)}, u32[]{:S(2)}) collective-permute-start(f32[4,128,256]{2,1,0:T(8,128)S(1)} %constant_dynamic-update-slice_fusion.refs_6_), channel_id=1, source_target_pairs={{0,1},{1,0},{2,3},{3,2},{4,5},{5,4},{6,7},{7,6},{8,9},{9,8},{10,11... | collective-permute-start | bytes 1572872 | tf_op jit(solution)/shard_map/ppermute | solution.py:302
  74.3 2.6 %collective-permute-start.13 = (f32[4,128,256]{2,1,0:T(8,128)S(1)}, f32[4,128,256]{2,1,0:T(8,128)S(1)}, u32[]{:S(2)}, u32[]{:S(2)}) collective-permute-start(f32[4,128,256]{2,1,0:T(8,128)S(1)} %collective-permute-done.12.refs_4_), channel_id=1, source_target_pairs={{0,1},{1,0},{2,3},{3,2},{4,5},{5,4},{6,7},{7,6},{8,9},{9,8},{10,11... | collective-permute-start | bytes 1572872 | tf_op jit(solution)/shard_map/ppermute | solution.py:302
